TPU v7x, 128 devices: a whole 4x4x4 slice. The times are simulated.
128 devices in a mesh: pipe: 8 (over z_lo, x), ctx: 8 (over y, core), tp: 2 (over z_hi).
Axes of the slice: x: 4, y: 4, z: 4 (z_hi: 2, z_lo: 2; z = z_hi * 2 + z_lo), core: 2. Of those that a mesh axis runs over, the one named last changes fastest.
Arguments:
- queries: bfloat16 [8, 2048, 8192], P('pipe', 'ctx', 'tp'), may hold values from -16 to 16
- key_codes: bfloat16 [8, 2048, 512], P('pipe', 'ctx', 'tp'), may hold values from -127 to 127
- value_codes: bfloat16 [8, 2048, 512], P('pipe', 'ctx', 'tp'), may hold values from -127 to 127
- kv_scales: float32 [8, 16, 8], P('pipe', 'ctx'), may hold values from 0.004 to 0.032
- saved_out: bfloat16 [8, 2048, 8192], P('pipe', 'ctx', 'tp'), may hold values from -6 to 6
- section_grads: bfloat16 [8, 2048, 8192], P('pipe', 'ctx', 'tp'), may hold values from -6 to 6
- block_order: int32 [16], replicated, may hold values from 0 to 15, as said below
- block_docs: int32 [16], replicated, may hold values from 0 to 2, never falling along the last dimension, each value on 1 to 9 neighbouring positions
Outputs:
- grad_queries: bfloat16 [8, 2048, 8192], P('pipe', 'ctx', 'tp')
- grad_keys: bfloat16 [8, 2048, 512], P('pipe', ('ctx', 'tp'))
- grad_values: bfloat16 [8, 2048, 512], P('pipe', ('ctx', 'tp'))
Inputs may be any that keep to these rules, and one draw needn't show every extreme that they name: `block_order`: a permutation of the 16 sequence blocks; stored blocks 2 d and 2 d + 1 are sequence blocks p and 15 - p for some p.
All inputs are finite; a program needn't handle non-finite values.
Results may differ from a plain program's by a relative error of at most 0.0072.
Values may be sent and summed in bfloat16 or wider, within the bound.
No kernel may reach another device: no remote copies, remote signals or barrier semaphores. Data moves between devices by JAX's collectives and lax.ppermute only.
A program may use at most 192 MiB of HBM per device.

v0:
```python
import jax
import jax.numpy as jnp
from jax import lax
from jax.sharding import PartitionSpec as P

HQ = 64
KVH = 4
HD = 128


masked_floor = -1e30


def from_behind(array, axis, by):
    size = lax.axis_size(axis)
    return lax.ppermute(array, axis, [(i, (i + by) % size) for i in range(size)])


def dequantize(codes, scales, block_rows, kv_here):
    rows_here = codes.shape[0]
    expanded = jnp.repeat(scales, block_rows, axis=0)
    values = codes.astype(jnp.float32).reshape(rows_here, kv_here, HD) * expanded[:, :, None]
    return values.astype(jnp.bfloat16).reshape(rows_here, kv_here * HD)


def on_device(
    queries, key_codes, value_codes, kv_scales, saved_out, section_grads, block_order, block_docs
):
    rows_here = queries.shape[1]
    block_rows = rows_here // 2
    kv_here = key_codes.shape[2] // HD
    repeats = HQ // KVH
    heads_here = queries.shape[2] // HD
    width_kv = kv_here * HD
    cycle_size = lax.axis_size("ctx")
    cycle_index = lax.axis_index("ctx")
    head_index = lax.axis_index("tp")
    inverse = HD ** (-0.5)
    incoming = from_behind(section_grads, "pipe", -1)
    key_scale = lax.dynamic_slice_in_dim(kv_scales[0], head_index * kv_here, kv_here, 1)
    value_scale = lax.dynamic_slice_in_dim(kv_scales[0], KVH + head_index * kv_here, kv_here, 1)
    keys = dequantize(key_codes[0], key_scale, block_rows, kv_here)
    values = dequantize(value_codes[0], value_scale, block_rows, kv_here)
    key_value = jnp.stack([keys, values])
    query = queries[0].reshape(rows_here, kv_here, repeats, HD)
    grad_out = incoming[0].reshape(rows_here, kv_here, repeats, HD)
    forward_out = saved_out[0].reshape(rows_here, kv_here, repeats, HD)
    block_ids = jnp.arange(block_order.shape[0], dtype=jnp.int32)

    def seq_block(rows):
        hit = (rows // block_rows)[:, None] == block_ids[None, :]
        return jnp.sum(jnp.where(hit, block_order[None, :], 0), axis=1)

    def document(blocks):
        hit = blocks[:, None] == block_ids[None, :]
        return jnp.sum(jnp.where(hit, block_docs[None, :], 0), axis=1)

    query_rows = cycle_index * rows_here + jnp.arange(rows_here, dtype=jnp.int32)
    query_block = seq_block(query_rows)
    query_pos = query_block * block_rows + query_rows % block_rows
    query_doc = document(query_block)

    def allowed(offset, count_rows):
        key_rows = offset + jnp.arange(count_rows, dtype=jnp.int32)
        key_block = seq_block(key_rows)
        key_pos = key_block * block_rows + key_rows % block_rows
        key_doc = document(key_block)
        return (key_pos[None, :] <= query_pos[:, None]) & (key_doc[None, :] == query_doc[:, None])

    def logits(key_piece):
        shaped = key_piece.reshape(-1, kv_here, HD)
        return (
            jnp.einsum("igrd,jgd->grij", query, shaped, preferred_element_type=jnp.float32)
            * inverse
        )

    piece = lax.all_gather(keys, "ctx", axis=0, tiled=True)
    running_max = jnp.full((kv_here, repeats, rows_here), masked_floor, jnp.float32)
    scores = logits(piece)
    visible = allowed(jnp.int32(0), piece.shape[0])[None, None]
    new_max = jnp.maximum(running_max, jnp.max(jnp.where(visible, scores, masked_floor), axis=-1))
    weights = jnp.where(visible, jnp.exp(scores - new_max[..., None]), 0.0)
    new_sum = jnp.sum(weights, axis=-1)
    log_norm = new_max + jnp.log(new_sum)
    row_dots = jnp.transpose(
        jnp.sum(grad_out.astype(jnp.float32) * forward_out.astype(jnp.float32), axis=-1), (1, 2, 0)
    )

    def block_grads(pair_block, offset):
        key_piece = pair_block[0].reshape(rows_here, kv_here, HD)
        value_piece = pair_block[1].reshape(rows_here, kv_here, HD)
        scores = logits(pair_block[0])
        visible = allowed(offset, rows_here)[None, None]
        probs = jnp.where(visible, jnp.exp(scores - log_norm[..., None]), 0.0)
        dprobs = jnp.einsum(
            "igrd,jgd->grij", grad_out, value_piece, preferred_element_type=jnp.float32
        )
        dscores = (probs * (dprobs - row_dots[..., None]) * inverse).astype(jnp.bfloat16)
        probs_low = probs.astype(jnp.bfloat16)
        grad_query = jnp.einsum(
            "grij,jgd->igrd", dscores, key_piece, preferred_element_type=jnp.float32
        )
        grad_key = jnp.einsum("grij,igrd->jgd", dscores, query, preferred_element_type=jnp.float32)
        grad_value = jnp.einsum(
            "grij,igrd->jgd", probs_low, grad_out, preferred_element_type=jnp.float32
        )
        return (
            grad_query,
            jnp.stack(
                [grad_key.reshape(rows_here, width_kv), grad_value.reshape(rows_here, width_kv)]
            ),
        )

    def anchor_slot(turn_index):
        return (cycle_index - turn_index) % cycle_size

    def advance(turn_index, carried, final_turn):
        current, partial_grads, grad_query = carried
        slot = anchor_slot(turn_index)
        query_term, pair_term = block_grads(current, slot * rows_here)
        grad_query = grad_query + query_term
        partial_grads = from_behind(partial_grads + pair_term, "ctx", 1)
        if not final_turn:
            current = from_behind(current, "ctx", 1)
        return (current, partial_grads, grad_query)

    start_grads = jnp.zeros((2, rows_here, width_kv), jnp.float32)
    start_query = jnp.zeros((rows_here, kv_here, repeats, HD), jnp.float32)
    carried = (key_value, start_grads, start_query)
    carried = lax.fori_loop(
        0,
        cycle_size - 1,
        lambda turn_index, state_now: advance(turn_index, state_now, False),
        carried,
    )
    carried = advance(cycle_size - 1, carried, True)
    current, partial_grads, grad_query = carried
    rounded = partial_grads.astype(jnp.bfloat16)
    regrouped = lax.all_to_all(rounded, "tp", split_axis=1, concat_axis=2, tiled=True)
    grad_queries = grad_query.astype(jnp.bfloat16).reshape(1, rows_here, heads_here * HD)
    grad_keys = regrouped[0][None]
    grad_values = regrouped[1][None]
    return (grad_queries, grad_keys, grad_values)


def solution(mesh):
    in_specs = (
        P("pipe", "ctx", "tp"),
        P("pipe", "ctx", "tp"),
        P("pipe", "ctx", "tp"),
        P("pipe", "ctx", None),
        P("pipe", "ctx", "tp"),
        P("pipe", "ctx", "tp"),
        P(),
        P(),
    )
    out_specs = (
        P("pipe", "ctx", "tp"),
        P("pipe", ("ctx", "tp"), None),
        P("pipe", ("ctx", "tp"), None),
    )
    return jax.shard_map(
        on_device, mesh=mesh, in_specs=in_specs, out_specs=out_specs, check_vma=False
    )
```

profile of v0, /device:TPU:1, one launch (start us, length us, event | category | flops | bytes accessed | tf_op | source)
XLA Modules:
  0.0 300.6 jit_solution(3861592225460697767)
XLA Ops:
  10.0 4.1 %copy.101 = bf16[1,256,4096]{1,2,0:T(8,128)(2,1)} copy(bf16[1,256,4096]{2,1,0:T(8,128)(2,1)} %param.15) | data formatting | bytes 4194304 | tf_op args[5]
  14.1 4.7 %collective-permute-start.2 = (bf16[1,256,4096]{1,2,0:T(8,128)(2,1)}, bf16[1,256,4096]{1,2,0:T(8,128)(2,1)}, u32[]{:S(2)}, u32[]{:S(2)}) collective-permute-start(bf16[1,256,4096]{1,2,0:T(8,128)(2,1)} %copy.101), channel_id=1, source_target_pairs={{0,112},{16,0},{32,16},{48,32},{64,48},{80,64},{96,80},{112,96},{1... | collective-permute-start | bytes 6291464 | tf_op jit(solution)/shard_map/ppermute | solution.py:16
  19.1 3.3 %copy.98 = bf16[1,256,4096]{1,2,0:T(8,128)(2,1)S(1)} copy(bf16[1,256,4096]{2,1,0:T(8,128)(2,1)} %param.10) | data formatting | bytes 4194304 | tf_op args[0]
  22.5 4.1 %copy.102 = bf16[1,256,4096]{1,2,0:T(8,128)(2,1)} copy(bf16[1,256,4096]{2,1,0:T(8,128)(2,1)} %param.14) | data formatting | bytes 4194304 | tf_op args[4]
  29.9 7.4 %all-gather.2.cloned.1.call-done = bf16[2048,256]{0,1:T(8,128)(2,1)} async-done(((bf16[256,256]{0,1:T(8,128)(2,1)}), bf16[2048,256]{0,1:T(8,128)(2,1)}) %all-gather.2.cloned.1.call-update) | async-done | bytes 1048592 | tf_op jit(solution)/shard_map/all_gather | solution.py:77
  37.3 24.7 %fusion.15 = (f32[2,16,256]{2,1,0:T(8,128)S(1)}, f32[2,2048,256,16]{2,1,3,0:T(8,128)}) fusion(pred[256,2048]{0,1:T(8,128)(4,1)S(1)} %compare_and_fusion.1, bf16[2048,2,128,1]{0,2,3,1:T(8,128)(2,1)} %bitcast.216, bf16[256,2,16,128]{0,3,2,1:T(8,128)(2,1)S(1)} %bitcast.203), kind=kOutput, calls=%fused_computation.31 | convolution fusion | flops 4345290752 | bytes 70811648 | tf_op jit(solution)/shard_map/igrd,jgd->grij/dot_general | solution.py:73
  62.0 21.6 %fusion.18 = f32[2,16,256]{2,1,0:T(8,128)S(1)} fusion(f32[2,2048,256,16]{2,1,3,0:T(8,128)} %get-tuple-element.527, f32[2,16,256]{2,1,0:T(8,128)S(1)} %broadcast_maximum_fusion, pred[256,2048]{0,1:T(8,128)(4,1)S(1)} %compare_and_fusion.1), kind=kLoop, calls=%fused_computation.34 | loop fusion | flops 67100672 | bytes 67698688 | tf_op jit(solution)/shard_map/reduce_sum | solution.py:83
  84.3 3.6 %fusion.25 = f32[256,2,16]{0,2,1:T(8,128)} fusion(bf16[256,2,16,128]{0,3,2,1:T(8,128)(2,1)} %bitcast.209, bf16[256,2,16,128]{0,3,2,1:T(8,128)(2,1)} %bitcast.10), kind=kLoop, calls=%fused_computation.44 | loop fusion | flops 4186112 | bytes 4227072 | tf_op jit(solution)/shard_map/reduce_sum | solution.py:86
  87.9 162.9 %while.22 = (s32[]{:T(128)}, bf16[2,256,256]{1,2,0:T(8,128)(2,1)}, f32[2,256,256]{1,2,0:T(8,128)S(1)}, f32[256,2,16,128]{3,0,2,1:T(8,128)}, s32[]{:T(128)}, /*in...) while((s32[]{:T(128)}, bf16[2,256,256]{1,2,0:T(8,128)(2,1)}, ...), condition=%wide.region_10.11_spmd.clone.clone, body=%wide.region_7.10_spmd.clone.clone.sunk | while | flops 2710010880 | bytes 78294568 | solution.py:130
  91.4 3.3 %fusion.105 = f32[2,256,128,1]{1,2,3,0:T(8,128)S(1)} fusion(bf16[256,2,16,128]{0,3,2,1:T(8,128)(2,1)} %get-tuple-element.660, f32[2,256,256,16]{2,1,3,0:T(8,128)S(1)} %fusion.103, f32[2,16,256]{2,1,0:T(8,128)} %get-tuple-element.659, pred[256,256]{0,1:T(8,128)(4,1)S(1)} %compare_and_fusion.4), kind=kOutput, calls=%fused_computation.10.clone.1 | convolution fusion | flops 545259520 | bytes 10846208 | tf_op jit(solution)/shard_map/while/body/eval_jaxpr/grij,igrd->jgd/dot_general | solution.py:104
  94.8 4.8 %fusion.106 = bf16[2,16,256,256]{2,3,1,0:T(8,128)(2,1)S(1)} fusion(f32[2,256,256,16]{2,1,3,0:T(8,128)S(1)} %fusion.103, f32[2,16,256]{2,1,0:T(8,128)} %get-tuple-element.661, f32[2,16,256]{2,1,0:T(8,128)} %get-tuple-element.659, pred[256,256]{0,1:T(8,128)(4,1)S(1)} %compare_and_fusion.4, bf16[256,2,128,1]{0,2,3,1:T(8,128)(2,1)S(1)} %bitcast.211, ...), kind=kOutput, calls=%fused_computation.4.clone.1 | convolution fusion | flops 551550976 | bytes 14942208 | tf_op jit(solution)/shard_map/while/body/eval_jaxpr/igrd,jgd->grij/dot_general | solution.py:95
  99.6 1.9 copy-done
  103.3 5.9 %bitcast_add_fusion.3 = f32[256,2,16,128]{3,0,2,1:T(8,128)} fusion(f32[256,2,16,128]{3,0,2,1:T(8,128)} %get-tuple-element.634, bf16[2,16,256,256]{2,3,1,0:T(8,128)(2,1)} %copy-done, bf16[256,2,128,1]{0,2,3,1:T(8,128)(2,1)S(1)} %bitcast.206, pred[]{:T(512)S(6)} %compare.52), kind=kOutput, calls=%fused_computation.9.clone.1 | convolution fusion | flops 538968064 | bytes 12713985 | tf_op jit(solution)/shard_map/while/body/eval_jaxpr/grij,jgd->igrd/dot_general | solution.py:100
  110.3 2.5 collective-permute-start
  114.5 3.3 %fusion.105 = f32[2,256,128,1]{1,2,3,0:T(8,128)S(1)} fusion(bf16[256,2,16,128]{0,3,2,1:T(8,128)(2,1)} %get-tuple-element.660, f32[2,256,256,16]{2,1,3,0:T(8,128)S(1)} %fusion.103, f32[2,16,256]{2,1,0:T(8,128)} %get-tuple-element.659, pred[256,256]{0,1:T(8,128)(4,1)S(1)} %compare_and_fusion.4), kind=kOutput, calls=%fused_computation.10.clone.1 | convolution fusion | flops 545259520 | bytes 10846208 | tf_op jit(solution)/shard_map/while/body/eval_jaxpr/grij,igrd->jgd/dot_general | solution.py:104
  117.8 4.8 %fusion.106 = bf16[2,16,256,256]{2,3,1,0:T(8,128)(2,1)S(1)} fusion(f32[2,256,256,16]{2,1,3,0:T(8,128)S(1)} %fusion.103, f32[2,16,256]{2,1,0:T(8,128)} %get-tuple-element.661, f32[2,16,256]{2,1,0:T(8,128)} %get-tuple-element.659, pred[256,256]{0,1:T(8,128)(4,1)S(1)} %compare_and_fusion.4, bf16[256,2,128,1]{0,2,3,1:T(8,128)(2,1)S(1)} %bitcast.211, ...), kind=kOutput, calls=%fused_computation.4.clone.1 | convolution fusion | flops 551550976 | bytes 14942208 | tf_op jit(solution)/shard_map/while/body/eval_jaxpr/igrd,jgd->grij/dot_general | solution.py:95
  122.6 1.9 copy-done
  126.1 7.2 %bitcast_add_fusion.3 = f32[256,2,16,128]{3,0,2,1:T(8,128)} fusion(f32[256,2,16,128]{3,0,2,1:T(8,128)} %get-tuple-element.634, bf16[2,16,256,256]{2,3,1,0:T(8,128)(2,1)} %copy-done, bf16[256,2,128,1]{0,2,3,1:T(8,128)(2,1)S(1)} %bitcast.206, pred[]{:T(512)S(6)} %compare.52), kind=kOutput, calls=%fused_computation.9.clone.1 | convolution fusion | flops 538968064 | bytes 12713985 | tf_op jit(solution)/shard_map/while/body/eval_jaxpr/grij,jgd->igrd/dot_general | solution.py:100
  137.8 3.3 %fusion.105 = f32[2,256,128,1]{1,2,3,0:T(8,128)S(1)} fusion(bf16[256,2,16,128]{0,3,2,1:T(8,128)(2,1)} %get-tuple-element.660, f32[2,256,256,16]{2,1,3,0:T(8,128)S(1)} %fusion.103, f32[2,16,256]{2,1,0:T(8,128)} %get-tuple-element.659, pred[256,256]{0,1:T(8,128)(4,1)S(1)} %compare_and_fusion.4), kind=kOutput, calls=%fused_computation.10.clone.1 | convolution fusion | flops 545259520 | bytes 10846208 | tf_op jit(solution)/shard_map/while/body/eval_jaxpr/grij,igrd->jgd/dot_general | solution.py:104
  141.1 4.7 %fusion.106 = bf16[2,16,256,256]{2,3,1,0:T(8,128)(2,1)S(1)} fusion(f32[2,256,256,16]{2,1,3,0:T(8,128)S(1)} %fusion.103, f32[2,16,256]{2,1,0:T(8,128)} %get-tuple-element.661, f32[2,16,256]{2,1,0:T(8,128)} %get-tuple-element.659, pred[256,256]{0,1:T(8,128)(4,1)S(1)} %compare_and_fusion.4, bf16[256,2,128,1]{0,2,3,1:T(8,128)(2,1)S(1)} %bitcast.211, ...), kind=kOutput, calls=%fused_computation.4.clone.1 | convolution fusion | flops 551550976 | bytes 14942208 | tf_op jit(solution)/shard_map/while/body/eval_jaxpr/igrd,jgd->grij/dot_general | solution.py:95
  145.9 1.9 copy-done
  149.4 7.2 %bitcast_add_fusion.3 = f32[256,2,16,128]{3,0,2,1:T(8,128)} fusion(f32[256,2,16,128]{3,0,2,1:T(8,128)} %get-tuple-element.634, bf16[2,16,256,256]{2,3,1,0:T(8,128)(2,1)} %copy-done, bf16[256,2,128,1]{0,2,3,1:T(8,128)(2,1)S(1)} %bitcast.206, pred[]{:T(512)S(6)} %compare.52), kind=kOutput, calls=%fused_computation.9.clone.1 | convolution fusion | flops 538968064 | bytes 12713985 | tf_op jit(solution)/shard_map/while/body/eval_jaxpr/grij,jgd->igrd/dot_general | solution.py:100
  160.6 3.3 %fusion.105 = f32[2,256,128,1]{1,2,3,0:T(8,128)S(1)} fusion(bf16[256,2,16,128]{0,3,2,1:T(8,128)(2,1)} %get-tuple-element.660, f32[2,256,256,16]{2,1,3,0:T(8,128)S(1)} %fusion.103, f32[2,16,256]{2,1,0:T(8,128)} %get-tuple-element.659, pred[256,256]{0,1:T(8,128)(4,1)S(1)} %compare_and_fusion.4), kind=kOutput, calls=%fused_computation.10.clone.1 | convolution fusion | flops 545259520 | bytes 10846208 | tf_op jit(solution)/shard_map/while/body/eval_jaxpr/grij,igrd->jgd/dot_general | solution.py:104
  164.0 4.8 %fusion.106 = bf16[2,16,256,256]{2,3,1,0:T(8,128)(2,1)S(1)} fusion(f32[2,256,256,16]{2,1,3,0:T(8,128)S(1)} %fusion.103, f32[2,16,256]{2,1,0:T(8,128)} %get-tuple-element.661, f32[2,16,256]{2,1,0:T(8,128)} %get-tuple-element.659, pred[256,256]{0,1:T(8,128)(4,1)S(1)} %compare_and_fusion.4, bf16[256,2,128,1]{0,2,3,1:T(8,128)(2,1)S(1)} %bitcast.211, ...), kind=kOutput, calls=%fused_computation.4.clone.1 | convolution fusion | flops 551550976 | bytes 14942208 | tf_op jit(solution)/shard_map/while/body/eval_jaxpr/igrd,jgd->grij/dot_general | solution.py:95
  172.2 7.2 %bitcast_add_fusion.3 = f32[256,2,16,128]{3,0,2,1:T(8,128)} fusion(f32[256,2,16,128]{3,0,2,1:T(8,128)} %get-tuple-element.634, bf16[2,16,256,256]{2,3,1,0:T(8,128)(2,1)} %copy-done, bf16[256,2,128,1]{0,2,3,1:T(8,128)(2,1)S(1)} %bitcast.206, pred[]{:T(512)S(6)} %compare.52), kind=kOutput, calls=%fused_computation.9.clone.1 | convolution fusion | flops 538968064 | bytes 12713985 | tf_op jit(solution)/shard_map/while/body/eval_jaxpr/grij,jgd->igrd/dot_general | solution.py:100
  180.4 2.0 collective-permute-start
  184.0 3.3 %fusion.105 = f32[2,256,128,1]{1,2,3,0:T(8,128)S(1)} fusion(bf16[256,2,16,128]{0,3,2,1:T(8,128)(2,1)} %get-tuple-element.660, f32[2,256,256,16]{2,1,3,0:T(8,128)S(1)} %fusion.103, f32[2,16,256]{2,1,0:T(8,128)} %get-tuple-element.659, pred[256,256]{0,1:T(8,128)(4,1)S(1)} %compare_and_fusion.4), kind=kOutput, calls=%fused_computation.10.clone.1 | convolution fusion | flops 545259520 | bytes 10846208 | tf_op jit(solution)/shard_map/while/body/eval_jaxpr/grij,igrd->jgd/dot_general | solution.py:104
  187.3 4.7 %fusion.106 = bf16[2,16,256,256]{2,3,1,0:T(8,128)(2,1)S(1)} fusion(f32[2,256,256,16]{2,1,3,0:T(8,128)S(1)} %fusion.103, f32[2,16,256]{2,1,0:T(8,128)} %get-tuple-element.661, f32[2,16,256]{2,1,0:T(8,128)} %get-tuple-element.659, pred[256,256]{0,1:T(8,128)(4,1)S(1)} %compare_and_fusion.4, bf16[256,2,128,1]{0,2,3,1:T(8,128)(2,1)S(1)} %bitcast.211, ...), kind=kOutput, calls=%fused_computation.4.clone.1 | convolution fusion | flops 551550976 | bytes 14942208 | tf_op jit(solution)/shard_map/while/body/eval_jaxpr/igrd,jgd->grij/dot_general | solution.py:95
  192.1 1.9 copy-done
  195.6 7.2 %bitcast_add_fusion.3 = f32[256,2,16,128]{3,0,2,1:T(8,128)} fusion(f32[256,2,16,128]{3,0,2,1:T(8,128)} %get-tuple-element.634, bf16[2,16,256,256]{2,3,1,0:T(8,128)(2,1)} %copy-done, bf16[256,2,128,1]{0,2,3,1:T(8,128)(2,1)S(1)} %bitcast.206, pred[]{:T(512)S(6)} %compare.52), kind=kOutput, calls=%fused_computation.9.clone.1 | convolution fusion | flops 538968064 | bytes 12713985 | tf_op jit(solution)/shard_map/while/body/eval_jaxpr/grij,jgd->igrd/dot_general | solution.py:100
  203.7 2.6 collective-permute-start
  208.0 3.3 %fusion.105 = f32[2,256,128,1]{1,2,3,0:T(8,128)S(1)} fusion(bf16[256,2,16,128]{0,3,2,1:T(8,128)(2,1)} %get-tuple-element.660, f32[2,256,256,16]{2,1,3,0:T(8,128)S(1)} %fusion.103, f32[2,16,256]{2,1,0:T(8,128)} %get-tuple-element.659, pred[256,256]{0,1:T(8,128)(4,1)S(1)} %compare_and_fusion.4), kind=kOutput, calls=%fused_computation.10.clone.1 | convolution fusion | flops 545259520 | bytes 10846208 | tf_op jit(solution)/shard_map/while/body/eval_jaxpr/grij,igrd->jgd/dot_general | solution.py:104
  211.4 4.8 %fusion.106 = bf16[2,16,256,256]{2,3,1,0:T(8,128)(2,1)S(1)} fusion(f32[2,256,256,16]{2,1,3,0:T(8,128)S(1)} %fusion.103, f32[2,16,256]{2,1,0:T(8,128)} %get-tuple-element.661, f32[2,16,256]{2,1,0:T(8,128)} %get-tuple-element.659, pred[256,256]{0,1:T(8,128)(4,1)S(1)} %compare_and_fusion.4, bf16[256,2,128,1]{0,2,3,1:T(8,128)(2,1)S(1)} %bitcast.211, ...), kind=kOutput, calls=%fused_computation.4.clone.1 | convolution fusion | flops 551550976 | bytes 14942208 | tf_op jit(solution)/shard_map/while/body/eval_jaxpr/igrd,jgd->grij/dot_general | solution.py:95
  216.1 1.9 copy-done
  219.6 7.2 %bitcast_add_fusion.3 = f32[256,2,16,128]{3,0,2,1:T(8,128)} fusion(f32[256,2,16,128]{3,0,2,1:T(8,128)} %get-tuple-element.634, bf16[2,16,256,256]{2,3,1,0:T(8,128)(2,1)} %copy-done, bf16[256,2,128,1]{0,2,3,1:T(8,128)(2,1)S(1)} %bitcast.206, pred[]{:T(512)S(6)} %compare.52), kind=kOutput, calls=%fused_computation.9.clone.1 | convolution fusion | flops 538968064 | bytes 12713985 | tf_op jit(solution)/shard_map/while/body/eval_jaxpr/grij,jgd->igrd/dot_general | solution.py:100
  227.8 2.6 collective-permute-start
  232.0 3.3 %fusion.105 = f32[2,256,128,1]{1,2,3,0:T(8,128)S(1)} fusion(bf16[256,2,16,128]{0,3,2,1:T(8,128)(2,1)} %get-tuple-element.660, f32[2,256,256,16]{2,1,3,0:T(8,128)S(1)} %fusion.103, f32[2,16,256]{2,1,0:T(8,128)} %get-tuple-element.659, pred[256,256]{0,1:T(8,128)(4,1)S(1)} %compare_and_fusion.4), kind=kOutput, calls=%fused_computation.10.clone.1 | convolution fusion | flops 545259520 | bytes 10846208 | tf_op jit(solution)/shard_map/while/body/eval_jaxpr/grij,igrd->jgd/dot_general | solution.py:104
  235.4 4.7 %fusion.106 = bf16[2,16,256,256]{2,3,1,0:T(8,128)(2,1)S(1)} fusion(f32[2,256,256,16]{2,1,3,0:T(8,128)S(1)} %fusion.103, f32[2,16,256]{2,1,0:T(8,128)} %get-tuple-element.661, f32[2,16,256]{2,1,0:T(8,128)} %get-tuple-element.659, pred[256,256]{0,1:T(8,128)(4,1)S(1)} %compare_and_fusion.4, bf16[256,2,128,1]{0,2,3,1:T(8,128)(2,1)S(1)} %bitcast.211, ...), kind=kOutput, calls=%fused_computation.4.clone.1 | convolution fusion | flops 551550976 | bytes 14942208 | tf_op jit(solution)/shard_map/while/body/eval_jaxpr/igrd,jgd->grij/dot_general | solution.py:95
  240.1 1.9 copy-done
  243.6 7.2 %bitcast_add_fusion.3 = f32[256,2,16,128]{3,0,2,1:T(8,128)} fusion(f32[256,2,16,128]{3,0,2,1:T(8,128)} %get-tuple-element.634, bf16[2,16,256,256]{2,3,1,0:T(8,128)(2,1)} %copy-done, bf16[256,2,128,1]{0,2,3,1:T(8,128)(2,1)S(1)} %bitcast.206, pred[]{:T(512)S(6)} %compare.52), kind=kOutput, calls=%fused_computation.9.clone.1 | convolution fusion | flops 538968064 | bytes 12713985 | tf_op jit(solution)/shard_map/while/body/eval_jaxpr/grij,jgd->igrd/dot_general | solution.py:100
  253.1 5.0 %fusion.27 = f32[2,256,128,1]{1,2,3,0:T(8,128)S(1)} fusion(bf16[256,2,16,128]{0,3,2,1:T(8,128)(2,1)} %bitcast.10, f32[2,256,256,16]{2,1,3,0:T(8,128)S(1)} %fusion.53, f32[2,16,256]{2,1,0:T(8,128)} %log_add_fusion, pred[256,256]{0,1:T(8,128)(4,1)S(1)} %copy-done.4), kind=kOutput, calls=%fused_computation.47 | convolution fusion | flops 545259520 | bytes 10846208 | tf_op jit(solution)/shard_map/grij,igrd->jgd/dot_general | solution.py:104
  258.3 6.3 %fusion.21 = bf16[2,16,256,256]{2,3,1,0:T(8,128)(2,1)S(1)} fusion(f32[2,256,256,16]{2,1,3,0:T(8,128)} %copy-done.2, f32[2,16,256]{2,1,0:T(8,128)} %bitcast.12, f32[2,16,256]{2,1,0:T(8,128)} %log_add_fusion, pred[256,256]{0,1:T(8,128)(4,1)S(1)} %copy-done.4, bf16[256,2,128,1]{0,2,3,1:T(8,128)(2,1)S(1)} %bitcast.218, bf16[256,2,16,128]{0,3,2,1:T(8,128)(2,1)} %bitcast.10), kind=kOutput, calls=%fused_computation.38 | convolution fusion | flops 551550976 | bytes 14942208 | tf_op jit(solution)/shard_map/igrd,jgd->grij/dot_general | solution.py:95
  267.4 2.6 collective-permute-start.3
  270.1 5.4 %copy.108 = f32[256,2,16,128]{0,3,2,1:T(8,128)} copy(f32[256,2,16,128]{3,0,2,1:T(8,128)} %get-tuple-element.384) | data formatting | bytes 8388608 | tf_op jit(solution)/shard_map/while | solution.py:130
  275.5 4.9 %fusion.54 = f32[2,128,16,256]{3,1,2,0:T(8,128)} fusion(bf16[256,2,128,1]{0,2,3,1:T(8,128)(2,1)S(1)} %bitcast.214, bf16[2,16,256,256]{2,3,1,0:T(8,128)(2,1)} %copy-done.1), kind=kOutput, calls=%fused_computation.118 | convolution fusion | flops 536870912 | bytes 8519680 | tf_op jit(solution)/shard_map/grij,jgd->igrd/dot_general | solution.py:100
  280.4 4.1 %all-to-all-start = ((bf16[2,256,256]{2,0,1:T(2,128)(2,1)}), bf16[2,256,256]{2,0,1:T(2,128)(2,1)S(1)}, u32[]{:S(2)}, u32[]{:S(2)}) async-start(bf16[2,256,256]{2,0,1:T(2,128)(2,1)} %collective-permute-done.3), calls=%async_computation | async-start | bytes 524288 | tf_op jit(solution)/shard_map/all_to_all | solution.py:139
  284.5 4.1 %fusion.26 = bf16[256,2,16,128]{0,3,2,1:T(8,128)(2,1)S(1)} fusion(f32[256,2,16,128]{0,3,2,1:T(8,128)} %copy.108, f32[2,128,16,256]{3,1,2,0:T(8,128)} %fusion.54), kind=kLoop, calls=%fused_computation.46 | loop fusion | flops 2097152 | bytes 10485760 | tf_op jit(solution)/shard_map/convert_element_type | solution.py:140
  288.6 2.9 copy.116
  (159 shorter events, 50.0 us)
Async XLA Ops:
  7.2 11.7 %copy-start.5 = (s32[16]{0:T(128)S(1)}, s32[16]{0:T(128)}, u32[]{:S(2)}) copy-start(s32[16]{0:T(128)} %param.16) | copy-start | bytes 196
  7.2 30.1 %all-gather.2.cloned.1.call-start = ((), (), s32[]{:S(2)}) async-start(), calls=%async_computation.1 | async-start | bytes 1179648 | tf_op jit(solution)/shard_map/all_gather | solution.py:77
  9.9 12.4 %copy-start.3 = (bf16[1,256,256]{2,1,0:T(8,128)(2,1)S(1)}, bf16[1,256,256]{2,1,0:T(8,128)(2,1)}, u32[]{:S(2)}) copy-start(bf16[1,256,256]{2,1,0:T(8,128)(2,1)} %param.12) | copy-start | bytes 393220
  14.1 70.2 %collective-permute-start.2 = (bf16[1,256,4096]{1,2,0:T(8,128)(2,1)}, bf16[1,256,4096]{1,2,0:T(8,128)(2,1)}, u32[]{:S(2)}, u32[]{:S(2)}) collective-permute-start(bf16[1,256,4096]{1,2,0:T(8,128)(2,1)} %copy.101), channel_id=1, source_target_pairs={{0,112},{16,0},{32,16},{48,32},{64,48},{80,64},{96,80},{112,96},{1... | collective-permute-start | bytes 6291464 | tf_op jit(solution)/shard_map/ppermute | solution.py:16
  19.1 7.6 %copy-start.6 = (s32[16]{0:T(128)S(1)}, s32[16]{0:T(128)}, u32[]{:S(2)}) copy-start(s32[16]{0:T(128)} %param.17) | copy-start | bytes 196
  89.1 20.1 %collective-permute-start = (bf16[2,256,256]{1,2,0:T(8,128)(2,1)S(1)}, bf16[2,256,256]{1,2,0:T(8,128)(2,1)}, u32[]{:S(2)}, u32[]{:S(2)}) collective-permute-start(bf16[2,256,256]{1,2,0:T(8,128)(2,1)S(1)} %copy.162), channel_id=1, source_target_pairs={{0,2},{2,4},{4,6},{6,8},{8,10},{10,12},{12,14},{14,0},{1,3},{3,5},... | collective-permute-start | bytes 786440 | tf_op jit(solution)/shard_map/while/body/eval_jaxpr/ppermute | solution.py:16
  99.6 1.9 copy-start
  103.0 6.4 %collective-permute-start.1 = (f32[2,256,256]{1,2,0:T(8,128)S(1)}, f32[2,256,256]{1,2,0:T(8,128)S(1)}, u32[]{:S(2)}, u32[]{:S(2)}) collective-permute-start(f32[2,256,256]{1,2,0:T(8,128)S(1)} %maximum_add_fusion.3), channel_id=1, source_target_pairs={{0,2},{2,4},{4,6},{6,8},{8,10},{10,12},{12,14},{14,0},{1,3},{3,5},... | collective-permute-start | bytes 1572872 | tf_op jit(solution)/shard_map/while/body/eval_jaxpr/ppermute | solution.py:16
  110.3 22.9 %collective-permute-start = (bf16[2,256,256]{1,2,0:T(8,128)(2,1)S(1)}, bf16[2,256,256]{1,2,0:T(8,128)(2,1)}, u32[]{:S(2)}, u32[]{:S(2)}) collective-permute-start(bf16[2,256,256]{1,2,0:T(8,128)(2,1)S(1)} %copy.162), channel_id=1, source_target_pairs={{0,2},{2,4},{4,6},{6,8},{8,10},{10,12},{12,14},{14,0},{1,3},{3,5},... | collective-permute-start | bytes 786440 | tf_op jit(solution)/shard_map/while/body/eval_jaxpr/ppermute | solution.py:16
  122.6 1.9 copy-start
  126.1 7.2 %collective-permute-start.1 = (f32[2,256,256]{1,2,0:T(8,128)S(1)}, f32[2,256,256]{1,2,0:T(8,128)S(1)}, u32[]{:S(2)}, u32[]{:S(2)}) collective-permute-start(f32[2,256,256]{1,2,0:T(8,128)S(1)} %maximum_add_fusion.3), channel_id=1, source_target_pairs={{0,2},{2,4},{4,6},{6,8},{8,10},{10,12},{12,14},{14,0},{1,3},{3,5},... | collective-permute-start | bytes 1572872 | tf_op jit(solution)/shard_map/while/body/eval_jaxpr/ppermute | solution.py:16
  134.2 22.3 %collective-permute-start = (bf16[2,256,256]{1,2,0:T(8,128)(2,1)S(1)}, bf16[2,256,256]{1,2,0:T(8,128)(2,1)}, u32[]{:S(2)}, u32[]{:S(2)}) collective-permute-start(bf16[2,256,256]{1,2,0:T(8,128)(2,1)S(1)} %copy.162), channel_id=1, source_target_pairs={{0,2},{2,4},{4,6},{6,8},{8,10},{10,12},{12,14},{14,0},{1,3},{3,5},... | collective-permute-start | bytes 786440 | tf_op jit(solution)/shard_map/while/body/eval_jaxpr/ppermute | solution.py:16
  145.9 1.9 copy-start
  149.4 7.2 %collective-permute-start.1 = (f32[2,256,256]{1,2,0:T(8,128)S(1)}, f32[2,256,256]{1,2,0:T(8,128)S(1)}, u32[]{:S(2)}, u32[]{:S(2)}) collective-permute-start(f32[2,256,256]{1,2,0:T(8,128)S(1)} %maximum_add_fusion.3), channel_id=1, source_target_pairs={{0,2},{2,4},{4,6},{6,8},{8,10},{10,12},{12,14},{14,0},{1,3},{3,5},... | collective-permute-start | bytes 1572872 | tf_op jit(solution)/shard_map/while/body/eval_jaxpr/ppermute | solution.py:16
  157.5 21.9 %collective-permute-start = (bf16[2,256,256]{1,2,0:T(8,128)(2,1)S(1)}, bf16[2,256,256]{1,2,0:T(8,128)(2,1)}, u32[]{:S(2)}, u32[]{:S(2)}) collective-permute-start(bf16[2,256,256]{1,2,0:T(8,128)(2,1)S(1)} %copy.162), channel_id=1, source_target_pairs={{0,2},{2,4},{4,6},{6,8},{8,10},{10,12},{12,14},{14,0},{1,3},{3,5},... | collective-permute-start | bytes 786440 | tf_op jit(solution)/shard_map/while/body/eval_jaxpr/ppermute | solution.py:16
  168.7 1.9 copy-start
  172.2 7.2 %collective-permute-start.1 = (f32[2,256,256]{1,2,0:T(8,128)S(1)}, f32[2,256,256]{1,2,0:T(8,128)S(1)}, u32[]{:S(2)}, u32[]{:S(2)}) collective-permute-start(f32[2,256,256]{1,2,0:T(8,128)S(1)} %maximum_add_fusion.3), channel_id=1, source_target_pairs={{0,2},{2,4},{4,6},{6,8},{8,10},{10,12},{12,14},{14,0},{1,3},{3,5},... | collective-permute-start | bytes 1572872 | tf_op jit(solution)/shard_map/while/body/eval_jaxpr/ppermute | solution.py:16
  180.4 22.4 %collective-permute-start = (bf16[2,256,256]{1,2,0:T(8,128)(2,1)S(1)}, bf16[2,256,256]{1,2,0:T(8,128)(2,1)}, u32[]{:S(2)}, u32[]{:S(2)}) collective-permute-start(bf16[2,256,256]{1,2,0:T(8,128)(2,1)S(1)} %copy.162), channel_id=1, source_target_pairs={{0,2},{2,4},{4,6},{6,8},{8,10},{10,12},{12,14},{14,0},{1,3},{3,5},... | collective-permute-start | bytes 786440 | tf_op jit(solution)/shard_map/while/body/eval_jaxpr/ppermute | solution.py:16
  192.1 1.9 copy-start
  195.6 7.2 %collective-permute-start.1 = (f32[2,256,256]{1,2,0:T(8,128)S(1)}, f32[2,256,256]{1,2,0:T(8,128)S(1)}, u32[]{:S(2)}, u32[]{:S(2)}) collective-permute-start(f32[2,256,256]{1,2,0:T(8,128)S(1)} %maximum_add_fusion.3), channel_id=1, source_target_pairs={{0,2},{2,4},{4,6},{6,8},{8,10},{10,12},{12,14},{14,0},{1,3},{3,5},... | collective-permute-start | bytes 1572872 | tf_op jit(solution)/shard_map/while/body/eval_jaxpr/ppermute | solution.py:16
  203.7 23.1 %collective-permute-start = (bf16[2,256,256]{1,2,0:T(8,128)(2,1)S(1)}, bf16[2,256,256]{1,2,0:T(8,128)(2,1)}, u32[]{:S(2)}, u32[]{:S(2)}) collective-permute-start(bf16[2,256,256]{1,2,0:T(8,128)(2,1)S(1)} %copy.162), channel_id=1, source_target_pairs={{0,2},{2,4},{4,6},{6,8},{8,10},{10,12},{12,14},{14,0},{1,3},{3,5},... | collective-permute-start | bytes 786440 | tf_op jit(solution)/shard_map/while/body/eval_jaxpr/ppermute | solution.py:16
  216.1 1.9 copy-start
  219.6 7.2 %collective-permute-start.1 = (f32[2,256,256]{1,2,0:T(8,128)S(1)}, f32[2,256,256]{1,2,0:T(8,128)S(1)}, u32[]{:S(2)}, u32[]{:S(2)}) collective-permute-start(f32[2,256,256]{1,2,0:T(8,128)S(1)} %maximum_add_fusion.3), channel_id=1, source_target_pairs={{0,2},{2,4},{4,6},{6,8},{8,10},{10,12},{12,14},{14,0},{1,3},{3,5},... | collective-permute-start | bytes 1572872 | tf_op jit(solution)/shard_map/while/body/eval_jaxpr/ppermute | solution.py:16
  227.8 23.1 %collective-permute-start = (bf16[2,256,256]{1,2,0:T(8,128)(2,1)S(1)}, bf16[2,256,256]{1,2,0:T(8,128)(2,1)}, u32[]{:S(2)}, u32[]{:S(2)}) collective-permute-start(bf16[2,256,256]{1,2,0:T(8,128)(2,1)S(1)} %copy.162), channel_id=1, source_target_pairs={{0,2},{2,4},{4,6},{6,8},{8,10},{10,12},{12,14},{14,0},{1,3},{3,5},... | collective-permute-start | bytes 786440 | tf_op jit(solution)/shard_map/while/body/eval_jaxpr/ppermute | solution.py:16
  240.1 1.9 copy-start
  243.6 7.2 %collective-permute-start.1 = (f32[2,256,256]{1,2,0:T(8,128)S(1)}, f32[2,256,256]{1,2,0:T(8,128)S(1)}, u32[]{:S(2)}, u32[]{:S(2)}) collective-permute-start(f32[2,256,256]{1,2,0:T(8,128)S(1)} %maximum_add_fusion.3), channel_id=1, source_target_pairs={{0,2},{2,4},{4,6},{6,8},{8,10},{10,12},{12,14},{14,0},{1,3},{3,5},... | collective-permute-start | bytes 1572872 | tf_op jit(solution)/shard_map/while/body/eval_jaxpr/ppermute | solution.py:16
  251.8 1.3 copy-start.4
  253.1 5.0 %copy-start.2 = (f32[2,256,256,16]{2,1,3,0:T(8,128)}, f32[2,256,256,16]{2,1,3,0:T(8,128)S(1)}, u32[]{:S(2)}) copy-start(f32[2,256,256,16]{2,1,3,0:T(8,128)S(1)} %fusion.53) | copy-start | bytes 25165828
  264.5 1.9 copy-start.1
  267.4 12.9 %collective-permute-start.3 = (bf16[2,256,256]{2,0,1:T(2,128)(2,1)S(1)}, bf16[2,256,256]{2,0,1:T(2,128)(2,1)}, u32[]{:S(2)}, u32[]{:S(2)}) collective-permute-start(bf16[2,256,256]{2,0,1:T(2,128)(2,1)S(1)} %maximum_add_fusion.1), channel_id=1, source_target_pairs={{0,2},{2,4},{4,6},{6,8},{8,10},{10,12},{12,14},{14,0},{1,3},{3,5},... | collective-permute-start | bytes 786440 | tf_op jit(solution)/shard_map/ppermute | solution.py:16
  280.4 11.1 %all-to-all-start = ((bf16[2,256,256]{2,0,1:T(2,128)(2,1)}), bf16[2,256,256]{2,0,1:T(2,128)(2,1)S(1)}, u32[]{:S(2)}, u32[]{:S(2)}) async-start(bf16[2,256,256]{2,0,1:T(2,128)(2,1)} %collective-permute-done.3), calls=%async_computation | async-start | bytes 524288 | tf_op jit(solution)/shard_map/all_to_all | solution.py:139
Sparse Core Ops, SparseCore 0:
  10.3 26.9 all-gather.1
where the time goes:
time: 304 us; the launch traced here: 301 us
  matrix products  168 us (55%)
  local copies, waits for them, and re-layouts  46.6 us (15%)
  other arithmetic  37.4 us (12%)
  starting transfers between devices  25.6 us (8%)
  between operations  14.3 us (5%)
  waiting for transfers between devices  7.71 us (3%)
    dot_general x8, matrix products, block_grads(): jnp.einsum('grij,jgd->igrd', dscores, key_piece, preferred_element_type=j...  53.9 us
    dot_general x8, matrix products, block_grads(): jnp.einsum('igrd,jgd->grij', grad_out, value_piece, preferred_element_typ...  39.5 us
    dot_general x9, matrix products, logits(): jnp.einsum('igrd,jgd->grij', query, shaped, preferred_element_type=jnp.fl...  35 us
    dot_general x8, matrix products, block_grads(): jnp.einsum('grij,igrd->jgd', probs_low, grad_out, preferred_element_type=...  28.3 us
    reduce_sum x1, other arithmetic, on_device(): new_sum = jnp.sum(weights, axis=-1)  21.6 us
    ppermute x16, starting transfers between devices, from_behind(): lax.ppermute(array, axis, [(i, (i + by) % size) for i in range(size)])  21.4 us
    while x21, local copies, waits for them, and re-layouts  20.1 us
    unnamed x22, local copies, waits for them, and re-layouts  16.1 us
  transfers between devices with their start and end apart: 18, of which 2 were waited for; matrix products, arithmetic and copies ran while one was open for 69% of the time, Pallas kernels for 0%

commit v1 on v0

v1 whole, which is shorter than its diff:
```python
import functools
import math

import jax
import jax.numpy as jnp
from jax import lax
from jax.experimental import pallas as pl
from jax.experimental.pallas import tpu as pltpu
from jax.sharding import PartitionSpec as P

HQ = 64
KVH = 4
HD = 128
BLK = 128
BLOCKS = 16
TOKENS = BLOCKS * BLK
LONGEST = 9
INVERSE = HD**-0.5
INVERSE2 = INVERSE * math.log2(math.e)
NT = (((1,), (1,)), ((), ()))
F32 = jnp.float32
BF16 = jnp.bfloat16

CHUNKS = ((0, 2048), (2048, 1024), (3072, 1024))
GROUP = HQ // KVH * HD
STEP = 512
SMEM = pl.BlockSpec(memory_space=pltpu.SMEM)
VMEM = pl.BlockSpec(memory_space=pltpu.VMEM)


def turned(array, axis, by):
    size = lax.axis_size(axis)
    return lax.ppermute(array, axis, [(i, (i + by) % size) for i in range(size)])


def core_swap(array):
    size = lax.axis_size("ctx")
    return lax.ppermute(array, "ctx", [(i, i ^ 1) for i in range(size)])


def stacked(tile):
    heads = tile.shape[1] // HD
    return jnp.concatenate([tile[:, i * HD : (i + 1) * HD] for i in range(heads)], axis=0)


def dequantize_kernel(place_ref, key_ref, value_ref, scale_ref, out_ref):
    head = place_ref[2] * 2
    for block in range(2):
        rows = slice(block * BLK, (block + 1) * BLK)
        for part, codes in enumerate((key_ref, value_ref)):
            for g in range(2):
                scale = scale_ref[block, part * KVH + head + g]
                tile = codes[rows, g * HD : (g + 1) * HD].astype(F32) * scale
                at = (part * 2 + g) * HD
                out_ref[rows, at : at + HD] = tile.astype(BF16)


def order_kernel(place_ref, order_ref, *refs):
    pieces = (refs[:4], refs[4:8])
    keys_ref, turned_ref, values_ref = refs[8:]
    y = place_ref[0]
    core = place_ref[1]
    for d in range(4):
        from_y = lax.rem(y + 4 - d, 4)
        for which in range(2):
            holder = core if which == 0 else 1 - core
            for block in range(2):
                seq = order_ref[from_y * 4 + holder * 2 + block]
                at = pl.multiple_of(seq * BLK, BLK)
                rows = slice(block * BLK, (block + 1) * BLK)
                tile = pieces[which][d][rows, :]
                for g in range(2):
                    key = tile[:, g * HD : (g + 1) * HD]
                    keys_ref[g, pl.ds(at, BLK), :] = key
                    turned_ref[g, :, pl.ds(at, BLK)] = jnp.transpose(key)
                    values_ref[g, pl.ds(at, BLK), :] = tile[:, (2 + g) * HD : (3 + g) * HD]


def block_pairs(size, start, key_ref, turned_ref, value_ref, q_ref, g_ref, o_ref, dq_ref, dk_ref, dv_ref):
    rows = size * BLK
    first = pl.multiple_of(start * BLK, BLK)
    keys = key_ref[0, pl.ds(first, rows), :]
    values = value_ref[0, pl.ds(first, rows), :]
    keys_turned = turned_ref[0, :, pl.ds(first, rows)]
    lane = lax.broadcasted_iota(jnp.int32, (BLK, HD), 1)
    dots = jnp.zeros((BLK, HD), F32)
    for h in range(STEP // HD):
        columns = slice(h * HD, (h + 1) * HD)
        product = g_ref[:, columns].astype(F32) * o_ref[:, columns].astype(F32)
        dots = jnp.where(lane == h, jnp.sum(product, axis=1, keepdims=True), dots)
    dots = jnp.transpose(dots)
    wide = 2 * HD
    key_index = lax.broadcasted_iota(jnp.int32, (BLK, wide), 0)
    query_index = lax.broadcasted_iota(jnp.int32, (BLK, wide), 1) % BLK
    dk = None
    dv = None
    for part in range(STEP // wide):
        columns = slice(part * wide, (part + 1) * wide)
        query = stacked(q_ref[:, columns])
        grad = stacked(g_ref[:, columns])
        scores = lax.dot_general(keys, query, NT, preferred_element_type=F32)
        dprobs = lax.dot_general(values, grad, NT, preferred_element_type=F32)
        row_dots = jnp.concatenate([dots[part * 2 + i : part * 2 + i + 1] for i in range(2)], axis=1)
        last = jnp.where(key_index <= query_index, scores[rows - BLK :], -jnp.inf)
        scores = last if size == 1 else jnp.concatenate([scores[: rows - BLK], last], axis=0)
        top = jnp.max(scores, axis=0, keepdims=True)
        weights = jnp.exp2((scores - top) * INVERSE2)
        total = jnp.sum(weights, axis=0, keepdims=True)
        probs = weights * (1.0 / total)
        dscores = (probs * (dprobs - row_dots)).astype(BF16)
        dv_part = jnp.dot(probs.astype(BF16), grad, preferred_element_type=F32)
        dk_part = jnp.dot(dscores, query, preferred_element_type=F32)
        dv = dv_part if dv is None else dv + dv_part
        dk = dk_part if dk is None else dk + dk_part
        dq = jnp.dot(keys_turned, dscores, preferred_element_type=F32) * INVERSE
        for i in range(2):
            at = part * wide + i * HD
            dq_ref[:, at : at + HD] = jnp.transpose(dq[:, i * HD : (i + 1) * HD]).astype(BF16)
    dv_ref[pl.ds(first, rows), :] += dv
    dk_ref[pl.ds(first, rows), :] += dk


def chunk_kernel(opens, closes, aliased, place_ref, order_ref, docs_ref, key_ref, turned_ref, value_ref, q_ref, g_ref, o_ref, *refs):
    refs = list(refs)
    sums_in = None if opens else refs.pop(0)
    if aliased:
        refs.pop(0)
    dq_ref = refs.pop(0)
    *out_refs, sums_ref = refs
    step = pl.program_id(0)
    half = pl.program_id(1)

    @pl.when((step == 0) & (half == 0))
    def _():
        sums_ref[...] = jnp.zeros_like(sums_ref) if opens else sums_in[...]

    seq = order_ref[place_ref[0] * 4 + place_ref[1] * 2 + half]
    doc = docs_ref[seq]
    start = jnp.int32(0)
    for b in range(BLOCKS):
        start = start + jnp.where(docs_ref[b] < doc, 1, 0)
    size = seq + 1 - start
    for i in range(1, LONGEST + 1):

        @pl.when(size == i)
        def _():
            block_pairs(
                i, start, key_ref, turned_ref, value_ref, q_ref, g_ref, o_ref, dq_ref, sums_ref.at[0], sums_ref.at[1]
            )

    if closes:

        @pl.when((step == pl.num_programs(0) - 1) & (half == 1))
        def _():
            for block in range(2):
                rows = slice(block * BLK, (block + 1) * BLK)
                for y in range(4):
                    for which in range(2):
                        core = place_ref[1] if which == 0 else 1 - place_ref[1]
                        at = pl.multiple_of(order_ref[y * 4 + core * 2 + block] * BLK, BLK)
                        out_refs[which * 2][y, rows, :] = (sums_ref[0, pl.ds(at, BLK), :] * INVERSE).astype(BF16)
                        out_refs[which * 2 + 1][y, rows, :] = sums_ref[1, pl.ds(at, BLK), :].astype(BF16)


def chunk_call(chunk, place, order, docs, keys, turned_keys, values, queries, grad, saved, sums, dq):
    first, width = chunk
    group = first // GROUP
    opens = first % GROUP == 0
    closes = (first + width) % GROUP == 0
    offset = first // STEP
    head = lambda s: pl.BlockSpec((1,) + s, lambda i, j, *_: (group, 0, 0))
    columns = pl.BlockSpec((BLK, STEP), lambda i, j, *_: (j, i + offset))
    own_columns = pl.BlockSpec((BLK, STEP), lambda i, j, *_: (j, i))
    whole = lambda s: pl.BlockSpec(s, lambda i, j, *_: (0,) * len(s))
    sums_shape = (2, TOKENS, HD)
    in_specs = [head((TOKENS, HD)), head((HD, TOKENS)), head((TOKENS, HD)), columns, own_columns, columns]
    operands = [keys, turned_keys, values, queries, grad, saved]
    if not opens:
        in_specs.append(whole(sums_shape))
        operands.append(sums)
    aliases = {}
    if dq is not None:
        aliases = {3 + len(operands): 0}
        in_specs.append(pl.BlockSpec(memory_space=pl.ANY))
        operands.append(dq)
    out_specs = [columns]
    out_shape = [jax.ShapeDtypeStruct(queries.shape, BF16)]
    scratch = []
    if closes:
        pieces = [jax.ShapeDtypeStruct((4, 2 * BLK, HD), BF16)] * 4
        out_specs += [whole(piece.shape) for piece in pieces]
        out_shape += pieces
        scratch = [pltpu.VMEM(sums_shape, F32)]
    else:
        out_specs.append(whole(sums_shape))
        out_shape.append(jax.ShapeDtypeStruct(sums_shape, F32))
    return pl.pallas_call(
        functools.partial(chunk_kernel, opens, closes, dq is not None),
        grid_spec=pltpu.PrefetchScalarGridSpec(
            num_scalar_prefetch=3,
            grid=(width // STEP, 2),
            in_specs=in_specs,
            out_specs=out_specs,
            scratch_shapes=scratch,
        ),
        out_shape=out_shape,
        input_output_aliases=aliases,
        compiler_params=pltpu.CompilerParams(vmem_limit_bytes=48 << 20),
        cost_estimate=TINY,
    )(place, order, docs, *operands)


def pair_kernel(place_ref, *refs):
    for d in range(4):
        y = lax.rem(place_ref[0] + d, 4)
        for part in range(2):
            columns = slice(part * HD, (part + 1) * HD)
            total = refs[part][y].astype(F32) + refs[2 + part][y].astype(F32)
            refs[4 + d][:, columns] = total.astype(refs[4 + d].dtype)


def chips_kernel(place_ref, *refs):
    groups = (refs[:4], refs[4:8])
    for out_ref, block in ((refs[8], place_ref[2]), (refs[9], 1 - place_ref[2])):
        rows = pl.ds(pl.multiple_of(block * BLK, BLK), BLK)
        for g, sums in enumerate(groups):
            total = sums[0][rows, :]
            for ref in sums[1:]:
                total = total + ref[rows, :].astype(F32)
            out_ref[:, g * 2 * HD : (g + 1) * 2 * HD] = total.astype(BF16)


def join_kernel(place_ref, keep_ref, sent_ref, *out_refs):
    for tp in range(2):
        for g in range(2):
            at = (tp * 2 + g) * HD
            for part in range(2):
                columns = slice((g * 2 + part) * HD, (g * 2 + part + 1) * HD)
                kept = keep_ref[:, columns].astype(F32)
                sent = sent_ref[:, columns].astype(F32)
                out_refs[part][:, at : at + HD] = jnp.where(place_ref[2] == tp, kept, sent).astype(BF16)


def tied(array, *others):
    return lax.optimization_barrier((array,) + others)[0]


TINY = pl.CostEstimate(flops=1_000_000, bytes_accessed=100_000, transcendentals=0)


def pair_sum(place, mine, arrived):
    piece = (2 * BLK, 2 * HD)
    own, *further = pl.pallas_call(
        pair_kernel,
        in_specs=[SMEM] + [VMEM] * 4,
        out_specs=[VMEM] * 4,
        out_shape=[jax.ShapeDtypeStruct(piece, F32)] + [jax.ShapeDtypeStruct(piece, BF16)] * 3,
        cost_estimate=TINY,
    )(place, *mine, *arrived)
    return own, further


def between_chips(further):
    return [turned(further[d - 1], "ctx", 2 * d) for d in range(1, 4)]


def on_device(queries, key_codes, value_codes, kv_scales, saved_out, section_grads, block_order, block_docs):
    pieces = [section_grads[0, :, first : first + width] for first, width in CHUNKS]
    incoming = [turned(pieces[0], "pipe", -1), turned(pieces[1], "pipe", -1)]
    incoming.append(turned(tied(pieces[2], incoming[0]), "pipe", -1))
    ctx = lax.axis_index("ctx")
    place = jnp.stack([ctx // 2, ctx % 2, lax.axis_index("tp")]).astype(jnp.int32)

    pair = pl.pallas_call(
        dequantize_kernel,
        in_specs=[SMEM, VMEM, VMEM, SMEM],
        out_specs=VMEM,
        out_shape=jax.ShapeDtypeStruct((2 * BLK, 4 * HD), BF16),
        cost_estimate=TINY,
    )(place, key_codes[0], value_codes[0], kv_scales[0])
    mine = [pair] + [turned(pair, "ctx", 2 * d) for d in range(1, 4)]
    other = [core_swap(piece) for piece in mine]
    keys, turned_keys, values = pl.pallas_call(
        order_kernel,
        in_specs=[SMEM, SMEM] + [VMEM] * 8,
        out_specs=[VMEM] * 3,
        out_shape=[
            jax.ShapeDtypeStruct((2, TOKENS, HD), BF16),
            jax.ShapeDtypeStruct((2, HD, TOKENS), BF16),
            jax.ShapeDtypeStruct((2, TOKENS, HD), BF16),
        ],
        compiler_params=pltpu.CompilerParams(vmem_limit_bytes=32 << 20),
        cost_estimate=TINY,
    )(place, block_order, *mine, *other)

    shared = (place, block_order, block_docs, keys, turned_keys, values, queries[0])
    dq, *parts0 = chunk_call(CHUNKS[0], *shared, incoming[0], saved_out[0], None, None)
    arrived0 = [core_swap(tied(part, incoming[1])) for part in parts0[2:]]
    dq, sums = chunk_call(CHUNKS[1], *shared, incoming[1], saved_out[0], None, dq)
    own0, further0 = pair_sum(place, parts0[:2], [tied(part, sums) for part in arrived0])
    sums0 = [own0] + between_chips(further0)
    grad2 = tied(incoming[2], own0)
    dq, *parts1 = chunk_call(CHUNKS[2], *shared, grad2, saved_out[0], sums, dq)
    own1, further1 = pair_sum(place, parts1[:2], [core_swap(tied(part, *sums0)) for part in parts1[2:]])
    sums1 = [own1] + between_chips(further1)
    half = jax.ShapeDtypeStruct((BLK, 4 * HD), BF16)
    keep, send = pl.pallas_call(
        chips_kernel, in_specs=[SMEM] + [VMEM] * 8, out_specs=[VMEM] * 2, out_shape=[half] * 2, cost_estimate=TINY
    )(place, *sums0, *sums1)
    out = jax.ShapeDtypeStruct((BLK, KVH * HD), BF16)
    grad_keys, grad_values = pl.pallas_call(
        join_kernel, in_specs=[SMEM] + [VMEM] * 2, out_specs=[VMEM] * 2, out_shape=[out] * 2, cost_estimate=TINY
    )(place, keep, turned(send, "tp", 1))
    return dq[None], grad_keys[None], grad_values[None]


def solution(mesh):
    in_specs = (
        P("pipe", "ctx", "tp"),
        P("pipe", "ctx", "tp"),
        P("pipe", "ctx", "tp"),
        P("pipe", "ctx", None),
        P("pipe", "ctx", "tp"),
        P("pipe", "ctx", "tp"),
        P(),
        P(),
    )
    out_specs = (
        P("pipe", "ctx", "tp"),
        P("pipe", ("ctx", "tp"), None),
        P("pipe", ("ctx", "tp"), None),
    )
    return jax.shard_map(on_device, mesh=mesh, in_specs=in_specs, out_specs=out_specs, check_vma=False)
```

time: 304 us -> 122 us (0.40)
  matrix products: 168 us -> 0 us
  Pallas kernels: 0 us -> 37.7 us
  other arithmetic: 37.4 us -> 0.61 us
  local copies, waits for them, and re-layouts: 46.6 us -> 11.2 us
  starting transfers between devices: 25.6 us -> 53.8 us
  between operations: 14.3 us -> 1.07 us
  waiting for transfers between devices: 7.71 us -> 16.8 us
    dot_general x41 -> x0, matrix products: 168 us -> none  [the longest x8 53.9 us: block_grads(): jnp.einsum('grij,jgd->igrd', dscores, key_piece, preferred_element_type=j...]
    pallas_call x0 -> x9, Pallas kernels: none -> 37.7 us  [the longest x3 26.8 us: chunk_call(): pl.pallas_call(functools.partial(chunk_kernel, opens, closes, dq is not N...]
    ppermute x16 -> x21, starting transfers between devices: 21.4 us -> 53.8 us  [the longest x13 38.1 us: turned(): lax.ppermute(array, axis, [(i, (i + by) % size) for i in range(size)])]
    reduce_sum x20 -> x0, other arithmetic: 26.8 us -> none  [the longest x1 21.6 us: on_device(): new_sum = jnp.sum(weights, axis=-1)]
    while x23 -> x0, local copies, waits for them, and re-layouts: 25.7 us -> none
    ppermute x16 -> x21, waiting for transfers between devices: 0.26 us -> 16.8 us  [the longest x13 15.3 us: turned(): lax.ppermute(array, axis, [(i, (i + by) % size) for i in range(size)])]
    unnamed x22 -> x48, local copies, waits for them, and re-layouts: 16.1 us -> 7.93 us
    all_gather x1 -> x0, waiting for transfers between devices: 7.44 us -> none  [on_device(): piece = lax.all_gather(keys, 'ctx', axis=0, tiled=True)]
  transfers between devices with their start and end apart: 18 -> 21, of which waited for: 2 -> 7; matrix products, arithmetic and copies ran while one was open for 69% -> 1% of each run, Pallas kernels for 0% -> 26%
where the time goes in v1:
time: 122 us; the launch traced here: 121 us
  starting transfers between devices  53.8 us (44%)
  Pallas kernels  37.7 us (31%)
  waiting for transfers between devices  16.8 us (14%)
  local copies, waits for them, and re-layouts  11.2 us (9%)
    ppermute x13, starting transfers between devices, turned(): lax.ppermute(array, axis, [(i, (i + by) % size) for i in range(size)])  38.1 us
    pallas_call x3, Pallas kernels, chunk_call(): pl.pallas_call(functools.partial(chunk_kernel, opens, closes, dq is not N...  26.8 us
    ppermute x8, starting transfers between devices, core_swap(): return lax.ppermute(array, 'ctx', [(i, i ^ 1) for i in range(size)])  15.7 us
    ppermute x13, waiting for transfers between devices, turned(): lax.ppermute(array, axis, [(i, (i + by) % size) for i in range(size)])  15.3 us
    unnamed x48, local copies, waits for them, and re-layouts  7.93 us
    pallas_call x2, Pallas kernels, pair_sum(): pl.pallas_call(pair_kernel, in_specs=[SMEM] + [VMEM] * 4, out_specs=[VMEM...  4.17 us
    squeeze x2, local copies, waits for them, and re-layouts, on_device(): section_grads[0, :, first:first + width]  3.31 us
  transfers between devices with their start and end apart: 21, of which 7 were waited for; matrix products, arithmetic and copies ran while one was open for 1% of the time, Pallas kernels for 26%

profile of v1, /device:TPU:1, one launch (start us, length us, event | category | flops | bytes accessed | tf_op | source)
XLA Modules:
  0.0 121.2 jit_solution(2548867841015365525)
XLA Ops:
  0.7 2.5 %slice_bitcast_fusion = bf16[256,2048]{1,0:T(8,128)(2,1)} fusion(bf16[1,256,4096]{2,1,0:T(8,128)(2,1)} %param.13), kind=kLoop, calls=%fused_computation | loop fusion | bytes 2097152 | tf_op jit(solution)/shard_map/squeeze | solution.py:268
  3.1 4.7 %collective-permute-start.7 = (bf16[256,2048]{1,0:T(8,128)(2,1)}, bf16[256,2048]{1,0:T(8,128)(2,1)S(1)}, u32[]{:S(2)}, u32[]{:S(2)}) collective-permute-start(bf16[256,2048]{1,0:T(8,128)(2,1)} %slice_bitcast_fusion), channel_id=1, source_target_pairs={{0,112},{16,0},{32,16},{48,32},{64,48},{80,64},{96,80},{112,96},{1... | collective-permute-start | bytes 3145736 | tf_op jit(solution)/shard_map/ppermute | solution.py:33
  7.8 0.6 pad_add_fusion.place_ref
  8.4 1.7 %shard_map.103.refs_0_ = bf16[256,512]{1,0:T(8,128)(2,1)} custom-call(s32[3]{0:T(128)} %pad_add_fusion.place_ref, bf16[256,256]{1,0:T(8,128)(2,1)} %bitcast.24, bf16[256,256]{1,0:T(8,128)(2,1)} %bitcast.25, f32[2,8]{1,0:T(2,128)} %bitcast.26), custom_call_target="tpu_custom_call" | custom-call | flops 1000000 | bytes 100000 | tf_op jit(solution)/shard_map/pallas_call | solution.py:274
  10.1 2.7 %collective-permute-start.2 = (bf16[256,512]{1,0:T(8,128)(2,1)}, bf16[256,512]{1,0:T(8,128)(2,1)S(1)}, u32[]{:S(2)}, u32[]{:S(2)}) collective-permute-start(bf16[256,512]{1,0:T(8,128)(2,1)} %shard_map.103.refs_0_), channel_id=1, source_target_pairs={{0,12},{2,14},{4,0},{6,2},{8,4},{10,6},{12,8},{14,10},{1,13},{3,15... | collective-permute-start | bytes 786440 | tf_op jit(solution)/shard_map/ppermute | solution.py:33
  12.9 0.3 collective-permute-start.1
  13.2 0.7 collective-permute-start
  13.9 0.9 slice_bitcast_fusion.1
  14.8 0.5 collective-permute-start.9
  15.3 3.6 %collective-permute-done.2.refs_3_ = bf16[256,512]{1,0:T(8,128)(2,1)S(1)} collective-permute-done((bf16[256,512]{1,0:T(8,128)(2,1)}, bf16[256,512]{1,0:T(8,128)(2,1)S(1)}, u32[]{:S(2)}, u32[]{:S(2)}) %collective-permute-start.2) | collective-permute-done | bytes 262176 | tf_op jit(solution)/shard_map/ppermute | solution.py:33
  18.9 6.4 %collective-permute-start.3 = (bf16[256,512]{1,0:T(8,128)(2,1)S(1)}, bf16[256,512]{1,0:T(8,128)(2,1)S(1)}, u32[]{:S(2)}, u32[]{:S(2)}) collective-permute-start(bf16[256,512]{1,0:T(8,128)(2,1)S(1)} %copy-done.3), channel_id=1, source_target_pairs={{0,2},{2,0},{4,6},{6,4},{8,10},{10,8},{12,14},{14,12},{1,3},{3,1},... | collective-permute-start | bytes 786440 | tf_op jit(solution)/shard_map/ppermute | solution.py:38
  25.4 3.0 %collective-permute-done.refs_1_ = bf16[256,512]{1,0:T(8,128)(2,1)S(1)} collective-permute-done((bf16[256,512]{1,0:T(8,128)(2,1)}, bf16[256,512]{1,0:T(8,128)(2,1)S(1)}, u32[]{:S(2)}, u32[]{:S(2)}) %collective-permute-start) | collective-permute-done | bytes 262176 | tf_op jit(solution)/shard_map/ppermute | solution.py:33
  28.4 0.5 collective-permute-start.5
  28.9 1.0 collective-permute-done.7.g_ref
  29.9 1.0 copy-done.1
  30.9 2.7 %collective-permute-start.4 = (bf16[256,512]{1,0:T(8,128)(2,1)S(1)}, bf16[256,512]{1,0:T(8,128)(2,1)S(1)}, u32[]{:S(2)}, u32[]{:S(2)}) collective-permute-start(bf16[256,512]{1,0:T(8,128)(2,1)S(1)} %collective-permute-done.refs_1_), channel_id=1, source_target_pairs={{0,2},{2,0},{4,6},{6,4},{8,10},{10,8},{12,14},{14,12},{1,3},{3,1},... | collective-permute-start | bytes 786440 | tf_op jit(solution)/shard_map/ppermute | solution.py:38
  33.6 4.2 %collective-permute-start.8 = (bf16[256,1024]{1,0:T(8,128)(2,1)}, bf16[256,1024]{1,0:T(8,128)(2,1)}, u32[]{:S(2)}, u32[]{:S(2)}) collective-permute-start(bf16[256,1024]{1,0:T(8,128)(2,1)} %get-tuple-element.41), channel_id=1, source_target_pairs={{0,112},{16,0},{32,16},{48,32},{64,48},{80,64},{96,80},{112,96},{1... | collective-permute-start | bytes 1572872 | tf_op jit(solution)/shard_map/ppermute | solution.py:33
  37.8 1.1 shard_map.104
  39.0 11.3 %shard_map.105 = (bf16[256,4096]{1,0:T(8,128)(2,1)}, bf16[4,256,128]{2,1,0:T(8,128)(2,1)S(1)}, bf16[4,256,128]{2,1,0:T(8,128)(2,1)S(1)}, bf16[4,256,128]{2,1,0:T(8,128)(2,1)S(1)}, bf16[4,256,128]{2,1,0:T(8,128)(2,1)S(1)}) custom-call(s32[3]{0:T(128)S(1)} %copy-done.8, s32[16]{0:T(128)S(1)} %copy-done.10, s32[16]{0:T(128)S(1)} %copy-done.11, ...), custom_call_target="tpu_custom_call" | custom-call | flops 1000000 | bytes 100000 | tf_op jit(solution)/shard_map/pallas_call | solution.py:197
  50.3 0.7 copy-done.6
  51.0 0.7 copy-done.7
  51.7 0.3 collective-permute-start.11
  52.0 0.2 collective-permute-start.10
  52.2 7.8 %shard_map.106 = (bf16[256,4096]{1,0:T(8,128)(2,1)}, f32[2,2048,128]{2,1,0:T(8,128)S(1)}) custom-call(s32[3]{0:T(128)S(1)} %copy-done.8, s32[16]{0:T(128)S(1)} %copy-done.10, s32[16]{0:T(128)S(1)} %copy-done.11, bf16[2,2048,128]{2,1,0:T(8,128)(2,1)S(1)} %get-tuple-element.38.key_ref, ...), custom_call_target="tpu_custom_call", output_to_operand_aliasing={{0}: (9, {})} | custom-call | flops 1000000 | bytes 100000 | tf_op jit(solution)/shard_map/pallas_call | solution.py:197
  60.0 1.3 %copy-done = f32[2,2048,128]{2,1,0:T(8,128)} copy-done((f32[2,2048,128]{2,1,0:T(8,128)}, f32[2,2048,128]{2,1,0:T(8,128)S(1)}, u32[]{:S(2)}) %copy-start) | copy-done | bytes 2097176
  61.4 0.7 copy-done.14
  62.2 2.1 %shard_map.107 = (f32[256,256]{1,0:T(8,128)}, bf16[256,256]{1,0:T(8,128)(2,1)}, bf16[256,256]{1,0:T(8,128)(2,1)}, bf16[256,256]{1,0:T(8,128)(2,1)}) custom-call(s32[3]{0:T(128)} %pad_add_fusion.place_ref, bf16[4,256,128]{2,1,0:T(8,128)(2,1)} %copy-done.6, bf16[4,256,128]{2,1,0:T(8,128)(2,1)} %copy-done.7, bf16[4,256,128]{2,1,0:T(8,128)(2,1)} %copy-done.14, ...), custom_call_target="tpu_custom_call" | custom-call | flops 1000000 | bytes 100000 | tf_op jit(solution)/shard_map/pallas_call | solution.py:253
  64.3 4.2 %collective-permute-start.12 = (bf16[256,256]{1,0:T(8,128)(2,1)}, bf16[256,256]{1,0:T(8,128)(2,1)S(1)}, u32[]{:S(2)}, u32[]{:S(2)}) collective-permute-start(bf16[256,256]{1,0:T(8,128)(2,1)} %get-tuple-element.56), channel_id=1, source_target_pairs={{0,4},{2,6},{4,8},{6,10},{8,12},{10,14},{12,0},{14,2},{1,5},{3,7},... | collective-permute-start | bytes 393224 | tf_op jit(solution)/shard_map/ppermute | solution.py:33
  68.4 9.0 %collective-permute-start.13 = (bf16[256,256]{1,0:T(8,128)(2,1)}, bf16[256,256]{1,0:T(8,128)(2,1)S(1)}, u32[]{:S(2)}, u32[]{:S(2)}) collective-permute-start(bf16[256,256]{1,0:T(8,128)(2,1)} %get-tuple-element.57), channel_id=1, source_target_pairs={{0,8},{2,10},{4,12},{6,14},{8,0},{10,2},{12,4},{14,6},{1,9},{3,11}... | collective-permute-start | bytes 393224 | tf_op jit(solution)/shard_map/ppermute | solution.py:33
  77.4 2.0 %collective-permute-start.14 = (bf16[256,256]{1,0:T(8,128)(2,1)}, bf16[256,256]{1,0:T(8,128)(2,1)S(1)}, u32[]{:S(2)}, u32[]{:S(2)}) collective-permute-start(bf16[256,256]{1,0:T(8,128)(2,1)} %get-tuple-element.58), channel_id=1, source_target_pairs={{0,12},{2,14},{4,0},{6,2},{8,4},{10,6},{12,8},{14,10},{1,13},{3,15... | collective-permute-start | bytes 393224 | tf_op jit(solution)/shard_map/ppermute | solution.py:33
  79.5 7.7 %shard_map.108 = (bf16[256,4096]{1,0:T(8,128)(2,1)}, bf16[4,256,128]{2,1,0:T(8,128)(2,1)S(1)}, bf16[4,256,128]{2,1,0:T(8,128)(2,1)S(1)}, bf16[4,256,128]{2,1,0:T(8,128)(2,1)S(1)}, bf16[4,256,128]{2,1,0:T(8,128)(2,1)S(1)}) custom-call(s32[3]{0:T(128)S(1)} %copy-done.9, s32[16]{0:T(128)S(1)} %copy-done.10, ...), custom_call_target="tpu_custom_call", output_to_operand_aliasing={{0}: (10, {})} | custom-call | flops 1000000 | bytes 100000 | tf_op jit(solution)/shard_map/pallas_call | solution.py:197
  87.2 0.7 copy-done.4
  87.9 0.7 copy-done.5
  88.7 5.4 %collective-permute-start.15 = (bf16[4,256,128]{2,1,0:T(8,128)(2,1)S(1)}, bf16[4,256,128]{2,1,0:T(8,128)(2,1)S(1)}, u32[]{:S(2)}, u32[]{:S(2)}) collective-permute-start(bf16[4,256,128]{2,1,0:T(8,128)(2,1)S(1)} %get-tuple-element.62), channel_id=1, source_target_pairs={{0,2},{2,0},{4,6},{6,4},{8,10},{10,8},{12,14},{14,12},{1,3},{3,1},... | collective-permute-start | bytes 786440 | tf_op jit(solution)/shard_map/ppermute | solution.py:38
  94.2 1.1 collective-permute-done.15.refs_2_
  95.2 0.4 collective-permute-done.16.refs_3_
  95.6 0.3 copy-done.15
  95.9 0.4 copy-done.16
  96.3 2.1 %shard_map.109 = (f32[256,256]{1,0:T(8,128)}, bf16[256,256]{1,0:T(8,128)(2,1)}, bf16[256,256]{1,0:T(8,128)(2,1)}, bf16[256,256]{1,0:T(8,128)(2,1)}) custom-call(s32[3]{0:T(128)} %pad_add_fusion.place_ref, bf16[4,256,128]{2,1,0:T(8,128)(2,1)} %copy-done.4, bf16[4,256,128]{2,1,0:T(8,128)(2,1)} %copy-done.5, bf16[4,256,128]{2,1,0:T(8,128)(2,1)} %copy-done.15, ...), custom_call_target="tpu_custom_call" | custom-call | flops 1000000 | bytes 100000 | tf_op jit(solution)/shard_map/pallas_call | solution.py:253
  98.4 4.3 %collective-permute-start.18 = (bf16[256,256]{1,0:T(8,128)(2,1)}, bf16[256,256]{1,0:T(8,128)(2,1)S(1)}, u32[]{:S(2)}, u32[]{:S(2)}) collective-permute-start(bf16[256,256]{1,0:T(8,128)(2,1)} %get-tuple-element.67), channel_id=1, source_target_pairs={{0,8},{2,10},{4,12},{6,14},{8,0},{10,2},{12,4},{14,6},{1,9},{3,11}... | collective-permute-start | bytes 393224 | tf_op jit(solution)/shard_map/ppermute | solution.py:33
  102.7 2.0 %collective-permute-start.19 = (bf16[256,256]{1,0:T(8,128)(2,1)}, bf16[256,256]{1,0:T(8,128)(2,1)S(1)}, u32[]{:S(2)}, u32[]{:S(2)}) collective-permute-start(bf16[256,256]{1,0:T(8,128)(2,1)} %get-tuple-element.68), channel_id=1, source_target_pairs={{0,12},{2,14},{4,0},{6,2},{8,4},{10,6},{12,8},{14,10},{1,13},{3,15... | collective-permute-start | bytes 393224 | tf_op jit(solution)/shard_map/ppermute | solution.py:33
  104.8 4.5 %collective-permute-done.18.refs_6_ = bf16[256,256]{1,0:T(8,128)(2,1)S(1)} collective-permute-done((bf16[256,256]{1,0:T(8,128)(2,1)}, bf16[256,256]{1,0:T(8,128)(2,1)S(1)}, u32[]{:S(2)}, u32[]{:S(2)}) %collective-permute-start.18) | collective-permute-done | bytes 131104 | tf_op jit(solution)/shard_map/ppermute | solution.py:33
  109.3 0.6 copy-done.21
  110.0 2.1 %shard_map.110 = (bf16[128,512]{1,0:T(8,128)(2,1)}, bf16[128,512]{1,0:T(8,128)(2,1)}) custom-call(s32[3]{0:T(128)} %pad_add_fusion.place_ref, f32[256,256]{1,0:T(8,128)} %get-tuple-element.52.refs_0_, bf16[256,256]{1,0:T(8,128)(2,1)} %copy-done.17, bf16[256,256]{1,0:T(8,128)(2,1)} %copy-done.18, bf16[256,256]{1,0:T(8,128)(2,1)} %copy-done.19, ...), custom_call_target="tpu_custom_call" | custom-call | flops 1000000 | bytes 100000 | tf_op jit(solution)/shard_map/pallas_call | solution.py:307
  112.1 3.3 %collective-permute-start.20 = (bf16[128,512]{1,0:T(8,128)(2,1)}, bf16[128,512]{1,0:T(8,128)(2,1)S(1)}, u32[]{:S(2)}, u32[]{:S(2)}) collective-permute-start(bf16[128,512]{1,0:T(8,128)(2,1)} %get-tuple-element.70), channel_id=1, source_target_pairs={{0,1},{1,0},{2,3},{3,2},{4,5},{5,4},{6,7},{7,6},{8,9},{9,8},{10,11... | collective-permute-start | bytes 393224 | tf_op jit(solution)/shard_map/ppermute | solution.py:33
  115.4 3.2 %collective-permute-done.20.sent_ref = bf16[128,512]{1,0:T(8,128)(2,1)S(1)} collective-permute-done((bf16[128,512]{1,0:T(8,128)(2,1)}, bf16[128,512]{1,0:T(8,128)(2,1)S(1)}, u32[]{:S(2)}, u32[]{:S(2)}) %collective-permute-start.20) | collective-permute-done | bytes 131104 | tf_op jit(solution)/shard_map/ppermute | solution.py:33
  118.6 0.7 copy-done.23
  119.2 1.7 %shard_map.111 = (bf16[128,512]{1,0:T(8,128)(2,1)}, bf16[128,512]{1,0:T(8,128)(2,1)}) custom-call(s32[3]{0:T(128)} %pad_add_fusion.place_ref, bf16[128,512]{1,0:T(8,128)(2,1)} %get-tuple-element.69.keep_ref, bf16[128,512]{1,0:T(8,128)(2,1)} %copy-done.23), custom_call_target="tpu_custom_call" | custom-call | flops 1000000 | bytes 100000 | tf_op jit(solution)/shard_map/pallas_call | solution.py:311
  (54 shorter events, 0.4 us)
Async XLA Ops:
  0.6 13.3 %copy-start.12 = (bf16[1,256,4096]{2,1,0:T(8,128)(2,1)S(1)}, bf16[1,256,4096]{2,1,0:T(8,128)(2,1)}, u32[]{:S(2)}) copy-start(bf16[1,256,4096]{2,1,0:T(8,128)(2,1)} %param.13) | copy-start | bytes 6291460
  0.6 37.2 %copy-start.10 = (s32[16]{0:T(128)S(1)}, s32[16]{0:T(128)}, u32[]{:S(2)}) copy-start(s32[16]{0:T(128)} %order_ref.7) | copy-start | bytes 196
  3.1 26.8 %collective-permute-start.7 = (bf16[256,2048]{1,0:T(8,128)(2,1)}, bf16[256,2048]{1,0:T(8,128)(2,1)S(1)}, u32[]{:S(2)}, u32[]{:S(2)}) collective-permute-start(bf16[256,2048]{1,0:T(8,128)(2,1)} %slice_bitcast_fusion), channel_id=1, source_target_pairs={{0,112},{16,0},{32,16},{48,32},{64,48},{80,64},{96,80},{112,96},{1... | collective-permute-start | bytes 3145736 | tf_op jit(solution)/shard_map/ppermute | solution.py:33
  8.4 29.4 %copy-start.8 = (s32[3]{0:T(128)S(1)}, s32[3]{0:T(128)}, u32[]{:S(2)}) copy-start(s32[3]{0:T(128)} %pad_add_fusion.place_ref) | copy-start | bytes 40
  10.1 8.8 %copy-start.3 = (bf16[256,512]{1,0:T(8,128)(2,1)S(1)}, bf16[256,512]{1,0:T(8,128)(2,1)}, u32[]{:S(2)}) copy-start(bf16[256,512]{1,0:T(8,128)(2,1)} %shard_map.103.refs_0_) | copy-start | bytes 786436
  10.1 28.8 %copy-start.11 = (s32[16]{0:T(128)S(1)}, s32[16]{0:T(128)}, u32[]{:S(2)}) copy-start(s32[16]{0:T(128)} %docs_ref.5) | copy-start | bytes 196
  10.1 8.8 %collective-permute-start.2 = (bf16[256,512]{1,0:T(8,128)(2,1)}, bf16[256,512]{1,0:T(8,128)(2,1)S(1)}, u32[]{:S(2)}, u32[]{:S(2)}) collective-permute-start(bf16[256,512]{1,0:T(8,128)(2,1)} %shard_map.103.refs_0_), channel_id=1, source_target_pairs={{0,12},{2,14},{4,0},{6,2},{8,4},{10,6},{12,8},{14,10},{1,13},{3,15... | collective-permute-start | bytes 786440 | tf_op jit(solution)/shard_map/ppermute | solution.py:33
  12.9 12.5 %collective-permute-start.1 = (bf16[256,512]{1,0:T(8,128)(2,1)}, bf16[256,512]{1,0:T(8,128)(2,1)S(1)}, u32[]{:S(2)}, u32[]{:S(2)}) collective-permute-start(bf16[256,512]{1,0:T(8,128)(2,1)} %shard_map.103.refs_0_), channel_id=1, source_target_pairs={{0,8},{2,10},{4,12},{6,14},{8,0},{10,2},{12,4},{14,6},{1,9},{3,11}... | collective-permute-start | bytes 786440 | tf_op jit(solution)/shard_map/ppermute | solution.py:33
  13.2 15.2 %collective-permute-start = (bf16[256,512]{1,0:T(8,128)(2,1)}, bf16[256,512]{1,0:T(8,128)(2,1)S(1)}, u32[]{:S(2)}, u32[]{:S(2)}) collective-permute-start(bf16[256,512]{1,0:T(8,128)(2,1)} %shard_map.103.refs_0_), channel_id=1, source_target_pairs={{0,4},{2,6},{4,8},{6,10},{8,12},{10,14},{12,0},{14,2},{1,5},{3,7},... | collective-permute-start | bytes 786440 | tf_op jit(solution)/shard_map/ppermute | solution.py:33
  14.8 36.9 %collective-permute-start.9 = (bf16[256,1024]{1,0:T(8,128)(2,1)S(1)}, bf16[256,1024]{1,0:T(8,128)(2,1)S(1)}, u32[]{:S(2)}, u32[]{:S(2)}) collective-permute-start(bf16[256,1024]{1,0:T(8,128)(2,1)S(1)} %get-tuple-element.73), channel_id=1, source_target_pairs={{0,112},{16,0},{32,16},{48,32},{64,48},{80,64},{96,80},{112,96},{1... | collective-permute-start | bytes 1572872 | tf_op jit(solution)/shard_map/ppermute | solution.py:33
  18.9 14.7 %collective-permute-start.3 = (bf16[256,512]{1,0:T(8,128)(2,1)S(1)}, bf16[256,512]{1,0:T(8,128)(2,1)S(1)}, u32[]{:S(2)}, u32[]{:S(2)}) collective-permute-start(bf16[256,512]{1,0:T(8,128)(2,1)S(1)} %copy-done.3), channel_id=1, source_target_pairs={{0,2},{2,0},{4,6},{6,4},{8,10},{10,8},{12,14},{14,12},{1,3},{3,1},... | collective-permute-start | bytes 786440 | tf_op jit(solution)/shard_map/ppermute | solution.py:38
  25.3 12.5 %collective-permute-start.6 = (bf16[256,512]{1,0:T(8,128)(2,1)S(1)}, bf16[256,512]{1,0:T(8,128)(2,1)S(1)}, u32[]{:S(2)}, u32[]{:S(2)}) collective-permute-start(bf16[256,512]{1,0:T(8,128)(2,1)S(1)} %collective-permute-done.2.refs_3_), channel_id=1, source_target_pairs={{0,2},{2,0},{4,6},{6,4},{8,10},{10,8},{12,14},{14,12},{1,3},{3,1},... | collective-permute-start | bytes 786440 | tf_op jit(solution)/shard_map/ppermute | solution.py:38
  28.4 9.4 %collective-permute-start.5 = (bf16[256,512]{1,0:T(8,128)(2,1)S(1)}, bf16[256,512]{1,0:T(8,128)(2,1)S(1)}, u32[]{:S(2)}, u32[]{:S(2)}) collective-permute-start(bf16[256,512]{1,0:T(8,128)(2,1)S(1)} %collective-permute-done.1.refs_2_), channel_id=1, source_target_pairs={{0,2},{2,0},{4,6},{6,4},{8,10},{10,8},{12,14},{14,12},{1,3},{3,1},... | collective-permute-start | bytes 786440 | tf_op jit(solution)/shard_map/ppermute | solution.py:38
  29.9 1.0 copy-start.1
  30.9 6.9 %collective-permute-start.4 = (bf16[256,512]{1,0:T(8,128)(2,1)S(1)}, bf16[256,512]{1,0:T(8,128)(2,1)S(1)}, u32[]{:S(2)}, u32[]{:S(2)}) collective-permute-start(bf16[256,512]{1,0:T(8,128)(2,1)S(1)} %collective-permute-done.refs_1_), channel_id=1, source_target_pairs={{0,2},{2,0},{4,6},{6,4},{8,10},{10,8},{12,14},{14,12},{1,3},{3,1},... | collective-permute-start | bytes 786440 | tf_op jit(solution)/shard_map/ppermute | solution.py:38
  33.6 5.4 %copy-start.2 = (bf16[256,2048]{1,0:T(8,128)(2,1)S(1)}, bf16[256,2048]{1,0:T(8,128)(2,1)}, u32[]{:S(2)}) copy-start(bf16[256,2048]{1,0:T(8,128)(2,1)} %copy-done.1) | copy-start | bytes 3145732
  33.6 45.9 %collective-permute-start.8 = (bf16[256,1024]{1,0:T(8,128)(2,1)}, bf16[256,1024]{1,0:T(8,128)(2,1)}, u32[]{:S(2)}, u32[]{:S(2)}) collective-permute-start(bf16[256,1024]{1,0:T(8,128)(2,1)} %get-tuple-element.41), channel_id=1, source_target_pairs={{0,112},{16,0},{32,16},{48,32},{64,48},{80,64},{96,80},{112,96},{1... | collective-permute-start | bytes 1572872 | tf_op jit(solution)/shard_map/ppermute | solution.py:33
  50.3 0.7 copy-start.6
  51.0 0.7 copy-start.7
  51.7 9.7 %collective-permute-start.11 = (bf16[4,256,128]{2,1,0:T(8,128)(2,1)S(1)}, bf16[4,256,128]{2,1,0:T(8,128)(2,1)S(1)}, u32[]{:S(2)}, u32[]{:S(2)}) collective-permute-start(bf16[4,256,128]{2,1,0:T(8,128)(2,1)S(1)} %get-tuple-element.50), channel_id=1, source_target_pairs={{0,2},{2,0},{4,6},{6,4},{8,10},{10,8},{12,14},{14,12},{1,3},{3,1},... | collective-permute-start | bytes 786440 | tf_op jit(solution)/shard_map/ppermute | solution.py:38
  52.0 9.3 %collective-permute-start.10 = (bf16[4,256,128]{2,1,0:T(8,128)(2,1)S(1)}, bf16[4,256,128]{2,1,0:T(8,128)(2,1)S(1)}, u32[]{:S(2)}, u32[]{:S(2)}) collective-permute-start(bf16[4,256,128]{2,1,0:T(8,128)(2,1)S(1)} %get-tuple-element.45), channel_id=1, source_target_pairs={{0,2},{2,0},{4,6},{6,4},{8,10},{10,8},{12,14},{14,12},{1,3},{3,1},... | collective-permute-start | bytes 786440 | tf_op jit(solution)/shard_map/ppermute | solution.py:38
  52.2 27.3 %copy-start.9 = (s32[3]{0:T(128)S(1)}, s32[3]{0:T(128)}, u32[]{:S(2)}) copy-start(s32[3]{0:T(128)} %pad_add_fusion.place_ref) | copy-start | bytes 40
  60.0 1.3 %copy-start = (f32[2,2048,128]{2,1,0:T(8,128)}, f32[2,2048,128]{2,1,0:T(8,128)S(1)}, u32[]{:S(2)}) copy-start(f32[2,2048,128]{2,1,0:T(8,128)S(1)} %get-tuple-element.47.refs_0_) | copy-start | bytes 6291460
  61.4 0.8 copy-start.13
  61.4 0.7 copy-start.14
  64.3 24.4 %collective-permute-start.12 = (bf16[256,256]{1,0:T(8,128)(2,1)}, bf16[256,256]{1,0:T(8,128)(2,1)S(1)}, u32[]{:S(2)}, u32[]{:S(2)}) collective-permute-start(bf16[256,256]{1,0:T(8,128)(2,1)} %get-tuple-element.56), channel_id=1, source_target_pairs={{0,4},{2,6},{4,8},{6,10},{8,12},{10,14},{12,0},{14,2},{1,5},{3,7},... | collective-permute-start | bytes 393224 | tf_op jit(solution)/shard_map/ppermute | solution.py:33
  68.4 20.2 %collective-permute-start.13 = (bf16[256,256]{1,0:T(8,128)(2,1)}, bf16[256,256]{1,0:T(8,128)(2,1)S(1)}, u32[]{:S(2)}, u32[]{:S(2)}) collective-permute-start(bf16[256,256]{1,0:T(8,128)(2,1)} %get-tuple-element.57), channel_id=1, source_target_pairs={{0,8},{2,10},{4,12},{6,14},{8,0},{10,2},{12,4},{14,6},{1,9},{3,11}... | collective-permute-start | bytes 393224 | tf_op jit(solution)/shard_map/ppermute | solution.py:33
  77.4 11.2 %collective-permute-start.14 = (bf16[256,256]{1,0:T(8,128)(2,1)}, bf16[256,256]{1,0:T(8,128)(2,1)S(1)}, u32[]{:S(2)}, u32[]{:S(2)}) collective-permute-start(bf16[256,256]{1,0:T(8,128)(2,1)} %get-tuple-element.58), channel_id=1, source_target_pairs={{0,12},{2,14},{4,0},{6,2},{8,4},{10,6},{12,8},{14,10},{1,13},{3,15... | collective-permute-start | bytes 393224 | tf_op jit(solution)/shard_map/ppermute | solution.py:33
  87.2 0.7 copy-start.4
  87.9 0.7 copy-start.5
  88.6 20.7 %copy-start.17 = (bf16[256,256]{1,0:T(8,128)(2,1)}, bf16[256,256]{1,0:T(8,128)(2,1)S(1)}, u32[]{:S(2)}) copy-start(bf16[256,256]{1,0:T(8,128)(2,1)S(1)} %collective-permute-done.12.refs_1_) | copy-start | bytes 393220
  88.6 20.7 %copy-start.18 = (bf16[256,256]{1,0:T(8,128)(2,1)}, bf16[256,256]{1,0:T(8,128)(2,1)S(1)}, u32[]{:S(2)}) copy-start(bf16[256,256]{1,0:T(8,128)(2,1)S(1)} %collective-permute-done.13.refs_2_) | copy-start | bytes 393220
  88.6 20.6 %copy-start.19 = (bf16[256,256]{1,0:T(8,128)(2,1)}, bf16[256,256]{1,0:T(8,128)(2,1)S(1)}, u32[]{:S(2)}) copy-start(bf16[256,256]{1,0:T(8,128)(2,1)S(1)} %collective-permute-done.14.refs_3_) | copy-start | bytes 393220
  88.7 6.6 %collective-permute-start.15 = (bf16[4,256,128]{2,1,0:T(8,128)(2,1)S(1)}, bf16[4,256,128]{2,1,0:T(8,128)(2,1)S(1)}, u32[]{:S(2)}, u32[]{:S(2)}) collective-permute-start(bf16[4,256,128]{2,1,0:T(8,128)(2,1)S(1)} %get-tuple-element.62), channel_id=1, source_target_pairs={{0,2},{2,0},{4,6},{6,4},{8,10},{10,8},{12,14},{14,12},{1,3},{3,1},... | collective-permute-start | bytes 786440 | tf_op jit(solution)/shard_map/ppermute | solution.py:38
  94.1 1.5 %collective-permute-start.16 = (bf16[4,256,128]{2,1,0:T(8,128)(2,1)S(1)}, bf16[4,256,128]{2,1,0:T(8,128)(2,1)S(1)}, u32[]{:S(2)}, u32[]{:S(2)}) collective-permute-start(bf16[4,256,128]{2,1,0:T(8,128)(2,1)S(1)} %get-tuple-element.64), channel_id=1, source_target_pairs={{0,2},{2,0},{4,6},{6,4},{8,10},{10,8},{12,14},{14,12},{1,3},{3,1},... | collective-permute-start | bytes 786440 | tf_op jit(solution)/shard_map/ppermute | solution.py:38
  95.2 0.7 copy-start.15
  95.6 0.7 copy-start.16
  98.4 6.4 %collective-permute-start.17 = (bf16[256,256]{1,0:T(8,128)(2,1)}, bf16[256,256]{1,0:T(8,128)(2,1)S(1)}, u32[]{:S(2)}, u32[]{:S(2)}) collective-permute-start(bf16[256,256]{1,0:T(8,128)(2,1)} %get-tuple-element.66), channel_id=1, source_target_pairs={{0,4},{2,6},{4,8},{6,10},{8,12},{10,14},{12,0},{14,2},{1,5},{3,7},... | collective-permute-start | bytes 393224 | tf_op jit(solution)/shard_map/ppermute | solution.py:33
  98.4 10.9 %collective-permute-start.18 = (bf16[256,256]{1,0:T(8,128)(2,1)}, bf16[256,256]{1,0:T(8,128)(2,1)S(1)}, u32[]{:S(2)}, u32[]{:S(2)}) collective-permute-start(bf16[256,256]{1,0:T(8,128)(2,1)} %get-tuple-element.67), channel_id=1, source_target_pairs={{0,8},{2,10},{4,12},{6,14},{8,0},{10,2},{12,4},{14,6},{1,9},{3,11}... | collective-permute-start | bytes 393224 | tf_op jit(solution)/shard_map/ppermute | solution.py:33
  102.7 6.5 %collective-permute-start.19 = (bf16[256,256]{1,0:T(8,128)(2,1)}, bf16[256,256]{1,0:T(8,128)(2,1)S(1)}, u32[]{:S(2)}, u32[]{:S(2)}) collective-permute-start(bf16[256,256]{1,0:T(8,128)(2,1)} %get-tuple-element.68), channel_id=1, source_target_pairs={{0,12},{2,14},{4,0},{6,2},{8,4},{10,6},{12,8},{14,10},{1,13},{3,15... | collective-permute-start | bytes 393224 | tf_op jit(solution)/shard_map/ppermute | solution.py:33
  104.8 4.5 %copy-start.20 = (bf16[256,256]{1,0:T(8,128)(2,1)}, bf16[256,256]{1,0:T(8,128)(2,1)S(1)}, u32[]{:S(2)}) copy-start(bf16[256,256]{1,0:T(8,128)(2,1)S(1)} %collective-permute-done.17.refs_5_) | copy-start | bytes 393220
  109.3 0.7 copy-start.21
  109.3 0.7 copy-start.22
  112.1 6.5 %collective-permute-start.20 = (bf16[128,512]{1,0:T(8,128)(2,1)}, bf16[128,512]{1,0:T(8,128)(2,1)S(1)}, u32[]{:S(2)}, u32[]{:S(2)}) collective-permute-start(bf16[128,512]{1,0:T(8,128)(2,1)} %get-tuple-element.70), channel_id=1, source_target_pairs={{0,1},{1,0},{2,3},{3,2},{4,5},{5,4},{6,7},{7,6},{8,9},{9,8},{10,11... | collective-permute-start | bytes 393224 | tf_op jit(solution)/shard_map/ppermute | solution.py:33
  118.6 0.7 copy-start.23

commit v2 on v1

v2 whole, which is shorter than its diff:
```python
import functools
import math

import jax
import jax.numpy as jnp
from jax import lax
from jax.experimental import pallas as pl
from jax.experimental.pallas import tpu as pltpu
from jax.sharding import PartitionSpec as P

HQ = 64
KVH = 4
HD = 128
BLK = 128
BLOCKS = 16
TOKENS = BLOCKS * BLK
ROWS = 2 * BLK
LONGEST = 9
INVERSE = HD**-0.5
INVERSE2 = INVERSE * math.log2(math.e)
NT = (((1,), (1,)), ((), ()))
F32 = jnp.float32
BF16 = jnp.bfloat16

GROUP = HQ // KVH * HD
STEP = 512
STEPS = GROUP // STEP
SMEM = pl.BlockSpec(memory_space=pltpu.SMEM)
VMEM = pl.BlockSpec(memory_space=pltpu.VMEM)
ANY = pl.BlockSpec(memory_space=pl.ANY)
TINY = pl.CostEstimate(flops=1_000_000, bytes_accessed=100_000, transcendentals=0)


def shape(*dims, dtype=BF16):
    return jax.ShapeDtypeStruct(dims, dtype)


def chip_turned(array, by):
    size = lax.axis_size("ctx")
    return lax.ppermute(array, "ctx", [(i, (i + 2 * by) % size) for i in range(size)])


def core_swap(array):
    size = lax.axis_size("ctx")
    return lax.ppermute(array, "ctx", [(i, i ^ 1) for i in range(size)])


def from_next_section(array, flip):
    sections, size = lax.axis_size("pipe"), lax.axis_size("ctx")
    moves = [
        (s * size + i, (s - 1) % sections * size + (i ^ flip)) for s in range(sections) for i in range(size)
    ]
    return lax.ppermute(array, ("pipe", "ctx"), moves)


def tied(array, *others):
    return lax.optimization_barrier((array,) + others)[0]


def dequantize_kernel(place_ref, key_ref, value_ref, scale_ref, keep_ref, send_ref):
    core = place_ref[1]
    for g in range(2):
        for block in range(2):
            rows = slice(block * BLK, (block + 1) * BLK)
            for part, codes in enumerate((key_ref, value_ref)):
                scale = scale_ref[block, part * KVH + place_ref[2] * 2 + g]
                tile = (codes[rows, g * HD : (g + 1) * HD].astype(F32) * scale).astype(BF16)

                @pl.when(core == g)
                def _():
                    keep_ref[rows, part * HD : (part + 1) * HD] = tile

                @pl.when(core != g)
                def _():
                    send_ref[rows, part * HD : (part + 1) * HD] = tile


def order_kernel(place_ref, order_ref, *refs):
    pieces = refs[:4]
    keys_ref, turned_ref, values_ref = refs[4:]
    y = place_ref[0]
    for d in range(4):
        from_y = lax.rem(y + 4 - d, 4)
        for half in range(2):
            holder = jnp.where(half == 0, place_ref[1], 1 - place_ref[1])
            for block in range(2):
                seq = order_ref[from_y * 4 + holder * 2 + block]
                at = pl.multiple_of(seq * BLK, BLK)
                tile = pieces[d][half, block * BLK : (block + 1) * BLK, :]
                keys_ref[pl.ds(at, BLK), :] = tile[:, :HD]
                turned_ref[:, pl.ds(at, BLK)] = jnp.transpose(tile[:, :HD])
                values_ref[pl.ds(at, BLK), :] = tile[:, HD:]


def stacked(tile):
    heads = tile.shape[1] // HD
    return jnp.concatenate([tile[:, i * HD : (i + 1) * HD] for i in range(heads)], axis=0)


def load_rows(query_from, grad_from, saved_from, q_ref, g_ref, dots_ref):
    lane = lax.broadcasted_iota(jnp.int32, (BLK, HD), 1)
    dots = jnp.zeros((BLK, HD), F32)
    for h in range(STEP // HD):
        columns = slice(h * HD, (h + 1) * HD)
        rows = slice(h * BLK, (h + 1) * BLK)
        grad = grad_from[:, columns]
        q_ref[rows, :] = query_from[:, columns]
        g_ref[rows, :] = grad
        product = grad.astype(F32) * saved_from[:, columns].astype(F32)
        dots = jnp.where(lane == h, jnp.sum(product, axis=1, keepdims=True), dots)
    dots_ref[...] = jnp.transpose(dots)


def block_pairs(size, start, key_ref, turned_ref, value_ref, q_ref, g_ref, dots_ref, dq_ref, dk_ref, dv_ref):
    rows = size * BLK
    first = pl.multiple_of(start * BLK, BLK)
    keys = key_ref[pl.ds(first, rows), :]
    values = value_ref[pl.ds(first, rows), :]
    keys_turned = turned_ref[:, pl.ds(first, rows)]
    wide = 2 * HD
    key_index = lax.broadcasted_iota(jnp.int32, (BLK, wide), 0)
    query_index = lax.broadcasted_iota(jnp.int32, (BLK, wide), 1) % BLK
    dk = None
    dv = None
    for part in range(STEP // wide):
        query = q_ref[part * wide : (part + 1) * wide, :]
        grad = g_ref[part * wide : (part + 1) * wide, :]
        scores = lax.dot_general(keys, query, NT, preferred_element_type=F32)
        dprobs = lax.dot_general(values, grad, NT, preferred_element_type=F32)
        row_dots = jnp.concatenate([dots_ref[part * 2 + i : part * 2 + i + 1, :] for i in range(2)], axis=1)
        last = jnp.where(key_index <= query_index, scores[rows - BLK :], -jnp.inf)
        scores = last if size == 1 else jnp.concatenate([scores[: rows - BLK], last], axis=0)
        top = jnp.max(scores, axis=0, keepdims=True)
        weights = jnp.exp2((scores - top) * INVERSE2)
        total = jnp.sum(weights, axis=0, keepdims=True)
        probs = weights * (1.0 / total)
        dscores = (probs * (dprobs - row_dots)).astype(BF16)
        dv_part = jnp.dot(probs.astype(BF16), grad, preferred_element_type=F32)
        dk_part = jnp.dot(dscores, query, preferred_element_type=F32)
        dv = dv_part if dv is None else dv + dv_part
        dk = dk_part if dk is None else dk + dk_part
        dq = jnp.dot(keys_turned, dscores, preferred_element_type=F32) * INVERSE
        for i in range(2):
            at = part * wide + i * HD
            dq_ref[:, at : at + HD] = jnp.transpose(dq[:, i * HD : (i + 1) * HD]).astype(BF16)
    dv_ref[pl.ds(first, rows), :] += dv
    dk_ref[pl.ds(first, rows), :] += dk


def rows_kernel(rows_of, place_ref, order_ref, docs_ref, key_ref, turned_ref, value_ref, query_ref, grad_ref, saved_ref, *refs):
    refs = list(refs)
    before_ref = refs.pop(0) if rows_of else None
    dq_ref, out_ref, q_scr, g_scr, dots_scr, *rest = refs
    sums_ref = rest.pop(0) if rows_of else out_ref
    step = pl.program_id(0)
    block = pl.program_id(1)

    @pl.when((step == 0) & (block == 0))
    def _():
        if rows_of:
            pltpu.make_async_copy(before_ref, rest[0], rest[1]).start()
        sums_ref[...] = jnp.zeros_like(sums_ref)

    load_rows(query_ref, grad_ref, saved_ref, q_scr, g_scr, dots_scr)
    core = 1 - place_ref[1] if rows_of else place_ref[1]
    seq = order_ref[place_ref[0] * 4 + core * 2 + block]
    doc = docs_ref[seq]
    start = jnp.int32(0)
    for b in range(BLOCKS):
        start = start + jnp.where(docs_ref[b] < doc, 1, 0)
    size = seq + 1 - start
    for i in range(1, LONGEST + 1):

        @pl.when(size == i)
        def _():
            block_pairs(
                i, start, key_ref, turned_ref, value_ref, q_scr, g_scr, dots_scr, dq_ref, sums_ref.at[0], sums_ref.at[1]
            )

    if rows_of:

        @pl.when((step == STEPS - 1) & (block == 1))
        def _():
            pltpu.make_async_copy(before_ref, rest[0], rest[1]).wait()
            for r in range(BLOCKS):
                at = pl.ds(pl.multiple_of(order_ref[r] * BLK, BLK), BLK)
                out_ref[r, :, :HD] = ((sums_ref[0, at, :] + rest[0][0, at, :]) * INVERSE).astype(BF16)
                out_ref[r, :, HD:] = (sums_ref[1, at, :] + rest[0][1, at, :]).astype(BF16)


def rows_call(rows_of, place, order, docs, kv, queries, saved, grads, sums):
    whole = lambda s: pl.BlockSpec(s, lambda i, j, *_: (0,) * len(s))
    group_at = pl.BlockSpec((BLK, STEP), lambda i, j, p, *_: (j, p[1] * STEPS + i))
    alone_at = pl.BlockSpec((BLK, STEP), lambda i, j, *_: (j, i))
    sums_shape = (2, TOKENS, HD)
    in_specs = [whole((TOKENS, HD)), whole((HD, TOKENS)), whole((TOKENS, HD)), group_at, alone_at, group_at]
    operands = [*kv, queries, grads, saved]
    scratch = [pltpu.VMEM((STEP, HD), BF16), pltpu.VMEM((STEP, HD), BF16), pltpu.VMEM((HD, BLK), F32)]
    if rows_of:
        in_specs.append(ANY)
        operands.append(sums)
        outs = [shape(ROWS, GROUP), shape(BLOCKS, BLK, 2 * HD)]
        scratch += [pltpu.VMEM(sums_shape, F32), pltpu.VMEM(sums_shape, F32), pltpu.SemaphoreType.DMA]
    else:
        outs = [shape(*queries.shape), shape(*sums_shape, dtype=F32)]
    return pl.pallas_call(
        functools.partial(rows_kernel, rows_of),
        grid_spec=pltpu.PrefetchScalarGridSpec(
            num_scalar_prefetch=3,
            grid=(STEPS, 2),
            in_specs=in_specs,
            out_specs=[alone_at if rows_of else group_at, whole(outs[1].shape)],
            scratch_shapes=scratch,
        ),
        out_shape=outs,
        compiler_params=pltpu.CompilerParams(vmem_limit_bytes=62 << 20),
        cost_estimate=TINY,
    )(place, order, docs, *operands)


def total_kernel(parts_ref, keys_ref, values_ref):
    for core in range(2):
        for tp in range(2):
            at = (tp * 2 + core) * HD
            total = parts_ref[core * 2 + tp].astype(F32)
            for y in range(1, 4):
                total = total + parts_ref[y * 4 + core * 2 + tp].astype(F32)
            keys_ref[:, at : at + HD] = total[:, :HD].astype(BF16)
            values_ref[:, at : at + HD] = total[:, HD:].astype(BF16)


def place_kernel(place_ref, piece_ref, _, out_ref):
    out_ref[...] = piece_ref[...]


def on_device(queries, key_codes, value_codes, kv_scales, saved_out, section_grads, block_order, block_docs):
    ctx = lax.axis_index("ctx")
    core = ctx % 2
    place = jnp.stack([ctx // 2, core, lax.axis_index("tp")]).astype(jnp.int32)
    queries, saved_out, section_grads = queries[0], saved_out[0], section_grads[0]

    grads = []
    for flip in range(2):
        group = core if flip == 0 else 1 - core
        piece = lax.dynamic_slice_in_dim(section_grads, group * GROUP, GROUP, 1)
        grads.append(from_next_section(piece, flip))

    keep, send = pl.pallas_call(
        dequantize_kernel,
        in_specs=[SMEM, VMEM, VMEM, SMEM],
        out_specs=[VMEM] * 2,
        out_shape=[shape(ROWS, 2 * HD)] * 2,
        cost_estimate=TINY,
    )(place, key_codes[0], value_codes[0], kv_scales[0])
    sent = [core_swap(array) for array in (queries, saved_out)]
    chip = tied(jnp.stack([keep, core_swap(send)]), *sent)
    chips = [chip] + [chip_turned(chip, d) for d in range(1, 4)]
    kv = pl.pallas_call(
        order_kernel,
        in_specs=[SMEM, SMEM] + [VMEM] * 4,
        out_specs=[VMEM] * 3,
        out_shape=[shape(TOKENS, HD), shape(HD, TOKENS), shape(TOKENS, HD)],
        compiler_params=pltpu.CompilerParams(vmem_limit_bytes=62 << 20),
        cost_estimate=TINY,
    )(place, block_order, *chips)

    shared = (place, block_order, block_docs, kv)
    dq, sums = rows_call(0, *shared, queries, saved_out, grads[0], None)
    dq_other, sums = rows_call(1, *shared, *sent, grads[1], sums)
    returned = core_swap(dq_other)
    parts = lax.all_to_all(sums, ("ctx", "tp"), 0, 0, tiled=True)
    dq = pl.pallas_call(
        place_kernel,
        grid_spec=pltpu.PrefetchScalarGridSpec(
            num_scalar_prefetch=1,
            grid=(4,),
            in_specs=[pl.BlockSpec((BLK // 2, GROUP), lambda i, p: (i, 0)), ANY],
            out_specs=pl.BlockSpec((BLK // 2, GROUP), lambda i, p: (i, 1 - p[1])),
        ),
        out_shape=shape(*queries.shape),
        input_output_aliases={2: 0},
        cost_estimate=TINY,
    )(place, returned, dq)
    grad_keys, grad_values = pl.pallas_call(
        total_kernel,
        in_specs=[VMEM],
        out_specs=[VMEM] * 2,
        out_shape=[shape(BLK, KVH * HD)] * 2,
        compiler_params=pltpu.CompilerParams(vmem_limit_bytes=62 << 20),
        cost_estimate=TINY,
    )(tied(parts, dq))
    return dq[None], grad_keys[None], grad_values[None]


def solution(mesh):
    in_specs = (
        P("pipe", "ctx", "tp"),
        P("pipe", "ctx", "tp"),
        P("pipe", "ctx", "tp"),
        P("pipe", "ctx", None),
        P("pipe", "ctx", "tp"),
        P("pipe", "ctx", "tp"),
        P(),
        P(),
    )
    out_specs = (
        P("pipe", "ctx", "tp"),
        P("pipe", ("ctx", "tp"), None),
        P("pipe", ("ctx", "tp"), None),
    )
    return jax.shard_map(on_device, mesh=mesh, in_specs=in_specs, out_specs=out_specs, check_vma=False)
```

time: 122 us -> 105 us (0.86); the launches traced: 121 us -> 106 us
  starting transfers between devices: 53.8 us -> 22.5 us
  waiting for transfers between devices: 16.8 us -> 30.6 us
  Pallas kernels: 37.7 us -> 45.8 us
  local copies, waits for them, and re-layouts: 11.2 us -> 4.74 us
    ppermute x13 -> x5, starting transfers between devices: 38.1 us -> 8.89 us  [the longest x2 5.04 us: from_next_section(): return lax.ppermute(array, ('pipe', 'ctx'), moves)]
    all_to_all x0 -> x1, waiting for transfers between devices: none -> 14.6 us  [on_device(): parts = lax.all_to_all(sums, ('ctx', 'tp'), 0, 0, tiled=True)]
    ppermute x8 -> x4, starting transfers between devices: 15.7 us -> 6.16 us  [core_swap(): return lax.ppermute(array, 'ctx', [(i, i ^ 1) for i in range(size)])]
    pallas_call x8 -> x5, Pallas kernels: 36 us -> 43.9 us  [the longest x2 35.3 us: rows_call(): pl.pallas_call(functools.partial(rows_kernel, rows_of), grid_spec=pltpu.P...]
    all_to_all x0 -> x1, starting transfers between devices: none -> 7.5 us  [on_device(): parts = lax.all_to_all(sums, ('ctx', 'tp'), 0, 0, tiled=True)]
    unnamed x48 -> x10, local copies, waits for them, and re-layouts: 7.93 us -> 1.98 us
    squeeze x2 -> x0, local copies, waits for them, and re-layouts: 3.31 us -> none  [on_device(): section_grads[0, :, first:first + width]]
    dynamic_slice x0 -> x1, local copies, waits for them, and re-layouts: none -> 2.76 us  [on_device(): piece = lax.dynamic_slice_in_dim(section_grads, group * GROUP, GROUP, 1)]
  transfers between devices with their start and end apart: 21 -> 10, of which waited for: 7 -> 4; matrix products, arithmetic and copies ran while one was open for 1% -> 4% of each run, Pallas kernels for 26% -> 27%
where the time goes in v2:
time: 105 us; the launch traced here: 106 us
  Pallas kernels  45.8 us (44%)
  waiting for transfers between devices  30.6 us (29%)
  starting transfers between devices  22.5 us (21%)
  local copies, waits for them, and re-layouts  4.74 us (5%)
  other arithmetic  1.54 us (1%)
    pallas_call x2, Pallas kernels, rows_call(): pl.pallas_call(functools.partial(rows_kernel, rows_of), grid_spec=pltpu.P...  35.3 us
    all_to_all x1, waiting for transfers between devices, on_device(): parts = lax.all_to_all(sums, ('ctx', 'tp'), 0, 0, tiled=True)  14.6 us
    ppermute x3, waiting for transfers between devices, chip_turned(): lax.ppermute(array, 'ctx', [(i, (i + 2 * by) % size) for i in range(size)])  14.4 us
    all_to_all x1, starting transfers between devices, on_device(): parts = lax.all_to_all(sums, ('ctx', 'tp'), 0, 0, tiled=True)  7.5 us
    ppermute x4, starting transfers between devices, core_swap(): return lax.ppermute(array, 'ctx', [(i, i ^ 1) for i in range(size)])  6.16 us
    ppermute x2, starting transfers between devices, from_next_section(): return lax.ppermute(array, ('pipe', 'ctx'), moves)  5.04 us
    pallas_call x1, Pallas kernels, on_device(): pl.pallas_call(place_kernel, grid_spec=pltpu.PrefetchScalarGridSpec(num_s...  4.03 us
    ppermute x3, starting transfers between devices, chip_turned(): lax.ppermute(array, 'ctx', [(i, (i + 2 * by) % size) for i in range(size)])  3.84 us
  transfers between devices with their start and end apart: 10, of which 4 were waited for; matrix products, arithmetic and copies ran while one was open for 4% of the time, Pallas kernels for 27%

profile of v2, /device:TPU:1, one launch (start us, length us, event | category | flops | bytes accessed | tf_op | source)
XLA Modules:
  0.0 105.9 jit_solution(4686492593469685524)
XLA Ops:
  0.6 1.5 %collective-permute-start.1 = (bf16[256,4096]{1,0:T(8,128)(2,1)}, bf16[256,4096]{1,0:T(8,128)(2,1)}, u32[]{:S(2)}, u32[]{:S(2)}) collective-permute-start(bf16[256,4096]{1,0:T(8,128)(2,1)} %bitcast.17), channel_id=1, source_target_pairs={{0,2},{2,0},{4,6},{6,4},{8,10},{10,8},{12,14},{14,12},{1,3},{3,1},... | collective-permute-start | bytes 6291464 | tf_op jit(solution)/shard_map/ppermute | solution.py:45
  2.1 0.1 collective-permute-start.2
  2.2 2.8 %dynamic-slice_bitcast_fusion = (bf16[256,2048]{1,0:T(8,128)(2,1)}, bf16[256,2048]{1,0:T(8,128)(2,1)S(1)}) fusion(bf16[1,256,4096]{2,1,0:T(8,128)(2,1)} %param.13, s32[]{:T(128)S(6)} %select_n.20, s32[]{:T(128)S(6)} %select_n.19), kind=kLoop, calls=%fused_computation | loop fusion | bytes 4194312 | tf_op jit(solution)/shard_map/dynamic_slice | solution.py:245
  5.0 3.9 %collective-permute-start.7 = (bf16[256,2048]{1,0:T(8,128)(2,1)}, bf16[256,2048]{1,0:T(8,128)(2,1)}, u32[]{:S(2)}, u32[]{:S(2)}) collective-permute-start(bf16[256,2048]{1,0:T(8,128)(2,1)} %get-tuple-element.29), channel_id=1, source_target_pairs={{0,112},{2,114},{4,116},{6,118},{8,120},{10,122},{12,124},{14,126}... | collective-permute-start | bytes 3145736 | tf_op jit(solution)/shard_map/ppermute | solution.py:53
  8.9 1.1 %collective-permute-start.6 = (bf16[256,2048]{1,0:T(8,128)(2,1)S(1)}, bf16[256,2048]{1,0:T(8,128)(2,1)}, u32[]{:S(2)}, u32[]{:S(2)}) collective-permute-start(bf16[256,2048]{1,0:T(8,128)(2,1)S(1)} %get-tuple-element.30), channel_id=1, source_target_pairs={{0,114},{2,112},{4,118},{6,116},{8,122},{10,120},{12,126},{14,124}... | collective-permute-start | bytes 3145736 | tf_op jit(solution)/shard_map/ppermute | solution.py:53
  10.0 0.6 pad_add_fusion.place_ref
  10.6 1.8 %shard_map.103 = (bf16[256,256]{1,0:T(8,128)(2,1)}, bf16[256,256]{1,0:T(8,128)(2,1)}) custom-call(s32[3]{0:T(128)} %pad_add_fusion.place_ref, bf16[256,256]{1,0:T(8,128)(2,1)} %bitcast.22, bf16[256,256]{1,0:T(8,128)(2,1)} %bitcast.23, f32[2,8]{1,0:T(2,128)} %bitcast.26), custom_call_target="tpu_custom_call" | custom-call | flops 1000000 | bytes 100000 | tf_op jit(solution)/shard_map/pallas_call | solution.py:248
  12.5 0.0 collective-permute-start
  12.5 1.6 %collective-permute-done = bf16[256,256]{1,0:T(8,128)(2,1)S(1)} collective-permute-done((bf16[256,256]{1,0:T(8,128)(2,1)}, bf16[256,256]{1,0:T(8,128)(2,1)S(1)}, u32[]{:S(2)}, u32[]{:S(2)}) %collective-permute-start) | collective-permute-done | bytes 131104 | tf_op jit(solution)/shard_map/ppermute | solution.py:45
  14.0 0.9 pad_maximum_fusion.refs_0_
  14.9 0.0 copy-start.1
  15.0 0.0 collective-permute-done.1.query_ref
  15.0 0.0 collective-permute-done.2.saved_ref
  15.0 2.8 %collective-permute-start.5 = (bf16[2,256,256]{2,1,0:T(8,128)(2,1)S(1)}, bf16[2,256,256]{2,1,0:T(8,128)(2,1)S(1)}, u32[]{:S(2)}, u32[]{:S(2)}) collective-permute-start(bf16[2,256,256]{2,1,0:T(8,128)(2,1)S(1)} %pad_maximum_fusion.refs_0_), channel_id=1, source_target_pairs={{0,12},{2,14},{4,0},{6,2},{8,4},{10,6},{12,8},{14,10},{1,13},{3,15... | collective-permute-start | bytes 786440 | tf_op jit(solution)/shard_map/ppermute | solution.py:40
  17.8 0.3 collective-permute-start.4
  18.1 0.7 collective-permute-start.3
  18.8 10.0 %collective-permute-done.5.refs_3_ = bf16[2,256,256]{2,1,0:T(8,128)(2,1)S(1)} collective-permute-done((bf16[2,256,256]{2,1,0:T(8,128)(2,1)S(1)}, bf16[2,256,256]{2,1,0:T(8,128)(2,1)S(1)}, u32[]{:S(2)}, u32[]{:S(2)}) %collective-permute-start.5) | collective-permute-done | bytes 262176 | tf_op jit(solution)/shard_map/ppermute | solution.py:40
  28.8 0.0 copy-start.3
  28.8 0.0 collective-permute-done.4.refs_2_
  28.8 0.0 copy-start.4
  28.8 4.4 %collective-permute-done.3.refs_1_ = bf16[2,256,256]{2,1,0:T(8,128)(2,1)} collective-permute-done((bf16[2,256,256]{2,1,0:T(8,128)(2,1)S(1)}, bf16[2,256,256]{2,1,0:T(8,128)(2,1)}, u32[]{:S(2)}, u32[]{:S(2)}) %collective-permute-start.3) | collective-permute-done | bytes 262176 | tf_op jit(solution)/shard_map/ppermute | solution.py:40
  33.2 0.0 copy-done.1
  33.2 0.0 copy-done.3
  33.2 0.0 copy-done.4
  33.2 2.6 %shard_map.104 = (bf16[2048,128]{1,0:T(8,128)(2,1)}, bf16[128,2048]{1,0:T(8,128)(2,1)}, bf16[2048,128]{1,0:T(8,128)(2,1)}) custom-call(s32[3]{0:T(128)} %pad_add_fusion.place_ref, s32[16]{0:T(128)} %order_ref.5, bf16[2,256,256]{2,1,0:T(8,128)(2,1)} %copy-done.1, bf16[2,256,256]{2,1,0:T(8,128)(2,1)} %collective-permute-done.3.refs_1_, ...), custom_call_target="tpu_custom_call" | custom-call | flops 1000000 | bytes 100000 | tf_op jit(solution)/shard_map/pallas_call | solution.py:258
  35.8 0.0 collective-permute-done.7.grad_ref
  35.8 20.7 %shard_map.105 = (bf16[256,4096]{1,0:T(8,128)(2,1)}, f32[2,2048,128]{2,1,0:T(8,128)}) custom-call(s32[3]{0:T(128)} %pad_add_fusion.place_ref, s32[16]{0:T(128)} %order_ref.5, s32[16]{0:T(128)} %docs_ref.3, bf16[2048,128]{1,0:T(8,128)(2,1)} %get-tuple-element.19.key_ref, bf16[128,2048]{1,0:T(8,128)(2,1)} %get-tuple-element.20.turned_ref, ...), custom_call_target="tpu_custom_call" | custom-call | flops 1000000 | bytes 100000 | tf_op jit(solution)/shard_map/pallas_call | solution.py:206
  56.5 0.0 collective-permute-done.6.grad_ref
  56.5 14.6 %shard_map.106 = (bf16[256,2048]{1,0:T(8,128)(2,1)}, bf16[16,128,256]{2,1,0:T(8,128)(2,1)}) custom-call(s32[3]{0:T(128)} %pad_add_fusion.place_ref, s32[16]{0:T(128)} %order_ref.5, s32[16]{0:T(128)} %docs_ref.3, bf16[2048,128]{1,0:T(8,128)(2,1)} %get-tuple-element.19.key_ref, bf16[128,2048]{1,0:T(8,128)(2,1)} %get-tuple-element.20.turned_ref, ...), custom_call_target="tpu_custom_call" | custom-call | flops 1000000 | bytes 100000 | tf_op jit(solution)/shard_map/pallas_call | solution.py:206
  71.1 4.6 %collective-permute-start.8 = (bf16[256,2048]{1,0:T(8,128)(2,1)}, bf16[256,2048]{1,0:T(8,128)(2,1)S(1)}, u32[]{:S(2)}, u32[]{:S(2)}) collective-permute-start(bf16[256,2048]{1,0:T(8,128)(2,1)} %get-tuple-element.23), channel_id=1, source_target_pairs={{0,2},{2,0},{4,6},{6,4},{8,10},{10,8},{12,14},{14,12},{1,3},{3,1},... | collective-permute-start | bytes 3145736 | tf_op jit(solution)/shard_map/ppermute | solution.py:45
  75.7 7.5 %all-to-all-start = ((bf16[16,128,256]{2,1,0:T(8,128)(2,1)}), bf16[16,128,256]{2,1,0:T(8,128)(2,1)S(1)}, u32[]{:S(2)}, u32[]{:S(2)}) async-start(bf16[16,128,256]{2,1,0:T(8,128)(2,1)} %get-tuple-element.25), calls=%async_computation | async-start | bytes 2097152 | tf_op jit(solution)/shard_map/all_to_all | solution.py:271
  83.2 0.0 collective-permute-done.8.piece_ref
  83.2 0.0 copy-start.2
  83.2 1.0 copy-done.2
  84.2 4.0 %shard_map.107 = bf16[256,4096]{1,0:T(8,128)(2,1)} custom-call(s32[3]{0:T(128)} %pad_add_fusion.place_ref, bf16[256,2048]{1,0:T(8,128)(2,1)} %copy-done.2, bf16[256,4096]{1,0:T(8,128)(2,1)} %get-tuple-element.24._), custom_call_target="tpu_custom_call", output_to_operand_aliasing={{}: (2, {})} | custom-call | flops 1000000 | bytes 100000 | tf_op jit(solution)/shard_map/pallas_call | solution.py:272
  88.2 14.6 %all-to-all-done.parts_ref = bf16[16,128,256]{2,1,0:T(8,128)(2,1)S(1)} async-done(((bf16[16,128,256]{2,1,0:T(8,128)(2,1)}), bf16[16,128,256]{2,1,0:T(8,128)(2,1)S(1)}, u32[]{:S(2)}, u32[]{:S(2)}) %all-to-all-start) | async-done | bytes 1048608 | tf_op jit(solution)/shard_map/all_to_all | solution.py:271
  102.8 0.0 copy-start
  102.8 1.0 copy-done
  103.8 2.0 %shard_map.108 = (bf16[128,512]{1,0:T(8,128)(2,1)}, bf16[128,512]{1,0:T(8,128)(2,1)}) custom-call(bf16[16,128,256]{2,1,0:T(8,128)(2,1)} %copy-done), custom_call_target="tpu_custom_call" | custom-call | flops 1000000 | bytes 100000 | tf_op jit(solution)/shard_map/pallas_call | solution.py:284
Async XLA Ops:
  0.6 14.3 %collective-permute-start.1 = (bf16[256,4096]{1,0:T(8,128)(2,1)}, bf16[256,4096]{1,0:T(8,128)(2,1)}, u32[]{:S(2)}, u32[]{:S(2)}) collective-permute-start(bf16[256,4096]{1,0:T(8,128)(2,1)} %bitcast.17), channel_id=1, source_target_pairs={{0,2},{2,0},{4,6},{6,4},{8,10},{10,8},{12,14},{14,12},{1,3},{3,1},... | collective-permute-start | bytes 6291464 | tf_op jit(solution)/shard_map/ppermute | solution.py:45
  2.1 12.8 %collective-permute-start.2 = (bf16[256,4096]{1,0:T(8,128)(2,1)}, bf16[256,4096]{1,0:T(8,128)(2,1)}, u32[]{:S(2)}, u32[]{:S(2)}) collective-permute-start(bf16[256,4096]{1,0:T(8,128)(2,1)} %bitcast.19), channel_id=1, source_target_pairs={{0,2},{2,0},{4,6},{6,4},{8,10},{10,8},{12,14},{14,12},{1,3},{3,1},... | collective-permute-start | bytes 6291464 | tf_op jit(solution)/shard_map/ppermute | solution.py:45
  5.0 30.8 %collective-permute-start.7 = (bf16[256,2048]{1,0:T(8,128)(2,1)}, bf16[256,2048]{1,0:T(8,128)(2,1)}, u32[]{:S(2)}, u32[]{:S(2)}) collective-permute-start(bf16[256,2048]{1,0:T(8,128)(2,1)} %get-tuple-element.29), channel_id=1, source_target_pairs={{0,112},{2,114},{4,116},{6,118},{8,120},{10,122},{12,124},{14,126}... | collective-permute-start | bytes 3145736 | tf_op jit(solution)/shard_map/ppermute | solution.py:53
  8.9 47.6 %collective-permute-start.6 = (bf16[256,2048]{1,0:T(8,128)(2,1)S(1)}, bf16[256,2048]{1,0:T(8,128)(2,1)}, u32[]{:S(2)}, u32[]{:S(2)}) collective-permute-start(bf16[256,2048]{1,0:T(8,128)(2,1)S(1)} %get-tuple-element.30), channel_id=1, source_target_pairs={{0,114},{2,112},{4,118},{6,116},{8,122},{10,120},{12,126},{14,124}... | collective-permute-start | bytes 3145736 | tf_op jit(solution)/shard_map/ppermute | solution.py:53
  12.5 1.6 %collective-permute-start = (bf16[256,256]{1,0:T(8,128)(2,1)}, bf16[256,256]{1,0:T(8,128)(2,1)S(1)}, u32[]{:S(2)}, u32[]{:S(2)}) collective-permute-start(bf16[256,256]{1,0:T(8,128)(2,1)} %get-tuple-element.17), channel_id=1, source_target_pairs={{0,2},{2,0},{4,6},{6,4},{8,10},{10,8},{12,14},{14,12},{1,3},{3,1},... | collective-permute-start | bytes 393224 | tf_op jit(solution)/shard_map/ppermute | solution.py:45
  14.9 18.3 %copy-start.1 = (bf16[2,256,256]{2,1,0:T(8,128)(2,1)}, bf16[2,256,256]{2,1,0:T(8,128)(2,1)S(1)}, u32[]{:S(2)}) copy-start(bf16[2,256,256]{2,1,0:T(8,128)(2,1)S(1)} %pad_maximum_fusion.refs_0_) | copy-start | bytes 786436
  15.0 13.8 %collective-permute-start.5 = (bf16[2,256,256]{2,1,0:T(8,128)(2,1)S(1)}, bf16[2,256,256]{2,1,0:T(8,128)(2,1)S(1)}, u32[]{:S(2)}, u32[]{:S(2)}) collective-permute-start(bf16[2,256,256]{2,1,0:T(8,128)(2,1)S(1)} %pad_maximum_fusion.refs_0_), channel_id=1, source_target_pairs={{0,12},{2,14},{4,0},{6,2},{8,4},{10,6},{12,8},{14,10},{1,13},{3,15... | collective-permute-start | bytes 786440 | tf_op jit(solution)/shard_map/ppermute | solution.py:40
  17.8 11.0 %collective-permute-start.4 = (bf16[2,256,256]{2,1,0:T(8,128)(2,1)S(1)}, bf16[2,256,256]{2,1,0:T(8,128)(2,1)S(1)}, u32[]{:S(2)}, u32[]{:S(2)}) collective-permute-start(bf16[2,256,256]{2,1,0:T(8,128)(2,1)S(1)} %pad_maximum_fusion.refs_0_), channel_id=1, source_target_pairs={{0,8},{2,10},{4,12},{6,14},{8,0},{10,2},{12,4},{14,6},{1,9},{3,11}... | collective-permute-start | bytes 786440 | tf_op jit(solution)/shard_map/ppermute | solution.py:40
  18.1 15.1 %collective-permute-start.3 = (bf16[2,256,256]{2,1,0:T(8,128)(2,1)S(1)}, bf16[2,256,256]{2,1,0:T(8,128)(2,1)}, u32[]{:S(2)}, u32[]{:S(2)}) collective-permute-start(bf16[2,256,256]{2,1,0:T(8,128)(2,1)S(1)} %pad_maximum_fusion.refs_0_), channel_id=1, source_target_pairs={{0,4},{2,6},{4,8},{6,10},{8,12},{10,14},{12,0},{14,2},{1,5},{3,7},... | collective-permute-start | bytes 786440 | tf_op jit(solution)/shard_map/ppermute | solution.py:40
  28.8 4.4 %copy-start.3 = (bf16[2,256,256]{2,1,0:T(8,128)(2,1)}, bf16[2,256,256]{2,1,0:T(8,128)(2,1)S(1)}, u32[]{:S(2)}) copy-start(bf16[2,256,256]{2,1,0:T(8,128)(2,1)S(1)} %collective-permute-done.5.refs_3_) | copy-start | bytes 786436
  28.8 4.4 %copy-start.4 = (bf16[2,256,256]{2,1,0:T(8,128)(2,1)}, bf16[2,256,256]{2,1,0:T(8,128)(2,1)S(1)}, u32[]{:S(2)}) copy-start(bf16[2,256,256]{2,1,0:T(8,128)(2,1)S(1)} %collective-permute-done.4.refs_2_) | copy-start | bytes 786436
  71.1 12.1 %collective-permute-start.8 = (bf16[256,2048]{1,0:T(8,128)(2,1)}, bf16[256,2048]{1,0:T(8,128)(2,1)S(1)}, u32[]{:S(2)}, u32[]{:S(2)}) collective-permute-start(bf16[256,2048]{1,0:T(8,128)(2,1)} %get-tuple-element.23), channel_id=1, source_target_pairs={{0,2},{2,0},{4,6},{6,4},{8,10},{10,8},{12,14},{14,12},{1,3},{3,1},... | collective-permute-start | bytes 3145736 | tf_op jit(solution)/shard_map/ppermute | solution.py:45
  75.7 27.1 %all-to-all-start = ((bf16[16,128,256]{2,1,0:T(8,128)(2,1)}), bf16[16,128,256]{2,1,0:T(8,128)(2,1)S(1)}, u32[]{:S(2)}, u32[]{:S(2)}) async-start(bf16[16,128,256]{2,1,0:T(8,128)(2,1)} %get-tuple-element.25), calls=%async_computation | async-start | bytes 2097152 | tf_op jit(solution)/shard_map/all_to_all | solution.py:271
  83.2 1.0 copy-start.2
  102.8 1.0 copy-start

commit v3 on v2

--- a/solution.py
+++ b/solution.py
@@ -38,6 +38,17 @@
 def chip_turned(array, by):
     size = lax.axis_size("ctx")
     return lax.ppermute(array, "ctx", [(i, (i + 2 * by) % size) for i in range(size)])
+
+
+def turned(array, axis):
+    size = lax.axis_size(axis)
+    return lax.ppermute(array, axis, [(i, (i + 1) % size) for i in range(size)])
+
+
+def across(array):
+    size = lax.axis_size("ctx")
+    moves = [(i * 2 + t, (i ^ 1) * 2 + 1 - t) for i in range(size) for t in range(2)]
+    return lax.ppermute(array, ("ctx", "tp"), moves)
 
 
 def core_swap(array):
@@ -150,8 +161,10 @@
 def rows_kernel(rows_of, place_ref, order_ref, docs_ref, key_ref, turned_ref, value_ref, query_ref, grad_ref, saved_ref, *refs):
     refs = list(refs)
     before_ref = refs.pop(0) if rows_of else None
-    dq_ref, out_ref, q_scr, g_scr, dots_scr, *rest = refs
-    sums_ref = rest.pop(0) if rows_of else out_ref
+    dq_ref = refs.pop(0)
+    out_refs = [refs.pop(0) for _ in range(4 if rows_of else 1)]
+    q_scr, g_scr, dots_scr, *rest = refs
+    sums_ref = rest.pop(0) if rows_of else out_refs[0]
     step = pl.program_id(0)
     block = pl.program_id(1)
 
@@ -182,10 +195,17 @@
         @pl.when((step == STEPS - 1) & (block == 1))
         def _():
             pltpu.make_async_copy(before_ref, rest[0], rest[1]).wait()
-            for r in range(BLOCKS):
-                at = pl.ds(pl.multiple_of(order_ref[r] * BLK, BLK), BLK)
-                out_ref[r, :, :HD] = ((sums_ref[0, at, :] + rest[0][0, at, :]) * INVERSE).astype(BF16)
-                out_ref[r, :, HD:] = (sums_ref[1, at, :] + rest[0][1, at, :]).astype(BF16)
+            for d in range(4):
+                out_ref = out_refs[d]
+                for r in range(4):
+                    core_to = place_ref[1] if r < 2 else 1 - place_ref[1]
+                    tp_to = place_ref[2] if r % 2 == 0 else 1 - place_ref[2]
+                    stored = lax.rem(place_ref[0] + d, 4) * 4 + core_to * 2 + tp_to
+                    at = pl.ds(pl.multiple_of(order_ref[stored] * BLK, BLK), BLK)
+                    dk = (sums_ref[0, at, :] + rest[0][0, at, :]) * INVERSE
+                    dv = sums_ref[1, at, :] + rest[0][1, at, :]
+                    out_ref[r, :, :HD] = dk.astype(out_ref.dtype)
+                    out_ref[r, :, HD:] = dv.astype(out_ref.dtype)
 
 
 def rows_call(rows_of, place, order, docs, kv, queries, saved, grads, sums):
@@ -199,7 +219,7 @@
     if rows_of:
         in_specs.append(ANY)
         operands.append(sums)
-        outs = [shape(ROWS, GROUP), shape(BLOCKS, BLK, 2 * HD)]
+        outs = [shape(ROWS, GROUP)] + [shape(4, BLK, 2 * HD, dtype=BF16 if d else F32) for d in range(4)]
         scratch += [pltpu.VMEM(sums_shape, F32), pltpu.VMEM(sums_shape, F32), pltpu.SemaphoreType.DMA]
     else:
         outs = [shape(*queries.shape), shape(*sums_shape, dtype=F32)]
@@ -209,24 +229,13 @@
             num_scalar_prefetch=3,
             grid=(STEPS, 2),
             in_specs=in_specs,
-            out_specs=[alone_at if rows_of else group_at, whole(outs[1].shape)],
+            out_specs=[alone_at if rows_of else group_at] + [whole(out.shape) for out in outs[1:]],
             scratch_shapes=scratch,
         ),
         out_shape=outs,
         compiler_params=pltpu.CompilerParams(vmem_limit_bytes=62 << 20),
         cost_estimate=TINY,
     )(place, order, docs, *operands)
-
-
-def total_kernel(parts_ref, keys_ref, values_ref):
-    for core in range(2):
-        for tp in range(2):
-            at = (tp * 2 + core) * HD
-            total = parts_ref[core * 2 + tp].astype(F32)
-            for y in range(1, 4):
-                total = total + parts_ref[y * 4 + core * 2 + tp].astype(F32)
-            keys_ref[:, at : at + HD] = total[:, :HD].astype(BF16)
-            values_ref[:, at : at + HD] = total[:, HD:].astype(BF16)
 
 
 def place_kernel(place_ref, piece_ref, _, out_ref):
@@ -266,9 +275,9 @@
 
     shared = (place, block_order, block_docs, kv)
     dq, sums = rows_call(0, *shared, queries, saved_out, grads[0], None)
-    dq_other, sums = rows_call(1, *shared, *sent, grads[1], sums)
+    dq_other, own, *further = rows_call(1, *shared, *sent, grads[1], sums)
     returned = core_swap(dq_other)
-    parts = lax.all_to_all(sums, ("ctx", "tp"), 0, 0, tiled=True)
+    arrived = [chip_turned(part, d + 1) for d, part in enumerate(further)]
     dq = pl.pallas_call(
         place_kernel,
         grid_spec=pltpu.PrefetchScalarGridSpec(
@@ -281,14 +290,21 @@
         input_output_aliases={2: 0},
         cost_estimate=TINY,
     )(place, returned, dq)
-    grad_keys, grad_values = pl.pallas_call(
-        total_kernel,
-        in_specs=[VMEM],
-        out_specs=[VMEM] * 2,
-        out_shape=[shape(BLK, KVH * HD)] * 2,
-        compiler_params=pltpu.CompilerParams(vmem_limit_bytes=62 << 20),
-        cost_estimate=TINY,
-    )(tied(parts, dq))
+    arrived[1] = tied(arrived[1], dq)
+    total = (own + sum(part.astype(F32) for part in arrived)).astype(BF16)
+    tp = place[2]
+    pieces = [total[0], turned(total[1], "tp"), core_swap(total[2]), across(total[3])]
+    outs = []
+    for part in range(2):
+        columns = []
+        for head in range(KVH):
+            same_tp, same_core = tp == head // 2, core == head % 2
+            near, apart = (
+                jnp.where(same_tp, pieces[2 * i], pieces[2 * i + 1])[:, part * HD : (part + 1) * HD] for i in range(2)
+            )
+            columns.append(jnp.where(same_core, near, apart))
+        outs.append(jnp.concatenate(columns, axis=1))
+    grad_keys, grad_values = outs
     return dq[None], grad_keys[None], grad_values[None]
 
 

time: 105 us -> 102 us (0.971); the launches traced: 106 us -> 101 us
  waiting for transfers between devices: 30.6 us -> 26 us
  Pallas kernels: 45.8 us -> 42.9 us
  other arithmetic: 1.54 us -> 3.1 us
    all_to_all x1 -> x0, waiting for transfers between devices: 14.6 us -> none  [on_device(): parts = lax.all_to_all(sums, ('ctx', 'tp'), 0, 0, tiled=True)]
    all_to_all x1 -> x0, starting transfers between devices: 7.5 us -> none  [on_device(): parts = lax.all_to_all(sums, ('ctx', 'tp'), 0, 0, tiled=True)]
    ppermute x3 -> x6, starting transfers between devices: 3.84 us -> 10.1 us  [chip_turned(): lax.ppermute(array, 'ctx', [(i, (i + 2 * by) % size) for i in range(size)])]
    ppermute x0 -> x2, waiting for transfers between devices: none -> 5.18 us  [the longest x1 3.97 us: across(): return lax.ppermute(array, ('ctx', 'tp'), moves)]
    ppermute x0 -> x2, starting transfers between devices: none -> 3.39 us  [the longest x1 3.38 us: turned(): return lax.ppermute(array, axis, [(i, (i + 1) % size) for i in range(size)])]
    ppermute x4 -> x5, starting transfers between devices: 6.16 us -> 3.71 us  [core_swap(): return lax.ppermute(array, 'ctx', [(i, i ^ 1) for i in range(size)])]
    ppermute x2, waiting for transfers between devices: 0.01 us -> 2.44 us  [from_next_section(): return lax.ppermute(array, ('pipe', 'ctx'), moves)]
    ppermute x3 -> x6, waiting for transfers between devices: 14.4 us -> 16.8 us  [chip_turned(): lax.ppermute(array, 'ctx', [(i, (i + 2 * by) % size) for i in range(size)])]
  transfers between devices with their start and end apart: 10 -> 15, of which waited for: 4 -> 9; matrix products, arithmetic and copies ran while one was open for 4% -> 5% of each run, Pallas kernels for 27% -> 26%
where the time goes in v3:
time: 102 us; the launch traced here: 101 us
  Pallas kernels  42.9 us (42%)
  waiting for transfers between devices  26 us (25%)
  starting transfers between devices  22.2 us (22%)
  local copies, waits for them, and re-layouts  5.75 us (6%)
  other arithmetic  3.1 us (3%)
    pallas_call x2, Pallas kernels, rows_call(): pl.pallas_call(functools.partial(rows_kernel, rows_of), grid_spec=pltpu.P...  34.3 us
    ppermute x6, waiting for transfers between devices, chip_turned(): lax.ppermute(array, 'ctx', [(i, (i + 2 * by) % size) for i in range(size)])  16.8 us
    ppermute x6, starting transfers between devices, chip_turned(): lax.ppermute(array, 'ctx', [(i, (i + 2 * by) % size) for i in range(size)])  10.1 us
    ppermute x2, starting transfers between devices, from_next_section(): return lax.ppermute(array, ('pipe', 'ctx'), moves)  5.04 us
    pallas_call x1, Pallas kernels, on_device(): pl.pallas_call(place_kernel, grid_spec=pltpu.PrefetchScalarGridSpec(num_s...  4.16 us
    ppermute x1, waiting for transfers between devices, across(): return lax.ppermute(array, ('ctx', 'tp'), moves)  3.97 us
    ppermute x5, starting transfers between devices, core_swap(): return lax.ppermute(array, 'ctx', [(i, i ^ 1) for i in range(size)])  3.71 us
    ppermute x1, starting transfers between devices, turned(): return lax.ppermute(array, axis, [(i, (i + 1) % size) for i in range(size)])  3.38 us
  transfers between devices with their start and end apart: 15, of which 9 were waited for; matrix products, arithmetic and copies ran while one was open for 5% of the time, Pallas kernels for 26%

profile of v3, /device:TPU:1, one launch (start us, length us, event | category | flops | bytes accessed | tf_op | source)
XLA Modules:
  0.0 100.7 jit_solution(14598424310841984810)
XLA Ops:
  0.6 1.5 %collective-permute-start.1 = (bf16[256,4096]{1,0:T(8,128)(2,1)}, bf16[256,4096]{1,0:T(8,128)(2,1)}, u32[]{:S(2)}, u32[]{:S(2)}) collective-permute-start(bf16[256,4096]{1,0:T(8,128)(2,1)} %bitcast.31), channel_id=1, source_target_pairs={{0,2},{2,0},{4,6},{6,4},{8,10},{10,8},{12,14},{14,12},{1,3},{3,1},... | collective-permute-start | bytes 6291464 | tf_op jit(solution)/shard_map/ppermute | solution.py:56
  2.1 0.1 collective-permute-start.2
  2.2 3.1 %dynamic-slice_bitcast_fusion = (bf16[256,2048]{1,0:T(8,128)(2,1)}, bf16[256,2048]{1,0:T(8,128)(2,1)}) fusion(bf16[1,256,4096]{2,1,0:T(8,128)(2,1)} %param.13, s32[]{:T(128)S(6)} %select_n.104, s32[]{:T(128)S(6)} %select_n.103), kind=kLoop, calls=%fused_computation | loop fusion | bytes 4194312 | tf_op jit(solution)/shard_map/dynamic_slice | solution.py:254
  5.3 3.9 %collective-permute-start.7 = (bf16[256,2048]{1,0:T(8,128)(2,1)}, bf16[256,2048]{1,0:T(8,128)(2,1)}, u32[]{:S(2)}, u32[]{:S(2)}) collective-permute-start(bf16[256,2048]{1,0:T(8,128)(2,1)} %get-tuple-element.31), channel_id=1, source_target_pairs={{0,112},{2,114},{4,116},{6,118},{8,120},{10,122},{12,124},{14,126}... | collective-permute-start | bytes 3145736 | tf_op jit(solution)/shard_map/ppermute | solution.py:64
  9.2 1.1 %collective-permute-start.6 = (bf16[256,2048]{1,0:T(8,128)(2,1)}, bf16[256,2048]{1,0:T(8,128)(2,1)S(1)}, u32[]{:S(2)}, u32[]{:S(2)}) collective-permute-start(bf16[256,2048]{1,0:T(8,128)(2,1)} %get-tuple-element.32), channel_id=1, source_target_pairs={{0,114},{2,112},{4,118},{6,116},{8,122},{10,120},{12,126},{14,124}... | collective-permute-start | bytes 3145736 | tf_op jit(solution)/shard_map/ppermute | solution.py:64
  10.4 0.7 pad_add_fusion.place_ref
  11.0 1.8 %shard_map.103 = (bf16[256,256]{1,0:T(8,128)(2,1)}, bf16[256,256]{1,0:T(8,128)(2,1)}) custom-call(s32[3]{0:T(128)} %pad_add_fusion.place_ref, bf16[256,256]{1,0:T(8,128)(2,1)} %bitcast.36, bf16[256,256]{1,0:T(8,128)(2,1)} %bitcast.37, f32[2,8]{1,0:T(2,128)} %bitcast.40), custom_call_target="tpu_custom_call" | custom-call | flops 1000000 | bytes 100000 | tf_op jit(solution)/shard_map/pallas_call | solution.py:257
  12.8 0.0 collective-permute-start
  12.8 1.6 %collective-permute-done = bf16[256,256]{1,0:T(8,128)(2,1)S(1)} collective-permute-done((bf16[256,256]{1,0:T(8,128)(2,1)}, bf16[256,256]{1,0:T(8,128)(2,1)S(1)}, u32[]{:S(2)}, u32[]{:S(2)}) %collective-permute-start) | collective-permute-done | bytes 131104 | tf_op jit(solution)/shard_map/ppermute | solution.py:56
  14.4 0.9 pad_maximum_fusion.refs_0_
  15.3 0.0 copy-start.1
  15.3 0.0 collective-permute-done.1.query_ref
  15.3 0.0 collective-permute-done.2.saved_ref
  15.3 1.4 %collective-permute-start.3 = (bf16[2,256,256]{2,1,0:T(8,128)(2,1)S(1)}, bf16[2,256,256]{2,1,0:T(8,128)(2,1)S(1)}, u32[]{:S(2)}, u32[]{:S(2)}) collective-permute-start(bf16[2,256,256]{2,1,0:T(8,128)(2,1)S(1)} %pad_maximum_fusion.refs_0_), channel_id=1, source_target_pairs={{0,4},{2,6},{4,8},{6,10},{8,12},{10,14},{12,0},{14,2},{1,5},{3,7},... | collective-permute-start | bytes 786440 | tf_op jit(solution)/shard_map/ppermute | solution.py:40
  16.7 2.6 %collective-permute-start.4 = (bf16[2,256,256]{2,1,0:T(8,128)(2,1)S(1)}, bf16[2,256,256]{2,1,0:T(8,128)(2,1)S(1)}, u32[]{:S(2)}, u32[]{:S(2)}) collective-permute-start(bf16[2,256,256]{2,1,0:T(8,128)(2,1)S(1)} %pad_maximum_fusion.refs_0_), channel_id=1, source_target_pairs={{0,8},{2,10},{4,12},{6,14},{8,0},{10,2},{12,4},{14,6},{1,9},{3,11}... | collective-permute-start | bytes 786440 | tf_op jit(solution)/shard_map/ppermute | solution.py:40
  19.3 1.1 %collective-permute-start.5 = (bf16[2,256,256]{2,1,0:T(8,128)(2,1)S(1)}, bf16[2,256,256]{2,1,0:T(8,128)(2,1)}, u32[]{:S(2)}, u32[]{:S(2)}) collective-permute-start(bf16[2,256,256]{2,1,0:T(8,128)(2,1)S(1)} %pad_maximum_fusion.refs_0_), channel_id=1, source_target_pairs={{0,12},{2,14},{4,0},{6,2},{8,4},{10,6},{12,8},{14,10},{1,13},{3,15... | collective-permute-start | bytes 786440 | tf_op jit(solution)/shard_map/ppermute | solution.py:40
  20.4 4.1 %collective-permute-done.3.refs_1_ = bf16[2,256,256]{2,1,0:T(8,128)(2,1)S(1)} collective-permute-done((bf16[2,256,256]{2,1,0:T(8,128)(2,1)S(1)}, bf16[2,256,256]{2,1,0:T(8,128)(2,1)S(1)}, u32[]{:S(2)}, u32[]{:S(2)}) %collective-permute-start.3) | collective-permute-done | bytes 262176 | tf_op jit(solution)/shard_map/ppermute | solution.py:40
  24.5 6.7 %collective-permute-done.4.refs_2_ = bf16[2,256,256]{2,1,0:T(8,128)(2,1)S(1)} collective-permute-done((bf16[2,256,256]{2,1,0:T(8,128)(2,1)S(1)}, bf16[2,256,256]{2,1,0:T(8,128)(2,1)S(1)}, u32[]{:S(2)}, u32[]{:S(2)}) %collective-permute-start.4) | collective-permute-done | bytes 262176 | tf_op jit(solution)/shard_map/ppermute | solution.py:40
  31.2 0.0 collective-permute-done.5.refs_3_
  31.2 0.0 copy-done.1
  31.3 0.0 copy-done.4
  31.3 0.7 copy-done.5
  31.9 2.6 %shard_map.104 = (bf16[2048,128]{1,0:T(8,128)(2,1)}, bf16[128,2048]{1,0:T(8,128)(2,1)}, bf16[2048,128]{1,0:T(8,128)(2,1)}) custom-call(s32[3]{0:T(128)} %pad_add_fusion.place_ref, s32[16]{0:T(128)} %order_ref.5, bf16[2,256,256]{2,1,0:T(8,128)(2,1)} %copy-done.1, bf16[2,256,256]{2,1,0:T(8,128)(2,1)} %copy-done.4, bf16[2,256,256]{2,1,0:T(8,128)(2,1)} %copy-done.5, ...), custom_call_target="tpu_custom_call" | custom-call | flops 1000000 | bytes 100000 | tf_op jit(solution)/shard_map/pallas_call | solution.py:267
  34.6 0.0 collective-permute-done.7.grad_ref
  34.6 17.1 %shard_map.105 = (bf16[256,4096]{1,0:T(8,128)(2,1)}, f32[2,2048,128]{2,1,0:T(8,128)}) custom-call(s32[3]{0:T(128)} %pad_add_fusion.place_ref, s32[16]{0:T(128)} %order_ref.5, s32[16]{0:T(128)} %docs_ref.3, bf16[2048,128]{1,0:T(8,128)(2,1)} %get-tuple-element.20.key_ref, bf16[128,2048]{1,0:T(8,128)(2,1)} %get-tuple-element.21.turned_ref, ...), custom_call_target="tpu_custom_call" | custom-call | flops 1000000 | bytes 100000 | tf_op jit(solution)/shard_map/pallas_call | solution.py:226
  51.7 2.4 %collective-permute-done.6.grad_ref = bf16[256,2048]{1,0:T(8,128)(2,1)S(1)} collective-permute-done((bf16[256,2048]{1,0:T(8,128)(2,1)}, bf16[256,2048]{1,0:T(8,128)(2,1)S(1)}, u32[]{:S(2)}, u32[]{:S(2)}) %collective-permute-start.6) | collective-permute-done | bytes 1048608 | tf_op jit(solution)/shard_map/ppermute | solution.py:64
  54.1 1.0 copy-done
  55.1 17.2 %shard_map.106 = (bf16[256,2048]{1,0:T(8,128)(2,1)}, f32[4,128,256]{2,1,0:T(8,128)}, bf16[4,128,256]{2,1,0:T(8,128)(2,1)}, bf16[4,128,256]{2,1,0:T(8,128)(2,1)}, bf16[4,128,256]{2,1,0:T(8,128)(2,1)}) custom-call(s32[3]{0:T(128)} %pad_add_fusion.place_ref, s32[16]{0:T(128)} %order_ref.5, s32[16]{0:T(128)} %docs_ref.3, ...), custom_call_target="tpu_custom_call" | custom-call | flops 1000000 | bytes 100000 | tf_op jit(solution)/shard_map/pallas_call | solution.py:226
  72.3 1.3 %collective-permute-start.8 = (bf16[256,2048]{1,0:T(8,128)(2,1)}, bf16[256,2048]{1,0:T(8,128)(2,1)S(1)}, u32[]{:S(2)}, u32[]{:S(2)}) collective-permute-start(bf16[256,2048]{1,0:T(8,128)(2,1)} %get-tuple-element.24), channel_id=1, source_target_pairs={{0,2},{2,0},{4,6},{6,4},{8,10},{10,8},{12,14},{14,12},{1,3},{3,1},... | collective-permute-start | bytes 3145736 | tf_op jit(solution)/shard_map/ppermute | solution.py:56
  73.6 3.6 %collective-permute-start.10 = (bf16[4,128,256]{2,1,0:T(8,128)(2,1)}, bf16[4,128,256]{2,1,0:T(8,128)(2,1)S(1)}, u32[]{:S(2)}, u32[]{:S(2)}) collective-permute-start(bf16[4,128,256]{2,1,0:T(8,128)(2,1)} %get-tuple-element.28), channel_id=1, source_target_pairs={{0,8},{2,10},{4,12},{6,14},{8,0},{10,2},{12,4},{14,6},{1,9},{3,11}... | collective-permute-start | bytes 786440 | tf_op jit(solution)/shard_map/ppermute | solution.py:40
  77.2 0.0 collective-permute-start.11
  77.2 1.4 %collective-permute-start.9 = (bf16[4,128,256]{2,1,0:T(8,128)(2,1)}, bf16[4,128,256]{2,1,0:T(8,128)(2,1)S(1)}, u32[]{:S(2)}, u32[]{:S(2)}) collective-permute-start(bf16[4,128,256]{2,1,0:T(8,128)(2,1)} %get-tuple-element.27), channel_id=1, source_target_pairs={{0,4},{2,6},{4,8},{6,10},{8,12},{10,14},{12,0},{14,2},{1,5},{3,7},... | collective-permute-start | bytes 786440 | tf_op jit(solution)/shard_map/ppermute | solution.py:40
  78.7 0.0 collective-permute-done.8.piece_ref
  78.7 1.0 copy-done.2
  79.7 4.2 %shard_map.107 = bf16[256,4096]{1,0:T(8,128)(2,1)} custom-call(s32[3]{0:T(128)} %pad_add_fusion.place_ref, bf16[256,2048]{1,0:T(8,128)(2,1)} %copy-done.2, bf16[256,4096]{1,0:T(8,128)(2,1)} %get-tuple-element.25._), custom_call_target="tpu_custom_call", output_to_operand_aliasing={{}: (2, {})} | custom-call | flops 1000000 | bytes 100000 | tf_op jit(solution)/shard_map/pallas_call | solution.py:281
  83.8 0.2 collective-permute-done.10
  84.0 5.4 %collective-permute-done.11 = bf16[4,128,256]{2,1,0:T(8,128)(2,1)S(1)} collective-permute-done((bf16[4,128,256]{2,1,0:T(8,128)(2,1)}, bf16[4,128,256]{2,1,0:T(8,128)(2,1)S(1)}, u32[]{:S(2)}, u32[]{:S(2)}) %collective-permute-start.11) | collective-permute-done | bytes 262176 | tf_op jit(solution)/shard_map/ppermute | solution.py:40
  89.4 0.4 collective-permute-done.9
  89.8 0.0 copy-done.3
  89.8 0.1 add_convert_fusion
  89.9 3.4 %collective-permute-start.12 = (bf16[128,256]{1,0:T(8,128)(2,1)S(1)}, bf16[128,256]{1,0:T(8,128)(2,1)S(1)}, u32[]{:S(2)}, u32[]{:S(2)}) collective-permute-start(bf16[128,256]{1,0:T(8,128)(2,1)S(1)} %get-tuple-element.35), channel_id=1, source_target_pairs={{0,1},{1,0},{2,3},{3,2},{4,5},{5,4},{6,7},{7,6},{8,9},{9,8},{10,11... | collective-permute-start | bytes 196616 | tf_op jit(solution)/shard_map/ppermute | solution.py:45
  93.3 0.8 collective-permute-start.13
  94.1 0.0 collective-permute-start.14
  94.1 1.2 %collective-permute-done.12 = bf16[128,256]{1,0:T(8,128)(2,1)S(1)} collective-permute-done((bf16[128,256]{1,0:T(8,128)(2,1)S(1)}, bf16[128,256]{1,0:T(8,128)(2,1)S(1)}, u32[]{:S(2)}, u32[]{:S(2)}) %collective-permute-start.12) | collective-permute-done | bytes 65568 | tf_op jit(solution)/shard_map/ppermute | solution.py:45
  95.4 0.0 collective-permute-done.13
  95.4 4.0 %collective-permute-done.14 = bf16[128,256]{1,0:T(8,128)(2,1)S(1)} collective-permute-done((bf16[128,256]{1,0:T(8,128)(2,1)S(1)}, bf16[128,256]{1,0:T(8,128)(2,1)S(1)}, u32[]{:S(2)}, u32[]{:S(2)}) %collective-permute-start.14) | collective-permute-done | bytes 65568 | tf_op jit(solution)/shard_map/ppermute | solution.py:51
  99.4 0.7 maximum_bitcast_fusion.1
  100.1 0.7 maximum_bitcast_fusion
  (9 shorter events, 0.1 us)
Async XLA Ops:
  0.6 14.7 %collective-permute-start.1 = (bf16[256,4096]{1,0:T(8,128)(2,1)}, bf16[256,4096]{1,0:T(8,128)(2,1)}, u32[]{:S(2)}, u32[]{:S(2)}) collective-permute-start(bf16[256,4096]{1,0:T(8,128)(2,1)} %bitcast.31), channel_id=1, source_target_pairs={{0,2},{2,0},{4,6},{6,4},{8,10},{10,8},{12,14},{14,12},{1,3},{3,1},... | collective-permute-start | bytes 6291464 | tf_op jit(solution)/shard_map/ppermute | solution.py:56
  2.1 13.2 %collective-permute-start.2 = (bf16[256,4096]{1,0:T(8,128)(2,1)}, bf16[256,4096]{1,0:T(8,128)(2,1)}, u32[]{:S(2)}, u32[]{:S(2)}) collective-permute-start(bf16[256,4096]{1,0:T(8,128)(2,1)} %bitcast.33), channel_id=1, source_target_pairs={{0,2},{2,0},{4,6},{6,4},{8,10},{10,8},{12,14},{14,12},{1,3},{3,1},... | collective-permute-start | bytes 6291464 | tf_op jit(solution)/shard_map/ppermute | solution.py:56
  5.3 29.3 %collective-permute-start.7 = (bf16[256,2048]{1,0:T(8,128)(2,1)}, bf16[256,2048]{1,0:T(8,128)(2,1)}, u32[]{:S(2)}, u32[]{:S(2)}) collective-permute-start(bf16[256,2048]{1,0:T(8,128)(2,1)} %get-tuple-element.31), channel_id=1, source_target_pairs={{0,112},{2,114},{4,116},{6,118},{8,120},{10,122},{12,124},{14,126}... | collective-permute-start | bytes 3145736 | tf_op jit(solution)/shard_map/ppermute | solution.py:64
  9.2 44.9 %collective-permute-start.6 = (bf16[256,2048]{1,0:T(8,128)(2,1)}, bf16[256,2048]{1,0:T(8,128)(2,1)S(1)}, u32[]{:S(2)}, u32[]{:S(2)}) collective-permute-start(bf16[256,2048]{1,0:T(8,128)(2,1)} %get-tuple-element.32), channel_id=1, source_target_pairs={{0,114},{2,112},{4,118},{6,116},{8,122},{10,120},{12,126},{14,124}... | collective-permute-start | bytes 3145736 | tf_op jit(solution)/shard_map/ppermute | solution.py:64
  12.8 1.6 %collective-permute-start = (bf16[256,256]{1,0:T(8,128)(2,1)}, bf16[256,256]{1,0:T(8,128)(2,1)S(1)}, u32[]{:S(2)}, u32[]{:S(2)}) collective-permute-start(bf16[256,256]{1,0:T(8,128)(2,1)} %get-tuple-element.18), channel_id=1, source_target_pairs={{0,2},{2,0},{4,6},{6,4},{8,10},{10,8},{12,14},{14,12},{1,3},{3,1},... | collective-permute-start | bytes 393224 | tf_op jit(solution)/shard_map/ppermute | solution.py:56
  15.3 15.9 %copy-start.1 = (bf16[2,256,256]{2,1,0:T(8,128)(2,1)}, bf16[2,256,256]{2,1,0:T(8,128)(2,1)S(1)}, u32[]{:S(2)}) copy-start(bf16[2,256,256]{2,1,0:T(8,128)(2,1)S(1)} %pad_maximum_fusion.refs_0_) | copy-start | bytes 786436
  15.3 9.2 %collective-permute-start.3 = (bf16[2,256,256]{2,1,0:T(8,128)(2,1)S(1)}, bf16[2,256,256]{2,1,0:T(8,128)(2,1)S(1)}, u32[]{:S(2)}, u32[]{:S(2)}) collective-permute-start(bf16[2,256,256]{2,1,0:T(8,128)(2,1)S(1)} %pad_maximum_fusion.refs_0_), channel_id=1, source_target_pairs={{0,4},{2,6},{4,8},{6,10},{8,12},{10,14},{12,0},{14,2},{1,5},{3,7},... | collective-permute-start | bytes 786440 | tf_op jit(solution)/shard_map/ppermute | solution.py:40
  16.7 14.5 %collective-permute-start.4 = (bf16[2,256,256]{2,1,0:T(8,128)(2,1)S(1)}, bf16[2,256,256]{2,1,0:T(8,128)(2,1)S(1)}, u32[]{:S(2)}, u32[]{:S(2)}) collective-permute-start(bf16[2,256,256]{2,1,0:T(8,128)(2,1)S(1)} %pad_maximum_fusion.refs_0_), channel_id=1, source_target_pairs={{0,8},{2,10},{4,12},{6,14},{8,0},{10,2},{12,4},{14,6},{1,9},{3,11}... | collective-permute-start | bytes 786440 | tf_op jit(solution)/shard_map/ppermute | solution.py:40
  19.3 11.9 %collective-permute-start.5 = (bf16[2,256,256]{2,1,0:T(8,128)(2,1)S(1)}, bf16[2,256,256]{2,1,0:T(8,128)(2,1)}, u32[]{:S(2)}, u32[]{:S(2)}) collective-permute-start(bf16[2,256,256]{2,1,0:T(8,128)(2,1)S(1)} %pad_maximum_fusion.refs_0_), channel_id=1, source_target_pairs={{0,12},{2,14},{4,0},{6,2},{8,4},{10,6},{12,8},{14,10},{1,13},{3,15... | collective-permute-start | bytes 786440 | tf_op jit(solution)/shard_map/ppermute | solution.py:40
  24.5 6.7 %copy-start.4 = (bf16[2,256,256]{2,1,0:T(8,128)(2,1)}, bf16[2,256,256]{2,1,0:T(8,128)(2,1)S(1)}, u32[]{:S(2)}) copy-start(bf16[2,256,256]{2,1,0:T(8,128)(2,1)S(1)} %collective-permute-done.3.refs_1_) | copy-start | bytes 786436
  31.2 0.7 copy-start.5
  54.1 1.0 copy-start
  72.3 6.4 %collective-permute-start.8 = (bf16[256,2048]{1,0:T(8,128)(2,1)}, bf16[256,2048]{1,0:T(8,128)(2,1)S(1)}, u32[]{:S(2)}, u32[]{:S(2)}) collective-permute-start(bf16[256,2048]{1,0:T(8,128)(2,1)} %get-tuple-element.24), channel_id=1, source_target_pairs={{0,2},{2,0},{4,6},{6,4},{8,10},{10,8},{12,14},{14,12},{1,3},{3,1},... | collective-permute-start | bytes 3145736 | tf_op jit(solution)/shard_map/ppermute | solution.py:56
  73.6 10.4 %collective-permute-start.10 = (bf16[4,128,256]{2,1,0:T(8,128)(2,1)}, bf16[4,128,256]{2,1,0:T(8,128)(2,1)S(1)}, u32[]{:S(2)}, u32[]{:S(2)}) collective-permute-start(bf16[4,128,256]{2,1,0:T(8,128)(2,1)} %get-tuple-element.28), channel_id=1, source_target_pairs={{0,8},{2,10},{4,12},{6,14},{8,0},{10,2},{12,4},{14,6},{1,9},{3,11}... | collective-permute-start | bytes 786440 | tf_op jit(solution)/shard_map/ppermute | solution.py:40
  77.2 12.2 %collective-permute-start.11 = (bf16[4,128,256]{2,1,0:T(8,128)(2,1)}, bf16[4,128,256]{2,1,0:T(8,128)(2,1)S(1)}, u32[]{:S(2)}, u32[]{:S(2)}) collective-permute-start(bf16[4,128,256]{2,1,0:T(8,128)(2,1)} %get-tuple-element.30), channel_id=1, source_target_pairs={{0,12},{2,14},{4,0},{6,2},{8,4},{10,6},{12,8},{14,10},{1,13},{3,15... | collective-permute-start | bytes 786440 | tf_op jit(solution)/shard_map/ppermute | solution.py:40
  77.2 12.6 %collective-permute-start.9 = (bf16[4,128,256]{2,1,0:T(8,128)(2,1)}, bf16[4,128,256]{2,1,0:T(8,128)(2,1)S(1)}, u32[]{:S(2)}, u32[]{:S(2)}) collective-permute-start(bf16[4,128,256]{2,1,0:T(8,128)(2,1)} %get-tuple-element.27), channel_id=1, source_target_pairs={{0,4},{2,6},{4,8},{6,10},{8,12},{10,14},{12,0},{14,2},{1,5},{3,7},... | collective-permute-start | bytes 786440 | tf_op jit(solution)/shard_map/ppermute | solution.py:40
  78.7 1.0 copy-start.2
  79.7 10.1 %copy-start.3 = (f32[4,128,256]{2,1,0:T(8,128)S(1)}, f32[4,128,256]{2,1,0:T(8,128)}, u32[]{:S(2)}) copy-start(f32[4,128,256]{2,1,0:T(8,128)} %get-tuple-element.26) | copy-start | bytes 1572868
  89.9 5.4 %collective-permute-start.12 = (bf16[128,256]{1,0:T(8,128)(2,1)S(1)}, bf16[128,256]{1,0:T(8,128)(2,1)S(1)}, u32[]{:S(2)}, u32[]{:S(2)}) collective-permute-start(bf16[128,256]{1,0:T(8,128)(2,1)S(1)} %get-tuple-element.35), channel_id=1, source_target_pairs={{0,1},{1,0},{2,3},{3,2},{4,5},{5,4},{6,7},{7,6},{8,9},{9,8},{10,11... | collective-permute-start | bytes 196616 | tf_op jit(solution)/shard_map/ppermute | solution.py:45
  93.3 2.0 %collective-permute-start.13 = (bf16[128,256]{1,0:T(8,128)(2,1)S(1)}, bf16[128,256]{1,0:T(8,128)(2,1)S(1)}, u32[]{:S(2)}, u32[]{:S(2)}) collective-permute-start(bf16[128,256]{1,0:T(8,128)(2,1)S(1)} %get-tuple-element.37), channel_id=1, source_target_pairs={{0,2},{2,0},{4,6},{6,4},{8,10},{10,8},{12,14},{14,12},{1,3},{3,1},... | collective-permute-start | bytes 196616 | tf_op jit(solution)/shard_map/ppermute | solution.py:56
  94.1 5.2 %collective-permute-start.14 = (bf16[128,256]{1,0:T(8,128)(2,1)S(1)}, bf16[128,256]{1,0:T(8,128)(2,1)S(1)}, u32[]{:S(2)}, u32[]{:S(2)}) collective-permute-start(bf16[128,256]{1,0:T(8,128)(2,1)S(1)} %get-tuple-element.36), channel_id=1, source_target_pairs={{0,3},{1,2},{2,1},{3,0},{4,7},{5,6},{6,5},{7,4},{8,11},{9,10},{10,... | collective-permute-start | bytes 196616 | tf_op jit(solution)/shard_map/ppermute | solution.py:51

commit v4 on v3

--- a/solution.py
+++ b/solution.py
@@ -25,6 +25,8 @@
 GROUP = HQ // KVH * HD
 STEP = 512
 STEPS = GROUP // STEP
+RING = 4
+DIRECT = GROUP - STEP
 SMEM = pl.BlockSpec(memory_space=pltpu.SMEM)
 VMEM = pl.BlockSpec(memory_space=pltpu.VMEM)
 ANY = pl.BlockSpec(memory_space=pl.ANY)
@@ -61,6 +63,18 @@
     moves = [
         (s * size + i, (s - 1) % sections * size + (i ^ flip)) for s in range(sections) for i in range(size)
     ]
+    return lax.ppermute(array, ("pipe", "ctx"), moves)
+
+
+def long_way(array, hop):
+    sections, size = lax.axis_size("pipe"), lax.axis_size("ctx")
+    moves = []
+    for s in range(sections):
+        ring, at = s // RING, s % RING
+        if hop == 0 and at == 0:
+            ring = (ring - 1) % (sections // RING)
+        target = ring * RING + (at + 1) % RING
+        moves += [(s * size + i, target * size + (i ^ 1 if hop == RING - 2 else i)) for i in range(size)]
     return lax.ppermute(array, ("pipe", "ctx"), moves)
 
 
@@ -158,8 +172,9 @@
     dk_ref[pl.ds(first, rows), :] += dk
 
 
-def rows_kernel(rows_of, place_ref, order_ref, docs_ref, key_ref, turned_ref, value_ref, query_ref, grad_ref, saved_ref, *refs):
+def rows_kernel(rows_of, place_ref, order_ref, docs_ref, key_ref, turned_ref, value_ref, query_ref, saved_ref, grad_ref, *refs):
     refs = list(refs)
+    around_ref = refs.pop(0) if rows_of else None
     before_ref = refs.pop(0) if rows_of else None
     dq_ref = refs.pop(0)
     out_refs = [refs.pop(0) for _ in range(4 if rows_of else 1)]
@@ -174,7 +189,18 @@
             pltpu.make_async_copy(before_ref, rest[0], rest[1]).start()
         sums_ref[...] = jnp.zeros_like(sums_ref)
 
-    load_rows(query_ref, grad_ref, saved_ref, q_scr, g_scr, dots_scr)
+    if rows_of:
+
+        @pl.when(step < DIRECT // STEP)
+        def _():
+            load_rows(query_ref, grad_ref, saved_ref, q_scr, g_scr, dots_scr)
+
+        @pl.when(step >= DIRECT // STEP)
+        def _():
+            load_rows(query_ref, around_ref, saved_ref, q_scr, g_scr, dots_scr)
+
+    else:
+        load_rows(query_ref, grad_ref, saved_ref, q_scr, g_scr, dots_scr)
     core = 1 - place_ref[1] if rows_of else place_ref[1]
     seq = order_ref[place_ref[0] * 4 + core * 2 + block]
     doc = docs_ref[seq]
@@ -213,8 +239,13 @@
     group_at = pl.BlockSpec((BLK, STEP), lambda i, j, p, *_: (j, p[1] * STEPS + i))
     alone_at = pl.BlockSpec((BLK, STEP), lambda i, j, *_: (j, i))
     sums_shape = (2, TOKENS, HD)
-    in_specs = [whole((TOKENS, HD)), whole((HD, TOKENS)), whole((TOKENS, HD)), group_at, alone_at, group_at]
-    operands = [*kv, queries, grads, saved]
+    in_specs = [whole((TOKENS, HD)), whole((HD, TOKENS)), whole((TOKENS, HD)), group_at, group_at]
+    operands = [*kv, queries, saved, *grads]
+    if rows_of:
+        in_specs.append(pl.BlockSpec((BLK, STEP), lambda i, j, *_: (j, jnp.minimum(i, DIRECT // STEP - 1))))
+        in_specs.append(pl.BlockSpec((BLK, STEP), lambda i, j, *_: (j, jnp.maximum(i - DIRECT // STEP, 0))))
+    else:
+        in_specs.append(alone_at)
     scratch = [pltpu.VMEM((STEP, HD), BF16), pltpu.VMEM((STEP, HD), BF16), pltpu.VMEM((HD, BLK), F32)]
     if rows_of:
         in_specs.append(ANY)
@@ -248,11 +279,14 @@
     place = jnp.stack([ctx // 2, core, lax.axis_index("tp")]).astype(jnp.int32)
     queries, saved_out, section_grads = queries[0], saved_out[0], section_grads[0]
 
-    grads = []
-    for flip in range(2):
-        group = core if flip == 0 else 1 - core
-        piece = lax.dynamic_slice_in_dim(section_grads, group * GROUP, GROUP, 1)
-        grads.append(from_next_section(piece, flip))
+    first = (1 - core) * GROUP
+    own_rows = lax.dynamic_slice_in_dim(section_grads, core * GROUP, GROUP, 1)
+    direct = lax.dynamic_slice_in_dim(section_grads, first, DIRECT, 1)
+    around = lax.dynamic_slice_in_dim(section_grads, first + DIRECT, GROUP - DIRECT, 1)
+    key_codes = tied(key_codes, own_rows, direct, around)
+    own_rows = from_next_section(own_rows, 0)
+    direct = from_next_section(direct, 1)
+    around = long_way(around, 0)
 
     keep, send = pl.pallas_call(
         dequantize_kernel,
@@ -264,6 +298,8 @@
     sent = [core_swap(array) for array in (queries, saved_out)]
     chip = tied(jnp.stack([keep, core_swap(send)]), *sent)
     chips = [chip] + [chip_turned(chip, d) for d in range(1, 4)]
+    around = long_way(tied(around, chips[2]), 1)
+    around = long_way(around, 2)
     kv = pl.pallas_call(
         order_kernel,
         in_specs=[SMEM, SMEM] + [VMEM] * 4,
@@ -274,8 +310,8 @@
     )(place, block_order, *chips)
 
     shared = (place, block_order, block_docs, kv)
-    dq, sums = rows_call(0, *shared, queries, saved_out, grads[0], None)
-    dq_other, own, *further = rows_call(1, *shared, *sent, grads[1], sums)
+    dq, sums = rows_call(0, *shared, queries, saved_out, [own_rows], None)
+    dq_other, own, *further = rows_call(1, *shared, *sent, [direct, around], sums)
     returned = core_swap(dq_other)
     arrived = [chip_turned(part, d + 1) for d, part in enumerate(further)]
     dq = pl.pallas_call(

time: 102 us -> 99.5 us (0.975)
  waiting for transfers between devices: 26 us -> 23.4 us
  Pallas kernels: 42.9 us -> 44 us
    ppermute x0 -> x3, waiting for transfers between devices: none -> 7.63 us  [long_way(): return lax.ppermute(array, ('pipe', 'ctx'), moves)]
    ppermute x6, waiting for transfers between devices: 16.8 us -> 9.33 us  [chip_turned(): lax.ppermute(array, 'ctx', [(i, (i + 2 * by) % size) for i in range(size)])]
    ppermute x2, waiting for transfers between devices: 2.44 us -> 0.01 us  [from_next_section(): return lax.ppermute(array, ('pipe', 'ctx'), moves)]
    ppermute x6, starting transfers between devices: 10.1 us -> 8.48 us  [chip_turned(): lax.ppermute(array, 'ctx', [(i, (i + 2 * by) % size) for i in range(size)])]
    pallas_call x2, Pallas kernels: 34.3 us -> 35.4 us  [rows_call(): pl.pallas_call(functools.partial(rows_kernel, rows_of), grid_spec=pltpu.P...]
    dynamic_slice x1 -> x3, local copies, waits for them, and re-layouts: 3.09 us -> 2.35 us  [the longest x1 1.29 us: on_device(): own_rows = lax.dynamic_slice_in_dim(section_grads, core * GROUP, GROUP, 1)]
    unnamed x12 -> x14, local copies, waits for them, and re-layouts: 2.64 us -> 2.4 us
  transfers between devices with their start and end apart: 15 -> 18, of which waited for: 9 -> 9; matrix products, arithmetic and copies ran while one was open for 5% -> 4% of each run, Pallas kernels for 26% -> 25%
where the time goes in v4:
time: 99.5 us; the launch traced here: 98.7 us
  Pallas kernels  44 us (44%)
  waiting for transfers between devices  23.4 us (24%)
  starting transfers between devices  22.8 us (23%)
  local copies, waits for them, and re-layouts  4.76 us (5%)
  other arithmetic  3.04 us (3%)
    pallas_call x2, Pallas kernels, rows_call(): pl.pallas_call(functools.partial(rows_kernel, rows_of), grid_spec=pltpu.P...  35.4 us
    ppermute x6, waiting for transfers between devices, chip_turned(): lax.ppermute(array, 'ctx', [(i, (i + 2 * by) % size) for i in range(size)])  9.33 us
    ppermute x6, starting transfers between devices, chip_turned(): lax.ppermute(array, 'ctx', [(i, (i + 2 * by) % size) for i in range(size)])  8.48 us
    ppermute x3, waiting for transfers between devices, long_way(): return lax.ppermute(array, ('pipe', 'ctx'), moves)  7.63 us
    ppermute x2, starting transfers between devices, from_next_section(): return lax.ppermute(array, ('pipe', 'ctx'), moves)  5.46 us
    ppermute x5, starting transfers between devices, core_swap(): return lax.ppermute(array, 'ctx', [(i, i ^ 1) for i in range(size)])  4.7 us
    ppermute x1, waiting for transfers between devices, across(): return lax.ppermute(array, ('ctx', 'tp'), moves)  4.31 us
    pallas_call x1, Pallas kernels, on_device(): pl.pallas_call(place_kernel, grid_spec=pltpu.PrefetchScalarGridSpec(num_s...  4.16 us
  transfers between devices with their start and end apart: 18, of which 9 were waited for; matrix products, arithmetic and copies ran while one was open for 4% of the time, Pallas kernels for 25%

profile of v4, /device:TPU:1, one launch (start us, length us, event | category | flops | bytes accessed | tf_op | source)
XLA Modules:
  0.0 98.7 jit_solution(17975956500887259448)
XLA Ops:
  0.6 1.5 %collective-permute-start.1 = (bf16[256,4096]{1,0:T(8,128)(2,1)}, bf16[256,4096]{1,0:T(8,128)(2,1)}, u32[]{:S(2)}, u32[]{:S(2)}) collective-permute-start(bf16[256,4096]{1,0:T(8,128)(2,1)} %bitcast.33), channel_id=1, source_target_pairs={{0,2},{2,0},{4,6},{6,4},{8,10},{10,8},{12,14},{14,12},{1,3},{3,1},... | collective-permute-start | bytes 6291464 | tf_op jit(solution)/shard_map/ppermute | solution.py:58
  2.1 0.1 collective-permute-start.2
  2.2 1.3 %dynamic-slice_bitcast_fusion = bf16[256,2048]{1,0:T(8,128)(2,1)S(1)} fusion(bf16[1,256,4096]{2,1,0:T(8,128)(2,1)} %param.13, s32[]{:T(128)S(6)} %select_n.106), kind=kLoop, calls=%fused_computation | loop fusion | bytes 2097156 | tf_op jit(solution)/shard_map/dynamic_slice | solution.py:283
  3.5 4.0 %collective-permute-start.10 = (bf16[256,2048]{1,0:T(8,128)(2,1)S(1)}, bf16[256,2048]{1,0:T(8,128)(2,1)}, u32[]{:S(2)}, u32[]{:S(2)}) collective-permute-start(bf16[256,2048]{1,0:T(8,128)(2,1)S(1)} %dynamic-slice_bitcast_fusion), channel_id=1, source_target_pairs={{0,112},{2,114},{4,116},{6,118},{8,120},{10,122},{12,124},{14,126}... | collective-permute-start | bytes 3145736 | tf_op jit(solution)/shard_map/ppermute | solution.py:66
  7.5 1.0 %dynamic-slice_bitcast_fusion.1 = bf16[256,1536]{1,0:T(8,128)(2,1)} fusion(bf16[1,256,4096]{2,1,0:T(8,128)(2,1)S(1)} %copy-done, s32[]{:T(128)S(6)} %select_n.107), kind=kLoop, calls=%fused_computation.1 | loop fusion | bytes 1572868 | tf_op jit(solution)/shard_map/dynamic_slice | solution.py:284
  8.6 0.6 pad_add_fusion.place_ref
  9.2 1.8 %shard_map.103 = (bf16[256,256]{1,0:T(8,128)(2,1)}, bf16[256,256]{1,0:T(8,128)(2,1)}) custom-call(s32[3]{0:T(128)} %pad_add_fusion.place_ref, bf16[256,256]{1,0:T(8,128)(2,1)} %bitcast.38, bf16[256,256]{1,0:T(8,128)(2,1)} %bitcast.39, f32[2,8]{1,0:T(2,128)} %bitcast.42), custom_call_target="tpu_custom_call" | custom-call | flops 1000000 | bytes 100000 | tf_op jit(solution)/shard_map/pallas_call | solution.py:291
  11.0 0.7 collective-permute-start
  11.7 0.0 collective-permute-start.7
  11.7 1.2 %collective-permute-done = bf16[256,256]{1,0:T(8,128)(2,1)S(1)} collective-permute-done((bf16[256,256]{1,0:T(8,128)(2,1)}, bf16[256,256]{1,0:T(8,128)(2,1)S(1)}, u32[]{:S(2)}, u32[]{:S(2)}) %collective-permute-start) | collective-permute-done | bytes 131104 | tf_op jit(solution)/shard_map/ppermute | solution.py:58
  12.9 0.9 pad_maximum_fusion.refs_0_
  13.8 0.0 copy-start.1
  13.8 0.0 collective-permute-done.1.query_ref
  13.9 0.0 collective-permute-done.2.saved_ref
  13.9 3.0 %collective-permute-start.4 = (bf16[2,256,256]{2,1,0:T(8,128)(2,1)S(1)}, bf16[2,256,256]{2,1,0:T(8,128)(2,1)S(1)}, u32[]{:S(2)}, u32[]{:S(2)}) collective-permute-start(bf16[2,256,256]{2,1,0:T(8,128)(2,1)S(1)} %pad_maximum_fusion.refs_0_), channel_id=1, source_target_pairs={{0,8},{2,10},{4,12},{6,14},{8,0},{10,2},{12,4},{14,6},{1,9},{3,11}... | collective-permute-start | bytes 786440 | tf_op jit(solution)/shard_map/ppermute | solution.py:42
  16.9 1.5 %collective-permute-start.6 = (bf16[256,1536]{1,0:T(8,128)(2,1)}, bf16[256,1536]{1,0:T(8,128)(2,1)}, u32[]{:S(2)}, u32[]{:S(2)}) collective-permute-start(bf16[256,1536]{1,0:T(8,128)(2,1)} %dynamic-slice_bitcast_fusion.1), channel_id=1, source_target_pairs={{0,114},{2,112},{4,118},{6,116},{8,122},{10,120},{12,126},{14,124}... | collective-permute-start | bytes 2359304 | tf_op jit(solution)/shard_map/ppermute | solution.py:66
  18.3 2.5 %collective-permute-done.7 = bf16[256,512]{1,0:T(8,128)(2,1)S(1)} collective-permute-done((bf16[256,512]{1,0:T(8,128)(2,1)S(1)}, bf16[256,512]{1,0:T(8,128)(2,1)S(1)}, u32[]{:S(2)}, u32[]{:S(2)}) %collective-permute-start.7) | collective-permute-done | bytes 262176 | tf_op jit(solution)/shard_map/ppermute | solution.py:78
  20.9 2.1 %collective-permute-done.4.refs_2_ = bf16[2,256,256]{2,1,0:T(8,128)(2,1)S(1)} collective-permute-done((bf16[2,256,256]{2,1,0:T(8,128)(2,1)S(1)}, bf16[2,256,256]{2,1,0:T(8,128)(2,1)S(1)}, u32[]{:S(2)}, u32[]{:S(2)}) %collective-permute-start.4) | collective-permute-done | bytes 262176 | tf_op jit(solution)/shard_map/ppermute | solution.py:42
  23.0 0.0 collective-permute-start.8
  23.0 1.3 %collective-permute-start.3 = (bf16[2,256,256]{2,1,0:T(8,128)(2,1)S(1)}, bf16[2,256,256]{2,1,0:T(8,128)(2,1)S(1)}, u32[]{:S(2)}, u32[]{:S(2)}) collective-permute-start(bf16[2,256,256]{2,1,0:T(8,128)(2,1)S(1)} %pad_maximum_fusion.refs_0_), channel_id=1, source_target_pairs={{0,4},{2,6},{4,8},{6,10},{8,12},{10,14},{12,0},{14,2},{1,5},{3,7},... | collective-permute-start | bytes 786440 | tf_op jit(solution)/shard_map/ppermute | solution.py:42
  24.3 1.5 %collective-permute-start.5 = (bf16[2,256,256]{2,1,0:T(8,128)(2,1)S(1)}, bf16[2,256,256]{2,1,0:T(8,128)(2,1)}, u32[]{:S(2)}, u32[]{:S(2)}) collective-permute-start(bf16[2,256,256]{2,1,0:T(8,128)(2,1)S(1)} %pad_maximum_fusion.refs_0_), channel_id=1, source_target_pairs={{0,12},{2,14},{4,0},{6,2},{8,4},{10,6},{12,8},{14,10},{1,13},{3,15... | collective-permute-start | bytes 786440 | tf_op jit(solution)/shard_map/ppermute | solution.py:42
  25.8 5.1 %collective-permute-done.8 = bf16[256,512]{1,0:T(8,128)(2,1)} collective-permute-done((bf16[256,512]{1,0:T(8,128)(2,1)S(1)}, bf16[256,512]{1,0:T(8,128)(2,1)}, u32[]{:S(2)}, u32[]{:S(2)}) %collective-permute-start.8) | collective-permute-done | bytes 262176 | tf_op jit(solution)/shard_map/ppermute | solution.py:78
  30.9 0.8 collective-permute-start.9
  31.7 0.7 copy-done.6
  32.4 0.0 collective-permute-done.5.refs_3_
  32.4 2.6 %shard_map.104 = (bf16[2048,128]{1,0:T(8,128)(2,1)}, bf16[128,2048]{1,0:T(8,128)(2,1)}, bf16[2048,128]{1,0:T(8,128)(2,1)}) custom-call(s32[3]{0:T(128)} %pad_add_fusion.place_ref, s32[16]{0:T(128)} %order_ref.5, bf16[2,256,256]{2,1,0:T(8,128)(2,1)} %copy-done.1, bf16[2,256,256]{2,1,0:T(8,128)(2,1)} %copy-done.6, bf16[2,256,256]{2,1,0:T(8,128)(2,1)} %copy-done.4, ...), custom_call_target="tpu_custom_call" | custom-call | flops 1000000 | bytes 100000 | tf_op jit(solution)/shard_map/pallas_call | solution.py:303
  35.0 16.0 %shard_map.105 = (bf16[256,4096]{1,0:T(8,128)(2,1)}, f32[2,2048,128]{2,1,0:T(8,128)}) custom-call(s32[3]{0:T(128)} %pad_add_fusion.place_ref, s32[16]{0:T(128)} %order_ref.5, s32[16]{0:T(128)} %docs_ref.3, bf16[2048,128]{1,0:T(8,128)(2,1)} %get-tuple-element.23.key_ref, bf16[128,2048]{1,0:T(8,128)(2,1)} %get-tuple-element.24.turned_ref, ...), custom_call_target="tpu_custom_call" | custom-call | flops 1000000 | bytes 100000 | tf_op jit(solution)/shard_map/pallas_call | solution.py:257
  51.1 0.0 collective-permute-done.6.grad_ref
  51.1 0.0 collective-permute-done.9.refs_0_
  51.1 0.7 copy-done.5
  51.8 19.3 %shard_map.106 = (bf16[256,2048]{1,0:T(8,128)(2,1)}, f32[4,128,256]{2,1,0:T(8,128)}, bf16[4,128,256]{2,1,0:T(8,128)(2,1)}, bf16[4,128,256]{2,1,0:T(8,128)(2,1)}, bf16[4,128,256]{2,1,0:T(8,128)(2,1)}) custom-call(s32[3]{0:T(128)} %pad_add_fusion.place_ref, s32[16]{0:T(128)} %order_ref.5, s32[16]{0:T(128)} %docs_ref.3, ...), custom_call_target="tpu_custom_call" | custom-call | flops 1000000 | bytes 100000 | tf_op jit(solution)/shard_map/pallas_call | solution.py:257
  71.2 1.3 %collective-permute-start.11 = (bf16[256,2048]{1,0:T(8,128)(2,1)}, bf16[256,2048]{1,0:T(8,128)(2,1)S(1)}, u32[]{:S(2)}, u32[]{:S(2)}) collective-permute-start(bf16[256,2048]{1,0:T(8,128)(2,1)} %get-tuple-element.28), channel_id=1, source_target_pairs={{0,2},{2,0},{4,6},{6,4},{8,10},{10,8},{12,14},{14,12},{1,3},{3,1},... | collective-permute-start | bytes 3145736 | tf_op jit(solution)/shard_map/ppermute | solution.py:58
  72.5 1.6 %collective-permute-start.12 = (bf16[4,128,256]{2,1,0:T(8,128)(2,1)}, bf16[4,128,256]{2,1,0:T(8,128)(2,1)S(1)}, u32[]{:S(2)}, u32[]{:S(2)}) collective-permute-start(bf16[4,128,256]{2,1,0:T(8,128)(2,1)} %get-tuple-element.31), channel_id=1, source_target_pairs={{0,4},{2,6},{4,8},{6,10},{8,12},{10,14},{12,0},{14,2},{1,5},{3,7},... | collective-permute-start | bytes 786440 | tf_op jit(solution)/shard_map/ppermute | solution.py:42
  74.1 1.1 %collective-permute-start.14 = (bf16[4,128,256]{2,1,0:T(8,128)(2,1)}, bf16[4,128,256]{2,1,0:T(8,128)(2,1)S(1)}, u32[]{:S(2)}, u32[]{:S(2)}) collective-permute-start(bf16[4,128,256]{2,1,0:T(8,128)(2,1)} %get-tuple-element.34), channel_id=1, source_target_pairs={{0,12},{2,14},{4,0},{6,2},{8,4},{10,6},{12,8},{14,10},{1,13},{3,15... | collective-permute-start | bytes 786440 | tf_op jit(solution)/shard_map/ppermute | solution.py:42
  75.2 0.0 collective-permute-done.11.piece_ref
  75.2 1.0 copy-done.2
  76.2 4.2 %shard_map.107 = bf16[256,4096]{1,0:T(8,128)(2,1)} custom-call(s32[3]{0:T(128)} %pad_add_fusion.place_ref, bf16[256,2048]{1,0:T(8,128)(2,1)} %copy-done.2, bf16[256,4096]{1,0:T(8,128)(2,1)} %get-tuple-element.29._), custom_call_target="tpu_custom_call", output_to_operand_aliasing={{}: (2, {})} | custom-call | flops 1000000 | bytes 100000 | tf_op jit(solution)/shard_map/pallas_call | solution.py:317
  80.3 1.8 %collective-permute-done.13 = bf16[4,128,256]{2,1,0:T(8,128)(2,1)S(1)} collective-permute-done((bf16[4,128,256]{2,1,0:T(8,128)(2,1)}, bf16[4,128,256]{2,1,0:T(8,128)(2,1)S(1)}, u32[]{:S(2)}, u32[]{:S(2)}) %collective-permute-start.13) | collective-permute-done | bytes 262176 | tf_op jit(solution)/shard_map/ppermute | solution.py:42
  82.1 5.4 %collective-permute-done.12 = bf16[4,128,256]{2,1,0:T(8,128)(2,1)S(1)} collective-permute-done((bf16[4,128,256]{2,1,0:T(8,128)(2,1)}, bf16[4,128,256]{2,1,0:T(8,128)(2,1)S(1)}, u32[]{:S(2)}, u32[]{:S(2)}) %collective-permute-start.12) | collective-permute-done | bytes 262176 | tf_op jit(solution)/shard_map/ppermute | solution.py:42
  87.5 0.0 collective-permute-done.14
  87.5 0.1 add_convert_fusion
  87.7 3.4 %collective-permute-start.15 = (bf16[128,256]{1,0:T(8,128)(2,1)S(1)}, bf16[128,256]{1,0:T(8,128)(2,1)S(1)}, u32[]{:S(2)}, u32[]{:S(2)}) collective-permute-start(bf16[128,256]{1,0:T(8,128)(2,1)S(1)} %get-tuple-element.37), channel_id=1, source_target_pairs={{0,1},{1,0},{2,3},{3,2},{4,5},{5,4},{6,7},{7,6},{8,9},{9,8},{10,11... | collective-permute-start | bytes 196616 | tf_op jit(solution)/shard_map/ppermute | solution.py:47
  91.1 1.0 %collective-permute-start.16 = (bf16[128,256]{1,0:T(8,128)(2,1)S(1)}, bf16[128,256]{1,0:T(8,128)(2,1)S(1)}, u32[]{:S(2)}, u32[]{:S(2)}) collective-permute-start(bf16[128,256]{1,0:T(8,128)(2,1)S(1)} %get-tuple-element.39), channel_id=1, source_target_pairs={{0,2},{2,0},{4,6},{6,4},{8,10},{10,8},{12,14},{14,12},{1,3},{3,1},... | collective-permute-start | bytes 196616 | tf_op jit(solution)/shard_map/ppermute | solution.py:58
  92.1 0.6 collective-permute-done.15
  92.7 0.3 collective-permute-done.16
  93.0 4.3 %collective-permute-done.17 = bf16[128,256]{1,0:T(8,128)(2,1)S(1)} collective-permute-done((bf16[128,256]{1,0:T(8,128)(2,1)S(1)}, bf16[128,256]{1,0:T(8,128)(2,1)S(1)}, u32[]{:S(2)}, u32[]{:S(2)}) %collective-permute-start.17) | collective-permute-done | bytes 65568 | tf_op jit(solution)/shard_map/ppermute | solution.py:53
  97.3 0.7 maximum_bitcast_fusion.1
  98.0 0.7 maximum_bitcast_fusion
  (19 shorter events, 0.1 us)
Async XLA Ops:
  0.6 6.9 %copy-start = (bf16[1,256,4096]{2,1,0:T(8,128)(2,1)S(1)}, bf16[1,256,4096]{2,1,0:T(8,128)(2,1)}, u32[]{:S(2)}) copy-start(bf16[1,256,4096]{2,1,0:T(8,128)(2,1)} %param.13) | copy-start | bytes 6291460
  0.6 13.2 %collective-permute-start.1 = (bf16[256,4096]{1,0:T(8,128)(2,1)}, bf16[256,4096]{1,0:T(8,128)(2,1)}, u32[]{:S(2)}, u32[]{:S(2)}) collective-permute-start(bf16[256,4096]{1,0:T(8,128)(2,1)} %bitcast.33), channel_id=1, source_target_pairs={{0,2},{2,0},{4,6},{6,4},{8,10},{10,8},{12,14},{14,12},{1,3},{3,1},... | collective-permute-start | bytes 6291464 | tf_op jit(solution)/shard_map/ppermute | solution.py:58
  2.1 11.7 %collective-permute-start.2 = (bf16[256,4096]{1,0:T(8,128)(2,1)}, bf16[256,4096]{1,0:T(8,128)(2,1)}, u32[]{:S(2)}, u32[]{:S(2)}) collective-permute-start(bf16[256,4096]{1,0:T(8,128)(2,1)} %bitcast.35), channel_id=1, source_target_pairs={{0,2},{2,0},{4,6},{6,4},{8,10},{10,8},{12,14},{14,12},{1,3},{3,1},... | collective-permute-start | bytes 6291464 | tf_op jit(solution)/shard_map/ppermute | solution.py:58
  3.5 31.5 %collective-permute-start.10 = (bf16[256,2048]{1,0:T(8,128)(2,1)S(1)}, bf16[256,2048]{1,0:T(8,128)(2,1)}, u32[]{:S(2)}, u32[]{:S(2)}) collective-permute-start(bf16[256,2048]{1,0:T(8,128)(2,1)S(1)} %dynamic-slice_bitcast_fusion), channel_id=1, source_target_pairs={{0,112},{2,114},{4,116},{6,118},{8,120},{10,122},{12,124},{14,126}... | collective-permute-start | bytes 3145736 | tf_op jit(solution)/shard_map/ppermute | solution.py:66
  11.0 1.9 %collective-permute-start = (bf16[256,256]{1,0:T(8,128)(2,1)}, bf16[256,256]{1,0:T(8,128)(2,1)S(1)}, u32[]{:S(2)}, u32[]{:S(2)}) collective-permute-start(bf16[256,256]{1,0:T(8,128)(2,1)} %get-tuple-element.21), channel_id=1, source_target_pairs={{0,2},{2,0},{4,6},{6,4},{8,10},{10,8},{12,14},{14,12},{1,3},{3,1},... | collective-permute-start | bytes 393224 | tf_op jit(solution)/shard_map/ppermute | solution.py:58
  11.7 9.1 %collective-permute-start.7 = (bf16[256,512]{1,0:T(8,128)(2,1)S(1)}, bf16[256,512]{1,0:T(8,128)(2,1)S(1)}, u32[]{:S(2)}, u32[]{:S(2)}) collective-permute-start(bf16[256,512]{1,0:T(8,128)(2,1)S(1)} %dynamic-slice_bitcast_fusion.2), channel_id=1, source_target_pairs={{0,80},{2,82},{4,84},{6,86},{8,88},{10,90},{12,92},{14,94},{16,32}... | collective-permute-start | bytes 786440 | tf_op jit(solution)/shard_map/ppermute | solution.py:78
  13.8 18.6 %copy-start.1 = (bf16[2,256,256]{2,1,0:T(8,128)(2,1)}, bf16[2,256,256]{2,1,0:T(8,128)(2,1)S(1)}, u32[]{:S(2)}) copy-start(bf16[2,256,256]{2,1,0:T(8,128)(2,1)S(1)} %pad_maximum_fusion.refs_0_) | copy-start | bytes 786436
  13.9 9.1 %collective-permute-start.4 = (bf16[2,256,256]{2,1,0:T(8,128)(2,1)S(1)}, bf16[2,256,256]{2,1,0:T(8,128)(2,1)S(1)}, u32[]{:S(2)}, u32[]{:S(2)}) collective-permute-start(bf16[2,256,256]{2,1,0:T(8,128)(2,1)S(1)} %pad_maximum_fusion.refs_0_), channel_id=1, source_target_pairs={{0,8},{2,10},{4,12},{6,14},{8,0},{10,2},{12,4},{14,6},{1,9},{3,11}... | collective-permute-start | bytes 786440 | tf_op jit(solution)/shard_map/ppermute | solution.py:42
  16.9 34.2 %collective-permute-start.6 = (bf16[256,1536]{1,0:T(8,128)(2,1)}, bf16[256,1536]{1,0:T(8,128)(2,1)}, u32[]{:S(2)}, u32[]{:S(2)}) collective-permute-start(bf16[256,1536]{1,0:T(8,128)(2,1)} %dynamic-slice_bitcast_fusion.1), channel_id=1, source_target_pairs={{0,114},{2,112},{4,118},{6,116},{8,122},{10,120},{12,126},{14,124}... | collective-permute-start | bytes 2359304 | tf_op jit(solution)/shard_map/ppermute | solution.py:66
  23.0 9.4 %copy-start.4 = (bf16[2,256,256]{2,1,0:T(8,128)(2,1)}, bf16[2,256,256]{2,1,0:T(8,128)(2,1)S(1)}, u32[]{:S(2)}) copy-start(bf16[2,256,256]{2,1,0:T(8,128)(2,1)S(1)} %collective-permute-done.4.refs_2_) | copy-start | bytes 786436
  23.0 7.9 %collective-permute-start.8 = (bf16[256,512]{1,0:T(8,128)(2,1)S(1)}, bf16[256,512]{1,0:T(8,128)(2,1)}, u32[]{:S(2)}, u32[]{:S(2)}) collective-permute-start(bf16[256,512]{1,0:T(8,128)(2,1)S(1)} %collective-permute-done.7), channel_id=1, source_target_pairs={{0,16},{2,18},{4,20},{6,22},{8,24},{10,26},{12,28},{14,30},{16,32}... | collective-permute-start | bytes 786440 | tf_op jit(solution)/shard_map/ppermute | solution.py:78
  23.0 8.7 %collective-permute-start.3 = (bf16[2,256,256]{2,1,0:T(8,128)(2,1)S(1)}, bf16[2,256,256]{2,1,0:T(8,128)(2,1)S(1)}, u32[]{:S(2)}, u32[]{:S(2)}) collective-permute-start(bf16[2,256,256]{2,1,0:T(8,128)(2,1)S(1)} %pad_maximum_fusion.refs_0_), channel_id=1, source_target_pairs={{0,4},{2,6},{4,8},{6,10},{8,12},{10,14},{12,0},{14,2},{1,5},{3,7},... | collective-permute-start | bytes 786440 | tf_op jit(solution)/shard_map/ppermute | solution.py:42
  24.3 8.1 %collective-permute-start.5 = (bf16[2,256,256]{2,1,0:T(8,128)(2,1)S(1)}, bf16[2,256,256]{2,1,0:T(8,128)(2,1)}, u32[]{:S(2)}, u32[]{:S(2)}) collective-permute-start(bf16[2,256,256]{2,1,0:T(8,128)(2,1)S(1)} %pad_maximum_fusion.refs_0_), channel_id=1, source_target_pairs={{0,12},{2,14},{4,0},{6,2},{8,4},{10,6},{12,8},{14,10},{1,13},{3,15... | collective-permute-start | bytes 786440 | tf_op jit(solution)/shard_map/ppermute | solution.py:42
  30.9 20.2 %collective-permute-start.9 = (bf16[256,512]{1,0:T(8,128)(2,1)}, bf16[256,512]{1,0:T(8,128)(2,1)S(1)}, u32[]{:S(2)}, u32[]{:S(2)}) collective-permute-start(bf16[256,512]{1,0:T(8,128)(2,1)} %collective-permute-done.8), channel_id=1, source_target_pairs={{0,18},{2,16},{4,22},{6,20},{8,26},{10,24},{12,30},{14,28},{16,34}... | collective-permute-start | bytes 786440 | tf_op jit(solution)/shard_map/ppermute | solution.py:78
  31.7 0.7 copy-start.6
  51.1 0.7 copy-start.5
  71.2 4.0 %collective-permute-start.11 = (bf16[256,2048]{1,0:T(8,128)(2,1)}, bf16[256,2048]{1,0:T(8,128)(2,1)S(1)}, u32[]{:S(2)}, u32[]{:S(2)}) collective-permute-start(bf16[256,2048]{1,0:T(8,128)(2,1)} %get-tuple-element.28), channel_id=1, source_target_pairs={{0,2},{2,0},{4,6},{6,4},{8,10},{10,8},{12,14},{14,12},{1,3},{3,1},... | collective-permute-start | bytes 3145736 | tf_op jit(solution)/shard_map/ppermute | solution.py:58
  72.5 9.6 %collective-permute-start.13 = (bf16[4,128,256]{2,1,0:T(8,128)(2,1)}, bf16[4,128,256]{2,1,0:T(8,128)(2,1)S(1)}, u32[]{:S(2)}, u32[]{:S(2)}) collective-permute-start(bf16[4,128,256]{2,1,0:T(8,128)(2,1)} %get-tuple-element.32), channel_id=1, source_target_pairs={{0,8},{2,10},{4,12},{6,14},{8,0},{10,2},{12,4},{14,6},{1,9},{3,11}... | collective-permute-start | bytes 786440 | tf_op jit(solution)/shard_map/ppermute | solution.py:42
  72.5 15.0 %collective-permute-start.12 = (bf16[4,128,256]{2,1,0:T(8,128)(2,1)}, bf16[4,128,256]{2,1,0:T(8,128)(2,1)S(1)}, u32[]{:S(2)}, u32[]{:S(2)}) collective-permute-start(bf16[4,128,256]{2,1,0:T(8,128)(2,1)} %get-tuple-element.31), channel_id=1, source_target_pairs={{0,4},{2,6},{4,8},{6,10},{8,12},{10,14},{12,0},{14,2},{1,5},{3,7},... | collective-permute-start | bytes 786440 | tf_op jit(solution)/shard_map/ppermute | solution.py:42
  74.1 13.4 %collective-permute-start.14 = (bf16[4,128,256]{2,1,0:T(8,128)(2,1)}, bf16[4,128,256]{2,1,0:T(8,128)(2,1)S(1)}, u32[]{:S(2)}, u32[]{:S(2)}) collective-permute-start(bf16[4,128,256]{2,1,0:T(8,128)(2,1)} %get-tuple-element.34), channel_id=1, source_target_pairs={{0,12},{2,14},{4,0},{6,2},{8,4},{10,6},{12,8},{14,10},{1,13},{3,15... | collective-permute-start | bytes 786440 | tf_op jit(solution)/shard_map/ppermute | solution.py:42
  75.2 1.0 copy-start.2
  76.2 11.4 %copy-start.3 = (f32[4,128,256]{2,1,0:T(8,128)S(1)}, f32[4,128,256]{2,1,0:T(8,128)}, u32[]{:S(2)}) copy-start(f32[4,128,256]{2,1,0:T(8,128)} %get-tuple-element.30) | copy-start | bytes 1572868
  87.7 5.0 %collective-permute-start.15 = (bf16[128,256]{1,0:T(8,128)(2,1)S(1)}, bf16[128,256]{1,0:T(8,128)(2,1)S(1)}, u32[]{:S(2)}, u32[]{:S(2)}) collective-permute-start(bf16[128,256]{1,0:T(8,128)(2,1)S(1)} %get-tuple-element.37), channel_id=1, source_target_pairs={{0,1},{1,0},{2,3},{3,2},{4,5},{5,4},{6,7},{7,6},{8,9},{9,8},{10,11... | collective-permute-start | bytes 196616 | tf_op jit(solution)/shard_map/ppermute | solution.py:47
  91.1 1.9 %collective-permute-start.16 = (bf16[128,256]{1,0:T(8,128)(2,1)S(1)}, bf16[128,256]{1,0:T(8,128)(2,1)S(1)}, u32[]{:S(2)}, u32[]{:S(2)}) collective-permute-start(bf16[128,256]{1,0:T(8,128)(2,1)S(1)} %get-tuple-element.39), channel_id=1, source_target_pairs={{0,2},{2,0},{4,6},{6,4},{8,10},{10,8},{12,14},{14,12},{1,3},{3,1},... | collective-permute-start | bytes 196616 | tf_op jit(solution)/shard_map/ppermute | solution.py:58
  92.1 5.2 %collective-permute-start.17 = (bf16[128,256]{1,0:T(8,128)(2,1)S(1)}, bf16[128,256]{1,0:T(8,128)(2,1)S(1)}, u32[]{:S(2)}, u32[]{:S(2)}) collective-permute-start(bf16[128,256]{1,0:T(8,128)(2,1)S(1)} %get-tuple-element.38), channel_id=1, source_target_pairs={{0,3},{1,2},{2,1},{3,0},{4,7},{5,6},{6,5},{7,4},{8,11},{9,10},{10,... | collective-permute-start | bytes 196616 | tf_op jit(solution)/shard_map/ppermute | solution.py:53
